TPU v7x, 512 devices: a whole 4x8x8 slice. The times are simulated.
512 devices in a mesh: region: 16 (over z, core), bulk: 32 (over y, x).
Axes of the slice: x: 4, y: 8, z: 8, core: 2. Of those that a mesh axis runs over, the one named last changes fastest.
Arguments:
- positions: float32 [32768, 3, 128], P(('region', 'bulk')), may hold values from -6 to 6
- fields: float32 [32768, 4, 128], P(('region', 'bulk')), may hold values from -6 to 6
- storage: float32 [32768, 128], P(('region', 'bulk')), may hold values from 0.5 to 2
- velocity: float32 [32768, 3, 128], P(('region', 'bulk')), may hold values from -4 to 4
- send_list: int32 [512, 3, 32, 1], P(('region', 'bulk')), may hold values from 0 to 63
- remote_local: int32 [512, 96, 2], P(('region', 'bulk')), may hold values from 0 to 63
- remote_mask: int32 [512, 96, 2, 16, 128], P(('region', 'bulk')), may hold values from 0 to 255
- local_pairs: int32 [512, 64, 2], P(('region', 'bulk')), may hold values from 0 to 63, as said below
- local_mask: int32 [512, 64, 16, 128], P(('region', 'bulk')), may hold values from 0 to 255
- migrate_list: int32 [512, 32, 1], P(('region', 'bulk')), may hold values from -1 to 63, as said below
Outputs:
- new_fields: float32 [32768, 4, 128], P(('region', 'bulk'))
- new_velocity: float32 [32768, 3, 128], P(('region', 'bulk'))
- arrived: float32 [16384, 11, 128], P(('region', 'bulk'))
Inputs may be any that keep to these rules, and one draw needn't show every extreme that they name: `local_pairs`: each pair names two different owned blocks. `migrate_list`: owned blocks named on one device are distinct; in each region some devices hand 1 blocks to each of several peers and the rest hand none.
All inputs are finite; a program needn't handle non-finite values.
Results may differ from a plain program's by a relative error of at most 0.00002.
Values sent between devices are 32-bit elements; how exact they have to be, the bound alone decides.
No kernel may reach another device: no remote copies, remote signals or barrier semaphores. Data moves between devices by JAX's collectives and lax.ppermute only.
A program may use at most 64 MiB of HBM per device.

v0:
```python
import jax
import jax.numpy as jnp
from jax import lax
from jax.sharding import PartitionSpec as P

bond_stiff = 0.1
press_gain = 0.05
leak_gain = 0.5
time_step = 0.5
inv_horizon = 0.25
group_rows = 16


def from_behind(shard, axis, by):
    peers = lax.axis_size(axis)
    return lax.ppermute(shard, axis, [(i, (i + by) % peers) for i in range(peers)])


def unpack_bonds(packed):
    shifts = jnp.arange(8, dtype=jnp.int32)
    bit_table = jnp.bitwise_and(
        jnp.right_shift(packed[:, :, None, :], shifts[None, None, :, None]), 1
    )
    return bit_table.reshape(packed.shape[0], packed.shape[1] * 8, packed.shape[2]).astype(
        jnp.float32
    )


def tile_group(owned, others, packed):
    intact = unpack_bonds(packed)
    broken = 1.0 - intact
    apart = [others[:, k, :, None] - owned[:, k, None, :] for k in range(3)]
    dist_sq = apart[0] * apart[0] + apart[1] * apart[1] + apart[2] * apart[2]
    weight = 1.0 / (1.0 + inv_horizon * dist_sq)
    spring = bond_stiff * weight * intact
    leakage = weight * broken
    mean_press = 0.5 * (others[:, 6, :, None] + owned[:, 6, None, :])
    terms = [
        spring * (others[:, 3 + k, :, None] - owned[:, 3 + k, None, :])
        - press_gain * leakage * mean_press * apart[k]
        for k in range(3)
    ]
    terms.append(leak_gain * leakage * (others[:, 6, :, None] - owned[:, 6, None, :]))
    on_owned = jnp.stack([jnp.sum(t, axis=1) for t in terms], axis=1)
    on_others = jnp.stack([-jnp.sum(t, axis=2) for t in terms], axis=1)
    return (on_owned, on_others)


def tiles(owned, others, packed):
    count = owned.shape[0]
    groups = count // group_rows

    def one_group(items):
        return tile_group(items[0], items[1], items[2])

    on_owned, on_others = lax.map(
        one_group,
        (
            owned.reshape(groups, group_rows, 7, -1),
            others.reshape(groups, group_rows, 7, -1),
            packed.reshape(groups, group_rows, packed.shape[1], packed.shape[2]),
        ),
    )
    return (on_owned.reshape(count, 4, -1), on_others.reshape(count, 4, -1))


def per_device(
    positions,
    fields,
    storage,
    velocity,
    send_list,
    remote_local,
    remote_mask,
    local_pairs,
    local_mask,
    migrate_list,
):
    points = jnp.concatenate([positions, fields], axis=1)
    width = points.shape[2]
    nbulk = lax.axis_size("bulk")
    sends = send_list[0]
    slots = sends.shape[2]
    outgoing = points[sends.reshape(-1)].reshape(3, nbulk, slots, 7, width)
    spread = lax.all_to_all(outgoing, "bulk", split_axis=1, concat_axis=1, tiled=True)
    lifted = [from_behind(spread[offset + 1], "region", offset) for offset in (-1, 1)]
    received = jnp.stack([lifted[0], spread[1], lifted[1]])
    received = received.reshape(-1, 7, width)
    bonded = remote_local[0]
    slot_count, touch = bonded.shape
    flat_local = bonded.reshape(-1)
    others = jnp.broadcast_to(received[:, None], (slot_count, touch, 7, width)).reshape(
        -1, 7, width
    )
    masks = remote_mask[0]
    on_owned, on_others = tiles(
        points[flat_local],
        others,
        masks.reshape(slot_count * touch, masks.shape[2], masks.shape[3]),
    )
    totals = jnp.zeros((points.shape[0], 4, width), jnp.float32)
    totals = totals.at[flat_local].add(on_owned)
    slot_back = (
        on_others.reshape(slot_count, touch, 4, width)
        .sum(axis=1)
        .reshape(3, nbulk, slots, 4, width)
    )
    pairs = local_pairs[0]
    first_block = pairs[:, 0]
    second_block = pairs[:, 1]
    pair_first, pair_second = tiles(points[first_block], points[second_block], local_mask[0])
    totals = totals.at[first_block].add(pair_first).at[second_block].add(pair_second)
    lowered = [from_behind(slot_back[offset + 1], "region", -offset) for offset in (-1, 1)]
    stacked_back = jnp.stack([lowered[0], slot_back[1], lowered[1]])
    returned = lax.all_to_all(stacked_back, "bulk", split_axis=1, concat_axis=1, tiled=True)
    totals = totals.at[sends.reshape(-1)].add(returned.reshape(-1, 4, width))
    new_velocity = velocity + time_step * totals[:, :3]
    displace = fields[:, :3] + time_step * new_velocity
    pressure = fields[:, 3] + time_step * totals[:, 3] / storage
    new_fields = jnp.concatenate([displace, pressure[:, None, :]], axis=1)
    moving = jnp.concatenate([new_fields, new_velocity, positions, storage[:, None, :]], axis=1)
    moves = migrate_list[0]
    chosen = moving[jnp.maximum(moves, 0).reshape(-1)].reshape(
        moves.shape[0], moves.shape[1], 11, width
    )
    chosen = jnp.where((moves >= 0)[:, :, None, None], chosen, 0.0)
    arrived = lax.all_to_all(chosen, "bulk", split_axis=0, concat_axis=0, tiled=True)
    return (new_fields, new_velocity, arrived.reshape(-1, 11, width))


def solution(mesh):
    return jax.shard_map(
        per_device,
        mesh=mesh,
        in_specs=(
            P(("region", "bulk"), None, None),
            P(("region", "bulk"), None, None),
            P(("region", "bulk"), None),
            P(("region", "bulk"), None, None),
            P(("region", "bulk"), None, None, None),
            P(("region", "bulk"), None, None),
            P(("region", "bulk"), None, None, None, None),
            P(("region", "bulk"), None, None),
            P(("region", "bulk"), None, None, None),
            P(("region", "bulk"), None, None),
        ),
        out_specs=(
            P(("region", "bulk"), None, None),
            P(("region", "bulk"), None, None),
            P(("region", "bulk"), None, None),
        ),
        check_vma=False,
    )
```

profile of v0, /device:TPU:8, one launch (start us, length us, event | category | flops | bytes accessed | tf_op | source)
XLA Modules:
  0.0 213.6 jit_solution(6573724571317715243)
XLA Ops:
  0.7 1.0 copy.369
  1.6 0.7 reduce.16
  2.4 1.0 pad_maximum_fusion.1
  3.4 0.7 gather_fusion
  4.1 1.1 copy.370
  5.2 10.2 %all-to-all-start = ((f32[3,32,1,7,128]{4,2,3,0,1:T(1,128)}), f32[3,32,1,7,128]{4,2,3,0,1:T(1,128)S(1)}, u32[]{:S(2)}, u32[]{:S(2)}) async-start(f32[3,32,1,7,128]{4,2,3,0,1:T(1,128)} %copy.370), calls=%async_computation | async-start | bytes 688128 | tf_op jit(solution)/shard_map/all_to_all | solution.py:85
  15.6 13.5 %all-to-all-done = f32[3,32,1,7,128]{4,2,3,0,1:T(1,128)S(1)} async-done(((f32[3,32,1,7,128]{4,2,3,0,1:T(1,128)}), f32[3,32,1,7,128]{4,2,3,0,1:T(1,128)S(1)}, u32[]{:S(2)}, u32[]{:S(2)}) %all-to-all-start) | async-done | bytes 344096 | tf_op jit(solution)/shard_map/all_to_all | solution.py:85
  29.2 5.9 %collective-permute-start = (f32[32,1,7,128]{3,0,2,1:T(8,128)S(1)}, f32[32,1,7,128]{3,0,2,1:T(8,128)S(1)}, u32[]{:S(2)}, u32[]{:S(2)}) collective-permute-start(f32[32,1,7,128]{3,0,2,1:T(8,128)S(1)} %bitcast.253), channel_id=1, source_target_pairs={{0,480},{32,0},{64,32},{96,64},{128,96},{160,128},{192,160},{224,1... | collective-permute-start | bytes 344072 | tf_op jit(solution)/shard_map/ppermute | solution.py:16
  35.2 0.9 gather_fusion.1
  37.6 3.3 %collective-permute-done.1 = f32[32,1,7,128]{3,0,2,1:T(8,128)S(1)} collective-permute-done((f32[32,1,7,128]{3,0,2,1:T(8,128)S(1)}, f32[32,1,7,128]{3,0,2,1:T(8,128)S(1)}, u32[]{:S(2)}, u32[]{:S(2)}) %collective-permute-start.1) | collective-permute-done | bytes 114720 | tf_op jit(solution)/shard_map/ppermute | solution.py:16
  41.2 89.6 %while.24 = (s32[]{:T(128)}, f32[12,16,4,128]{3,1,0,2:T(8,128)}, f32[12,16,4,128]{3,1,0,2:T(8,128)}, f32[12,16,7,128]{3,1,0,2:T(8,128)S(1)}, f32[12,16,7,128]{3,...) while((s32[]{:T(128)}, f32[12,16,4,128]{3,1,0,2:T(8,128)}, f32[12,16,4,128]{3,1,0,2:T(8,128)}, ...), condition=%wide.region_9.10_spmd, body=%wide.region_0.9_spmd.sunk | while | flops 11837442 | bytes 1655385 | solution.py:56
  42.3 0.9 dynamic-slice_bitcast_fusion.9
  43.2 3.6 %fusion.46 = (f32[16,16,8]{2,1,0:T(8,128)S(1)}, f32[16,128]{1,0:T(8,128)S(1)}, f32[16,128]{1,0:T(8,128)S(1)}, f32[16,16,8]{2,1,0:T(8,128)S(1)}, f32[16,128]{1,0:...) fusion(f32[16,128]{1,0:T(8,128)S(1)} %get-tuple-element.404, ...), kind=kLoop, calls=%fused_computation.34.clone.1 | loop fusion | flops 11780096 | bytes 311296 | tf_op jit(solution)/shard_map/while/body/eval_jaxpr/reduce_sum | solution.py:45
  49.8 0.9 dynamic-slice_bitcast_fusion.9
  50.7 3.6 %fusion.46 = (f32[16,16,8]{2,1,0:T(8,128)S(1)}, f32[16,128]{1,0:T(8,128)S(1)}, f32[16,128]{1,0:T(8,128)S(1)}, f32[16,16,8]{2,1,0:T(8,128)S(1)}, f32[16,128]{1,0:...) fusion(f32[16,128]{1,0:T(8,128)S(1)} %get-tuple-element.404, ...), kind=kLoop, calls=%fused_computation.34.clone.1 | loop fusion | flops 11780096 | bytes 311296 | tf_op jit(solution)/shard_map/while/body/eval_jaxpr/reduce_sum | solution.py:45
  57.2 0.9 dynamic-slice_bitcast_fusion.9
  58.1 3.6 %fusion.46 = (f32[16,16,8]{2,1,0:T(8,128)S(1)}, f32[16,128]{1,0:T(8,128)S(1)}, f32[16,128]{1,0:T(8,128)S(1)}, f32[16,16,8]{2,1,0:T(8,128)S(1)}, f32[16,128]{1,0:...) fusion(f32[16,128]{1,0:T(8,128)S(1)} %get-tuple-element.404, ...), kind=kLoop, calls=%fused_computation.34.clone.1 | loop fusion | flops 11780096 | bytes 311296 | tf_op jit(solution)/shard_map/while/body/eval_jaxpr/reduce_sum | solution.py:45
  64.7 0.9 dynamic-slice_bitcast_fusion.9
  65.6 3.6 %fusion.46 = (f32[16,16,8]{2,1,0:T(8,128)S(1)}, f32[16,128]{1,0:T(8,128)S(1)}, f32[16,128]{1,0:T(8,128)S(1)}, f32[16,16,8]{2,1,0:T(8,128)S(1)}, f32[16,128]{1,0:...) fusion(f32[16,128]{1,0:T(8,128)S(1)} %get-tuple-element.404, ...), kind=kLoop, calls=%fused_computation.34.clone.1 | loop fusion | flops 11780096 | bytes 311296 | tf_op jit(solution)/shard_map/while/body/eval_jaxpr/reduce_sum | solution.py:45
  72.2 0.9 dynamic-slice_bitcast_fusion.9
  73.1 3.6 %fusion.46 = (f32[16,16,8]{2,1,0:T(8,128)S(1)}, f32[16,128]{1,0:T(8,128)S(1)}, f32[16,128]{1,0:T(8,128)S(1)}, f32[16,16,8]{2,1,0:T(8,128)S(1)}, f32[16,128]{1,0:...) fusion(f32[16,128]{1,0:T(8,128)S(1)} %get-tuple-element.404, ...), kind=kLoop, calls=%fused_computation.34.clone.1 | loop fusion | flops 11780096 | bytes 311296 | tf_op jit(solution)/shard_map/while/body/eval_jaxpr/reduce_sum | solution.py:45
  79.6 0.9 dynamic-slice_bitcast_fusion.9
  80.5 3.6 %fusion.46 = (f32[16,16,8]{2,1,0:T(8,128)S(1)}, f32[16,128]{1,0:T(8,128)S(1)}, f32[16,128]{1,0:T(8,128)S(1)}, f32[16,16,8]{2,1,0:T(8,128)S(1)}, f32[16,128]{1,0:...) fusion(f32[16,128]{1,0:T(8,128)S(1)} %get-tuple-element.404, ...), kind=kLoop, calls=%fused_computation.34.clone.1 | loop fusion | flops 11780096 | bytes 311296 | tf_op jit(solution)/shard_map/while/body/eval_jaxpr/reduce_sum | solution.py:45
  85.3 0.7 fusion.47
  87.1 0.9 dynamic-slice_bitcast_fusion.9
  88.0 3.6 %fusion.46 = (f32[16,16,8]{2,1,0:T(8,128)S(1)}, f32[16,128]{1,0:T(8,128)S(1)}, f32[16,128]{1,0:T(8,128)S(1)}, f32[16,16,8]{2,1,0:T(8,128)S(1)}, f32[16,128]{1,0:...) fusion(f32[16,128]{1,0:T(8,128)S(1)} %get-tuple-element.404, ...), kind=kLoop, calls=%fused_computation.34.clone.1 | loop fusion | flops 11780096 | bytes 311296 | tf_op jit(solution)/shard_map/while/body/eval_jaxpr/reduce_sum | solution.py:45
  92.8 0.7 fusion.47
  94.5 0.9 dynamic-slice_bitcast_fusion.9
  95.5 3.6 %fusion.46 = (f32[16,16,8]{2,1,0:T(8,128)S(1)}, f32[16,128]{1,0:T(8,128)S(1)}, f32[16,128]{1,0:T(8,128)S(1)}, f32[16,16,8]{2,1,0:T(8,128)S(1)}, f32[16,128]{1,0:...) fusion(f32[16,128]{1,0:T(8,128)S(1)} %get-tuple-element.404, ...), kind=kLoop, calls=%fused_computation.34.clone.1 | loop fusion | flops 11780096 | bytes 311296 | tf_op jit(solution)/shard_map/while/body/eval_jaxpr/reduce_sum | solution.py:45
  102.0 0.9 dynamic-slice_bitcast_fusion.9
  102.9 3.6 %fusion.46 = (f32[16,16,8]{2,1,0:T(8,128)S(1)}, f32[16,128]{1,0:T(8,128)S(1)}, f32[16,128]{1,0:T(8,128)S(1)}, f32[16,16,8]{2,1,0:T(8,128)S(1)}, f32[16,128]{1,0:...) fusion(f32[16,128]{1,0:T(8,128)S(1)} %get-tuple-element.404, ...), kind=kLoop, calls=%fused_computation.34.clone.1 | loop fusion | flops 11780096 | bytes 311296 | tf_op jit(solution)/shard_map/while/body/eval_jaxpr/reduce_sum | solution.py:45
  109.5 0.9 dynamic-slice_bitcast_fusion.9
  110.4 3.6 %fusion.46 = (f32[16,16,8]{2,1,0:T(8,128)S(1)}, f32[16,128]{1,0:T(8,128)S(1)}, f32[16,128]{1,0:T(8,128)S(1)}, f32[16,16,8]{2,1,0:T(8,128)S(1)}, f32[16,128]{1,0:...) fusion(f32[16,128]{1,0:T(8,128)S(1)} %get-tuple-element.404, ...), kind=kLoop, calls=%fused_computation.34.clone.1 | loop fusion | flops 11780096 | bytes 311296 | tf_op jit(solution)/shard_map/while/body/eval_jaxpr/reduce_sum | solution.py:45
  115.1 0.7 fusion.47
  117.0 0.9 dynamic-slice_bitcast_fusion.9
  117.9 3.6 %fusion.46 = (f32[16,16,8]{2,1,0:T(8,128)S(1)}, f32[16,128]{1,0:T(8,128)S(1)}, f32[16,128]{1,0:T(8,128)S(1)}, f32[16,16,8]{2,1,0:T(8,128)S(1)}, f32[16,128]{1,0:...) fusion(f32[16,128]{1,0:T(8,128)S(1)} %get-tuple-element.404, ...), kind=kLoop, calls=%fused_computation.34.clone.1 | loop fusion | flops 11780096 | bytes 311296 | tf_op jit(solution)/shard_map/while/body/eval_jaxpr/reduce_sum | solution.py:45
  122.6 0.7 fusion.47
  124.4 0.9 dynamic-slice_bitcast_fusion.9
  125.4 3.6 %fusion.46 = (f32[16,16,8]{2,1,0:T(8,128)S(1)}, f32[16,128]{1,0:T(8,128)S(1)}, f32[16,128]{1,0:T(8,128)S(1)}, f32[16,16,8]{2,1,0:T(8,128)S(1)}, f32[16,128]{1,0:...) fusion(f32[16,128]{1,0:T(8,128)S(1)} %get-tuple-element.404, ...), kind=kLoop, calls=%fused_computation.34.clone.1 | loop fusion | flops 11780096 | bytes 311296 | tf_op jit(solution)/shard_map/while/body/eval_jaxpr/reduce_sum | solution.py:45
  130.1 0.7 fusion.47
  130.8 1.5 reduce_sum.153
  132.3 2.9 %collective-permute-start.3 = (f32[32,1,4,128]{3,0,2,1:T(8,128)S(1)}, f32[32,1,4,128]{3,0,2,1:T(8,128)S(1)}, u32[]{:S(2)}, u32[]{:S(2)}) collective-permute-start(f32[32,1,4,128]{3,0,2,1:T(8,128)S(1)} %get-tuple-element.282), channel_id=1, source_target_pairs={{0,480},{32,0},{64,32},{96,64},{128,96},{160,128},{192,160},{224,1... | collective-permute-start | bytes 196616 | tf_op jit(solution)/shard_map/ppermute | solution.py:16
  135.2 29.9 %while.25 = (s32[]{:T(128)}, f32[4,16,4,128]{3,1,0,2:T(8,128)}, f32[4,16,4,128]{3,1,0,2:T(8,128)}, f32[4,16,7,128]{3,2,1,0:T(8,128)S(1)}, f32[4,16,7,128]{3,1,2,...) while((s32[]{:T(128)}, f32[4,16,4,128]{3,1,0,2:T(8,128)}, f32[4,16,4,128]{3,1,0,2:T(8,128)}, ...), condition=%wide.region_20.21_spmd, body=%wide.region_11.20_spmd.sunk | while | flops 11837442 | bytes 1655385 | solution.py:56
  136.4 0.9 dynamic-slice_bitcast_fusion.11
  137.3 3.6 %fusion.48 = (f32[16,16,8]{2,1,0:T(8,128)S(1)}, f32[16,128]{1,0:T(8,128)S(1)}, f32[16,128]{1,0:T(8,128)S(1)}, f32[16,16,8]{2,1,0:T(8,128)S(1)}, f32[16,128]{1,0:...) fusion(f32[16,128]{1,0:T(8,128)S(1)} %get-tuple-element.434, ...), kind=kLoop, calls=%fused_computation.82.clone.1 | loop fusion | flops 11780096 | bytes 311296 | tf_op jit(solution)/shard_map/while/body/eval_jaxpr/reduce_sum | solution.py:45
  143.8 0.9 dynamic-slice_bitcast_fusion.11
  144.8 3.6 %fusion.48 = (f32[16,16,8]{2,1,0:T(8,128)S(1)}, f32[16,128]{1,0:T(8,128)S(1)}, f32[16,128]{1,0:T(8,128)S(1)}, f32[16,16,8]{2,1,0:T(8,128)S(1)}, f32[16,128]{1,0:...) fusion(f32[16,128]{1,0:T(8,128)S(1)} %get-tuple-element.434, ...), kind=kLoop, calls=%fused_computation.82.clone.1 | loop fusion | flops 11780096 | bytes 311296 | tf_op jit(solution)/shard_map/while/body/eval_jaxpr/reduce_sum | solution.py:45
  151.3 0.9 dynamic-slice_bitcast_fusion.11
  152.2 3.6 %fusion.48 = (f32[16,16,8]{2,1,0:T(8,128)S(1)}, f32[16,128]{1,0:T(8,128)S(1)}, f32[16,128]{1,0:T(8,128)S(1)}, f32[16,16,8]{2,1,0:T(8,128)S(1)}, f32[16,128]{1,0:...) fusion(f32[16,128]{1,0:T(8,128)S(1)} %get-tuple-element.434, ...), kind=kLoop, calls=%fused_computation.82.clone.1 | loop fusion | flops 11780096 | bytes 311296 | tf_op jit(solution)/shard_map/while/body/eval_jaxpr/reduce_sum | solution.py:45
  158.8 0.9 dynamic-slice_bitcast_fusion.11
  159.7 3.6 %fusion.48 = (f32[16,16,8]{2,1,0:T(8,128)S(1)}, f32[16,128]{1,0:T(8,128)S(1)}, f32[16,128]{1,0:T(8,128)S(1)}, f32[16,16,8]{2,1,0:T(8,128)S(1)}, f32[16,128]{1,0:...) fusion(f32[16,128]{1,0:T(8,128)S(1)} %get-tuple-element.434, ...), kind=kLoop, calls=%fused_computation.82.clone.1 | loop fusion | flops 11780096 | bytes 311296 | tf_op jit(solution)/shard_map/while/body/eval_jaxpr/reduce_sum | solution.py:45
  165.1 0.8 copy.386
  165.9 6.4 %all-to-all-start.1 = ((f32[3,32,1,4,128]{4,3,0,2,1:T(4,128)}), f32[3,32,1,4,128]{4,3,0,2,1:T(4,128)S(1)}, u32[]{:S(2)}, u32[]{:S(2)}) async-start(f32[3,32,1,4,128]{4,3,0,2,1:T(4,128)} %copy.386), calls=%async_computation.1 | async-start | bytes 393216 | tf_op jit(solution)/shard_map/all_to_all | solution.py:115
  172.4 1.0 copy.382
  173.9 7.2 %scatter_fusion = f32[64,4,128]{2,1,0:T(4,128)S(1)} fusion(f32[64,4,128]{2,1,0:T(4,128)S(1)} %broadcast_in_dim.56, s32[192]{0:T(256)S(1)} %bitcast.260, f32[192,4,128]{2,1,0:T(4,128)S(1)} %copy.377), kind=kCustom, calls=%fused_computation.5 | custom fusion | flops 98304 | bytes 1180416 | tf_op jit(solution)/shard_map/scatter-add | solution.py:102
  181.0 2.8 %scatter_fusion.1 = f32[64,4,128]{2,1,0:T(4,128)S(1)} fusion(f32[64,4,128]{2,1,0:T(4,128)S(1)} %scatter_fusion, s32[64]{0:T(128)S(1)} %get-tuple-element.285, f32[64,4,128]{2,1,0:T(4,128)S(1)} %copy.382), kind=kCustom, calls=%fused_computation.6 | custom fusion | flops 32768 | bytes 393472 | tf_op jit(solution)/shard_map/scatter-add | solution.py:112
  183.8 2.8 %scatter_fusion.2 = f32[64,4,128]{2,1,0:T(4,128)S(1)} fusion(f32[64,4,128]{2,1,0:T(4,128)S(1)} %scatter_fusion.1, s32[64]{0:T(128)S(1)} %get-tuple-element.284, f32[64,4,128]{2,1,0:T(4,128)S(1)} %copy.384), kind=kCustom, calls=%fused_computation.7 | custom fusion | flops 32768 | bytes 393472 | tf_op jit(solution)/shard_map/scatter-add | solution.py:112
  186.7 3.9 %scatter_fusion.3 = f32[64,4,128]{2,1,0:T(4,128)S(1)} fusion(f32[64,4,128]{2,1,0:T(4,128)S(1)} %scatter_fusion.2, s32[96]{0:T(128)S(1)} %fusion.37, f32[96,4,128]{2,1,0:T(4,128)S(1)} %copy.388), kind=kCustom, calls=%fused_computation.8 | custom fusion | flops 49152 | bytes 590208 | tf_op jit(solution)/shard_map/scatter-add | solution.py:116
  190.8 0.7 concatenate.12
  192.2 0.9 copy.394
  193.1 9.7 %all-to-all-start.2 = ((f32[32,1,11,128]{3,1,2,0:T(1,128)}), f32[32,1,11,128]{3,1,2,0:T(1,128)S(1)}, u32[]{:S(2)}, u32[]{:S(2)}) async-start(f32[32,1,11,128]{3,1,2,0:T(1,128)} %copy.394), calls=%async_computation.2 | async-start | bytes 360448 | tf_op jit(solution)/shard_map/all_to_all | solution.py:127
  203.5 0.7 pad_maximum_fusion.3
  204.2 8.7 %all-to-all-done.2 = f32[32,1,11,128]{3,1,2,0:T(1,128)S(1)} async-done(((f32[32,1,11,128]{3,1,2,0:T(1,128)}), f32[32,1,11,128]{3,1,2,0:T(1,128)S(1)}, u32[]{:S(2)}, u32[]{:S(2)}) %all-to-all-start.2) | async-done | bytes 180256 | tf_op jit(solution)/shard_map/all_to_all | solution.py:127
  212.9 0.7 copy.419
  (521 shorter events, 44.9 us)
Async XLA Ops:
  0.6 14.7 %copy-start.5 = (s32[1,96,2]{1,2,0:T(2,128)S(1)}, s32[1,96,2]{1,2,0:T(2,128)}, u32[]{:S(2)}) copy-start(s32[1,96,2]{1,2,0:T(2,128)} %param.19) | copy-start | bytes 2308
  0.6 15.0 %copy-start.6 = (s32[1,64,2]{1,2,0:T(2,128)S(1)}, s32[1,64,2]{1,2,0:T(2,128)}, u32[]{:S(2)}) copy-start(s32[1,64,2]{1,2,0:T(2,128)} %param.21) | copy-start | bytes 1540
  5.2 23.9 %all-to-all-start = ((f32[3,32,1,7,128]{4,2,3,0,1:T(1,128)}), f32[3,32,1,7,128]{4,2,3,0,1:T(1,128)S(1)}, u32[]{:S(2)}, u32[]{:S(2)}) async-start(f32[3,32,1,7,128]{4,2,3,0,1:T(1,128)} %copy.370), calls=%async_computation | async-start | bytes 688128 | tf_op jit(solution)/shard_map/all_to_all | solution.py:85
  29.2 8.4 %collective-permute-start = (f32[32,1,7,128]{3,0,2,1:T(8,128)S(1)}, f32[32,1,7,128]{3,0,2,1:T(8,128)S(1)}, u32[]{:S(2)}, u32[]{:S(2)}) collective-permute-start(f32[32,1,7,128]{3,0,2,1:T(8,128)S(1)} %bitcast.253), channel_id=1, source_target_pairs={{0,480},{32,0},{64,32},{96,64},{128,96},{160,128},{192,160},{224,1... | collective-permute-start | bytes 344072 | tf_op jit(solution)/shard_map/ppermute | solution.py:16
  35.1 5.8 %collective-permute-start.1 = (f32[32,1,7,128]{3,0,2,1:T(8,128)S(1)}, f32[32,1,7,128]{3,0,2,1:T(8,128)S(1)}, u32[]{:S(2)}, u32[]{:S(2)}) collective-permute-start(f32[32,1,7,128]{3,0,2,1:T(8,128)S(1)} %bitcast.254), channel_id=1, source_target_pairs={{0,32},{32,64},{64,96},{96,128},{128,160},{160,192},{192,224},{224... | collective-permute-start | bytes 344072 | tf_op jit(solution)/shard_map/ppermute | solution.py:16
  132.3 32.8 %collective-permute-start.2 = (f32[32,1,4,128]{3,0,2,1:T(8,128)S(1)}, f32[32,1,4,128]{3,0,2,1:T(8,128)S(1)}, u32[]{:S(2)}, u32[]{:S(2)}) collective-permute-start(f32[32,1,4,128]{3,0,2,1:T(8,128)S(1)} %get-tuple-element.281), channel_id=1, source_target_pairs={{0,32},{32,64},{64,96},{96,128},{128,160},{160,192},{192,224},{224... | collective-permute-start | bytes 196616 | tf_op jit(solution)/shard_map/ppermute | solution.py:16
  132.3 32.8 %collective-permute-start.3 = (f32[32,1,4,128]{3,0,2,1:T(8,128)S(1)}, f32[32,1,4,128]{3,0,2,1:T(8,128)S(1)}, u32[]{:S(2)}, u32[]{:S(2)}) collective-permute-start(f32[32,1,4,128]{3,0,2,1:T(8,128)S(1)} %get-tuple-element.282), channel_id=1, source_target_pairs={{0,480},{32,0},{64,32},{96,64},{128,96},{160,128},{192,160},{224,1... | collective-permute-start | bytes 196616 | tf_op jit(solution)/shard_map/ppermute | solution.py:16
  135.2 37.1 %copy-start.7 = (s32[1,32,1]{1,2,0:T(1,128)S(1)}, s32[1,32,1]{1,2,0:T(1,128)}, u32[]{:S(2)}) copy-start(s32[1,32,1]{1,2,0:T(1,128)} %param.23) | copy-start | bytes 388
  135.2 37.1 %copy-start = (f32[64,4,128]{2,1,0:T(4,128)S(1)}, f32[64,4,128]{2,1,0:T(4,128)}, u32[]{:S(2)}) copy-start(f32[64,4,128]{2,1,0:T(4,128)} %param.15) | copy-start | bytes 393220
  165.1 8.3 %copy-start.2 = (f32[4,16,4,128]{3,1,0,2:T(8,128)S(1)}, f32[4,16,4,128]{3,1,0,2:T(8,128)}, u32[]{:S(2)}) copy-start(f32[4,16,4,128]{3,1,0,2:T(8,128)} %get-tuple-element.71) | copy-start | bytes 393220
  165.1 8.4 %copy-start.1 = (f32[12,16,4,128]{3,1,0,2:T(8,128)S(1)}, f32[12,16,4,128]{3,1,0,2:T(8,128)}, u32[]{:S(2)}) copy-start(f32[12,16,4,128]{3,1,0,2:T(8,128)} %get-tuple-element.69) | copy-start | bytes 1179652
  165.9 20.6 %all-to-all-start.1 = ((f32[3,32,1,4,128]{4,3,0,2,1:T(4,128)}), f32[3,32,1,4,128]{4,3,0,2,1:T(4,128)S(1)}, u32[]{:S(2)}, u32[]{:S(2)}) async-start(f32[3,32,1,4,128]{4,3,0,2,1:T(4,128)} %copy.386), calls=%async_computation.1 | async-start | bytes 393216 | tf_op jit(solution)/shard_map/all_to_all | solution.py:115
  173.8 16.8 %copy-start.4 = (f32[64,3,128]{2,0,1:T(8,128)S(1)}, f32[64,3,128]{2,0,1:T(8,128)}, u32[]{:S(2)}) copy-start(f32[64,3,128]{2,0,1:T(8,128)} %param.17) | copy-start | bytes 294916
  181.0 9.8 %copy-start.3 = (f32[64,128]{1,0:T(8,128)S(1)}, f32[64,128]{1,0:T(8,128)}, u32[]{:S(2)}) copy-start(f32[64,128]{1,0:T(8,128)} %param.16) | copy-start | bytes 98308
  193.1 19.8 %all-to-all-start.2 = ((f32[32,1,11,128]{3,1,2,0:T(1,128)}), f32[32,1,11,128]{3,1,2,0:T(1,128)S(1)}, u32[]{:S(2)}, u32[]{:S(2)}) async-start(f32[32,1,11,128]{3,1,2,0:T(1,128)} %copy.394), calls=%async_computation.2 | async-start | bytes 360448 | tf_op jit(solution)/shard_map/all_to_all | solution.py:127
where the time goes:
time: 214 us
  other arithmetic  90.8 us (42%)
  local copies, waits for them, and re-layouts  58.4 us (27%)
  starting transfers between devices  35.2 us (16%)
  waiting for transfers between devices  25.4 us (12%)
  loops' own time  2.65 us (1%)
    reduce_sum x16, other arithmetic, tile_group(): on_others = jnp.stack([-jnp.sum(t, axis=2) for t in terms], axis=1)  58.2 us
    shift_right_arithmetic x16, local copies, waits for them, and re-layouts, unpack_bonds(): jnp.right_shift(packed[:, :, None, :], shifts[None, None, :, None])  14.7 us
    all_to_all x1, waiting for transfers between devices, per_device(): lax.all_to_all(outgoing, 'bulk', split_axis=1, concat_axis=1, tiled=True)  13.5 us
    dynamic_update_slice x16, other arithmetic, tiles(): lax.map(one_group, (owned.reshape(groups, group_rows, 7, -1), others.resh...  10.6 us
    all_to_all x1, starting transfers between devices, per_device(): lax.all_to_all(outgoing, 'bulk', split_axis=1, concat_axis=1, tiled=True)  10.2 us
    all_to_all x1, starting transfers between devices, per_device(): lax.all_to_all(chosen, 'bulk', split_axis=0, concat_axis=0, tiled=True)  9.74 us
    neg x128, local copies, waits for them, and re-layouts, tile_group(): on_others = jnp.stack([-jnp.sum(t, axis=2) for t in terms], axis=1)  9.5 us
    ppermute x4, starting transfers between devices, from_behind(): lax.ppermute(shard, axis, [(i, (i + by) % peers) for i in range(peers)])  8.87 us
  transfers between devices with their start and end apart: 7, of which 3 were waited for; matrix products, arithmetic and copies ran while one was open for 22% of the time, Pallas kernels for 0%

commit v1 on v0

v1 whole, which is shorter than its diff:
```python
import functools

import jax
import jax.numpy as jnp
from jax import lax
from jax.experimental import pallas as pl
from jax.experimental.pallas import tpu as pltpu
from jax.sharding import PartitionSpec as P

bond_stiff = 0.1
press_gain = 0.05
leak_gain = 0.5
time_step = 0.5
inv_horizon = 0.25
vmem_bytes = 40 * 1024 * 1024
f32 = jnp.float32
bf16 = jnp.bfloat16


def from_behind(shard, axis, by):
    peers = lax.axis_size(axis)
    return lax.ppermute(shard, axis, [(i, (i + by) % peers) for i in range(peers)])


def features(block):
    width = block.shape[1]
    x, p, u = block[0:3], block[3:4], block[4:7]
    one = jnp.ones((1, width), f32)
    rows = jnp.concatenate([x, p, p * x, one, u, one, jnp.zeros((4, width), f32)], axis=0)
    high = rows.astype(bf16)
    rest = rows - high.astype(f32)
    middle = rest.astype(bf16)
    low = (rest - middle.astype(f32)).astype(bf16)
    return jnp.concatenate([high, middle, low], axis=0)


def terms_of(sums, x, p, u):
    mean_gain = 0.5 * press_gain
    out = [
        bond_stiff * (sums[8 + k] - u[k] * sums[11])
        - mean_gain * (p * (sums[k] - x[k] * sums[7]) + (sums[4 + k] - x[k] * sums[3]))
        for k in range(3)
    ]
    out.append(leak_gain * (sums[3] - p * sums[7]))
    return out


def block_rows(ref, first, count, stride):
    return ref[pl.ds(first, count, stride=stride), :]


def columns(blocks_ref, turned_ref):
    for g in range(turned_ref.shape[0]):
        turned_ref[g] = jnp.transpose(blocks_ref[pl.ds(g * 128, 128), :])


def bond_weights(others, owned, words, bits):
    apart = [others[k] - 0.5 * owned[k : k + 1] for k in range(3)]
    size = apart[0] * apart[0] + 1.0 + (apart[1] * apart[1] + apart[2] * apart[2])
    weight = pltpu.reciprocal(size, approx=True)
    intact = (words & bits) != 0
    high = weight.astype(bf16)
    high_wide = high.astype(f32)
    low_wide = weight - high_wide
    low = low_wide.astype(bf16)
    intact_high = jnp.where(intact, high_wide, 0.0).astype(bf16)
    intact_low = jnp.where(intact, low_wide, 0.0).astype(bf16)
    return intact_high, high, intact_low, low


def split_sums(product):
    product = product[0:16] + product[16:32] + product[32:48]
    intact, every = product[:, :128], product[:, 128:]
    return jnp.concatenate([every[0:8] - intact[0:8], intact[8:16]], axis=0)


def tile_sums(weights, owned_feature, other_feature):
    intact_high, high, intact_low, low = weights
    by_other = jnp.concatenate(
        [
            jnp.concatenate([intact_high, high], axis=1),
            jnp.concatenate([intact_low, low], axis=1),
        ],
        axis=0,
    )
    on_owned = jnp.dot(
        jnp.concatenate([other_feature, other_feature], axis=1),
        by_other,
        preferred_element_type=f32,
    )
    by_owned = jnp.concatenate(
        [
            jnp.concatenate([intact_high, intact_low], axis=1),
            jnp.concatenate([high, low], axis=1),
        ],
        axis=0,
    )
    on_other = lax.dot_general(
        jnp.concatenate([owned_feature, owned_feature], axis=1),
        by_owned,
        (((1,), (1,)), ((), ())),
        preferred_element_type=f32,
    )
    return split_sums(on_owned), split_sums(on_other)


def tile_loop(
    slots, touch, per_step, owned_of, mask_ref, other_blocks, other_feature, turned_ref, points_ref,
    feature_ref, sums_ref, weights_ref, other_of, store_other,
):
    bits = jnp.left_shift(1, lax.broadcasted_iota(jnp.int32, (16, 8, 128), 1)).reshape(128, 128)
    steps = slots // per_step

    def weigh(step, half):
        for n in range(per_step):
            slot = step * per_step + n
            other = other_of(slot)
            turned = pltpu.roll(turned_ref[other // 16], lax.rem(128 - 8 * lax.rem(other, 16), 128), 1)
            others = [jnp.broadcast_to(0.5 * turned[:, k : k + 1], (128, 128)) for k in range(3)]
            for e in range(touch):
                tile = slot * touch + e
                owned = owned_of(slot, e)
                words = jnp.broadcast_to(mask_ref[tile][:, None, :], (16, 8, 128)).reshape(128, 128)
                a, b, c, d = bond_weights(others, points_ref[owned], words, bits)
                at = n * touch + e
                weights_ref[half, at, 0:128, 0:128] = a
                weights_ref[half, at, 0:128, 128:256] = b
                weights_ref[half, at, 128:256, 0:128] = c
                weights_ref[half, at, 128:256, 128:256] = d

    def add_up(step, half):
        for n in range(per_step):
            slot = step * per_step + n
            feature = other_feature(slot)
            on_other = None
            for e in range(touch):
                owned = owned_of(slot, e)
                kept = weights_ref[half, n * touch + e]
                parts = (kept[:128, :128], kept[:128, 128:], kept[128:, :128], kept[128:, 128:])
                on_owned, more = tile_sums(parts, feature_ref[owned], feature)
                sums_ref[owned] += on_owned
                on_other = more if on_other is None else on_other + more
            store_other(slot, on_other)

    weigh(0, 0)

    def body(k, carry):
        weigh(2 * k + 1, 1)
        add_up(2 * k, 0)
        weigh(jnp.minimum(2 * k + 2, steps - 1), 0)
        add_up(2 * k + 1, 1)
        return carry

    lax.fori_loop(0, steps // 2, body, 0)


def owned_terms(sums_ref, points_ref, count):
    rows = sums_ref.reshape(count * 16, 128)
    sums = [block_rows(rows, r, count, 16) for r in range(12)]
    flat = points_ref.reshape(count * 8, 128)
    own = [block_rows(flat, r, count, 8) for r in range(7)]
    return terms_of(sums, own[0:3], own[3], own[4:7])


def pack_kernel(sends_ref, moves_ref, positions_ref, fields_ref, out_ref, points_ref):
    count = positions_ref.shape[1]
    peers = out_ref.shape[0]
    flat = points_ref.reshape(count * 8, 128)
    for k in range(3):
        flat[pl.ds(k, count, stride=8), :] = positions_ref[k]
        flat[pl.ds(4 + k, count, stride=8), :] = block_rows(fields_ref, k, count, 4)
    flat[pl.ds(3, count, stride=8), :] = block_rows(fields_ref, 3, count, 4)
    flat[pl.ds(7, count, stride=8), :] = jnp.zeros((count, 128), f32)

    def one_peer(peer, carry):
        move = moves_ref[0, 0, peer]
        live = (move >= 0).astype(f32)
        moved = points_ref[jnp.maximum(move, 0)] * live
        for o in range(3):
            out_ref[peer, 8 * o : 8 * o + 7] = points_ref[sends_ref[o, 0, peer], 0:7]
            out_ref[peer, 8 * o + 7 : 8 * o + 8] = moved[o : o + 1]
        return carry

    lax.fori_loop(0, peers, one_peer, 0, unroll=8)


def local_kernel(pairs_ref, points_ref, mask_ref, totals_ref, feature_ref, sums_ref, turned_ref, weights_ref):
    count = points_ref.shape[0]
    tiles = mask_ref.shape[0]
    sums_ref[...] = jnp.zeros_like(sums_ref)
    columns(points_ref.reshape(count * 8, 128), turned_ref)

    def one_block(block, carry):
        feature_ref[block] = features(points_ref[block])
        return carry

    lax.fori_loop(0, count, one_block, 0, unroll=4)

    def store_other(slot, on_other):
        sums_ref[pairs_ref[1, slot]] += on_other

    tile_loop(
        tiles, 1, 4, lambda slot, e: pairs_ref[0, slot], mask_ref, None,
        lambda slot: feature_ref[pairs_ref[1, slot]], turned_ref, points_ref, feature_ref, sums_ref,
        weights_ref, lambda slot: pairs_ref[1, slot], store_other,
    )
    for k, row in enumerate(owned_terms(sums_ref, points_ref, count)):
        totals_ref[k] = row


def remote_kernel(
    groups, local_ref, totals_in_ref, points_ref, feature_ref, *rest
):
    lifted = rest[: len(groups)]
    masks = rest[len(groups) : 2 * len(groups)]
    totals_ref = rest[2 * len(groups)]
    back = rest[2 * len(groups) + 1 : 3 * len(groups) + 1]
    sums_ref, turned_ref, weights_ref, other_sums = rest[3 * len(groups) + 1 :]
    count = points_ref.shape[0]
    slots = lifted[0].shape[0]
    sums_ref[...] = jnp.zeros_like(sums_ref)
    for part, group in enumerate(groups):
        blocks = lifted[part]
        columns(blocks.reshape(slots * 8, 128), turned_ref)

        def store_other(slot, on_other):
            other_sums[slot] = on_other

        tile_loop(
            slots, 2, 2, lambda slot, e: local_ref[e, group * slots + slot], masks[part], None,
            lambda slot: features(blocks[slot]), turned_ref, points_ref, feature_ref, sums_ref,
            weights_ref, lambda slot: slot, store_other,
        )
        back_rows = back[part].reshape(slots * 4, 128)
        for k, row in enumerate(owned_terms(other_sums, blocks, slots)):
            back_rows[pl.ds(k, slots, stride=4), :] = row
    for k, row in enumerate(owned_terms(sums_ref, points_ref, count)):
        totals_ref[k] = totals_in_ref[k] + row


def update_kernel(
    sends_ref, moves_ref, totals_ref, returned_ref, fields_ref, velocity_ref, storage_ref,
    new_fields_ref, new_velocity_ref, moving_ref, sums_ref, rows_ref,
):
    count = storage_ref.shape[0]
    peers = returned_ref.shape[0]
    sums_ref[...] = jnp.zeros_like(sums_ref)

    def one_peer(peer, carry):
        for o in range(3):
            sums_ref[sends_ref[o, 0, peer]] += returned_ref[peer, 4 * o : 4 * o + 4]
        return carry

    lax.fori_loop(0, peers, one_peer, 0, unroll=4)
    sums = sums_ref.reshape(count * 4, 128)
    rows = rows_ref.reshape(count * 8, 128)
    for k in range(3):
        speed = velocity_ref[k] + time_step * (totals_ref[k] + block_rows(sums, k, count, 4))
        moved = block_rows(fields_ref, k, count, 4) + time_step * speed
        new_velocity_ref[k] = speed
        new_fields_ref[pl.ds(k, count, stride=4), :] = moved
        rows[pl.ds(k, count, stride=8), :] = moved
        rows[pl.ds(4 + k, count, stride=8), :] = speed
    stored = storage_ref[...]
    pressure = (
        block_rows(fields_ref, 3, count, 4)
        + time_step * (totals_ref[3] + block_rows(sums, 3, count, 4)) / stored
    )
    new_fields_ref[pl.ds(3, count, stride=4), :] = pressure
    rows[pl.ds(3, count, stride=8), :] = pressure
    rows[pl.ds(7, count, stride=8), :] = stored

    def one_move(peer, carry):
        move = moves_ref[0, 0, peer]
        moving_ref[peer] = rows_ref[jnp.maximum(move, 0)] * (move >= 0).astype(f32)
        return carry

    lax.fori_loop(0, peers, one_move, 0, unroll=4)


def arrive_kernel(late_ref, early_ref, out_ref):
    peers = late_ref.shape[0]
    late = late_ref.reshape(peers * 8, 128)
    early = early_ref.reshape(peers * 24, 128)
    for k in range(7):
        out_ref[k] = block_rows(late, k, peers, 8)
    for k in range(3):
        out_ref[7 + k] = block_rows(early, 8 * k + 7, peers, 24)
    out_ref[10] = block_rows(late, 7, peers, 8)


def in_vmem():
    return pl.BlockSpec(memory_space=pltpu.VMEM)


def in_smem():
    return pl.BlockSpec(memory_space=pltpu.SMEM)


def params():
    return pltpu.CompilerParams(vmem_limit_bytes=vmem_bytes)


def cost(flops):
    return pl.CostEstimate(flops=flops, bytes_accessed=2 * 1024 * 1024, transcendentals=0)


def shape(*dims, dtype=f32):
    return jax.ShapeDtypeStruct(dims, dtype)


def remote_tiles(groups, local, totals, points, feature, lifted, mask):
    count = points.shape[0]
    slots = lifted[0].shape[0]
    tiles = 2 * slots
    return pl.pallas_call(
        functools.partial(remote_kernel, groups),
        grid=(1,),
        out_shape=[shape(4, count, 128)] + [shape(slots, 4, 128)] * len(groups),
        in_specs=[in_smem()]
        + [in_vmem()] * (3 + len(groups))
        + [pl.BlockSpec((tiles, 16, 128), functools.partial(lambda g, i: (g, 0, 0), g)) for g in groups],
        out_specs=[in_vmem()] * (1 + len(groups)),
        scratch_shapes=[
            pltpu.VMEM((count, 16, 128), f32),
            pltpu.VMEM((slots // 16, 128, 128), f32),
            pltpu.VMEM((2, 4, 256, 256), bf16),
            pltpu.VMEM((slots, 16, 128), f32),
        ],
        compiler_params=params(),
        cost_estimate=cost(len(groups) * 4 * 10**9),
        name="remote_tiles",
    )(local, totals, points, feature, *lifted, *([mask] * len(groups)))


def per_device(
    positions,
    fields,
    storage,
    velocity,
    send_list,
    remote_local,
    remote_mask,
    local_pairs,
    local_mask,
    migrate_list,
):
    count = positions.shape[0]
    peers = send_list.shape[2]
    sends = send_list[0].transpose(0, 2, 1)
    moves = migrate_list.transpose(0, 2, 1)
    rows_first = positions.transpose(1, 0, 2)
    flat_fields = fields.reshape(count * 4, 128)
    outgoing, points = pl.pallas_call(
        pack_kernel,
        out_shape=[shape(peers, 24, 128), shape(count, 8, 128)],
        in_specs=[in_smem(), in_smem(), in_vmem(), in_vmem()],
        out_specs=[in_vmem()] * 2,
        compiler_params=params(),
        name="pack",
    )(sends, moves, rows_first, flat_fields)
    spread = lax.all_to_all(outgoing, "bulk", split_axis=0, concat_axis=0, tiled=True)
    pairs = local_pairs[0].transpose(1, 0)
    tiles = local_mask.shape[1]
    totals, feature = pl.pallas_call(
        local_kernel,
        out_shape=[shape(4, count, 128), shape(count, 48, 128, dtype=bf16)],
        in_specs=[in_smem(), in_vmem(), in_vmem()],
        out_specs=[in_vmem()] * 2,
        scratch_shapes=[
            pltpu.VMEM((count, 16, 128), f32),
            pltpu.VMEM((count // 16, 128, 128), f32),
            pltpu.VMEM((2, 4, 256, 256), bf16),
        ],
        compiler_params=params(),
        cost_estimate=cost(4 * 10**9),
        name="local_tiles",
    )(pairs, points, local_mask[0])
    lifted = [
        from_behind(spread[:, 8 * (offset + 1) : 8 * (offset + 1) + 8], "region", offset)
        for offset in (-1, 1)
    ]
    local = remote_local[0].transpose(1, 0)
    mask = remote_mask[0].reshape(-1, remote_mask.shape[3], remote_mask.shape[4])
    totals, here_back = remote_tiles((1,), local, totals, points, feature, [spread[:, 8:16]], mask)
    totals, down_back, up_back = remote_tiles((0, 2), local, totals, points, feature, lifted, mask)
    lowered = [from_behind(part, "region", -offset) for part, offset in ((down_back, -1), (up_back, 1))]
    stacked = jnp.concatenate([lowered[0], here_back, lowered[1]], axis=1)
    returned = lax.all_to_all(stacked, "bulk", split_axis=0, concat_axis=0, tiled=True)
    new_fields, new_velocity, moving = pl.pallas_call(
        update_kernel,
        out_shape=[shape(count * 4, 128), shape(3, count, 128), shape(peers, 8, 128)],
        in_specs=[in_smem()] * 2 + [in_vmem()] * 5,
        out_specs=[in_vmem()] * 3,
        scratch_shapes=[pltpu.VMEM((count, 4, 128), f32), pltpu.VMEM((count, 8, 128), f32)],
        compiler_params=params(),
        name="update",
    )(sends, moves, totals, returned, flat_fields, velocity.transpose(1, 0, 2), storage)
    late = lax.all_to_all(moving, "bulk", split_axis=0, concat_axis=0, tiled=True)
    arrived = pl.pallas_call(
        arrive_kernel,
        out_shape=shape(11, peers, 128),
        in_specs=[in_vmem()] * 2,
        out_specs=in_vmem(),
        compiler_params=params(),
        name="arrive",
    )(late, spread)
    return (
        new_fields.reshape(count, 4, 128),
        new_velocity.transpose(1, 0, 2),
        arrived.transpose(1, 0, 2),
    )


def solution(mesh):
    spec = lambda rank: P(("region", "bulk"), *([None] * (rank - 1)))
    return jax.shard_map(
        per_device,
        mesh=mesh,
        in_specs=tuple(spec(rank) for rank in (3, 3, 2, 3, 4, 3, 5, 3, 4, 3)),
        out_specs=(spec(3), spec(3), spec(3)),
        check_vma=False,
    )
```

time: 214 us -> 104 us (0.49)
  other arithmetic: 90.8 us -> 0.05 us
  local copies, waits for them, and re-layouts: 58.4 us -> 4.91 us
  Pallas kernels: 0 us -> 40.9 us
  blocking collectives: 0 us -> 34.3 us
  waiting for transfers between devices: 25.4 us -> 2.48 us
  starting transfers between devices: 35.2 us -> 20.6 us
  loops' own time: 2.65 us -> 0 us
    reduce_sum x17 -> x0, other arithmetic: 59.7 us -> none  [the longest x16 58.2 us: tile_group(): on_others = jnp.stack([-jnp.sum(t, axis=2) for t in terms], axis=1)]
    pallas_call x0 -> x6, Pallas kernels: none -> 40.9 us  [the longest x2 24.3 us: remote_tiles(): pl.pallas_call(functools.partial(remote_kernel, groups), grid=(1,), out_s...]
    all_to_all x0 -> x2, blocking collectives: none -> 34.3 us  [the longest x1 20.4 us: per_device(): lax.all_to_all(stacked, 'bulk', split_axis=0, concat_axis=0, tiled=True)]
    all_to_all x3 -> x1, waiting for transfers between devices: 22.1 us -> 0.53 us  [per_device(): lax.all_to_all(outgoing, 'bulk', split_axis=0, concat_axis=0, tiled=True)]
    scatter-add x4 -> x0, other arithmetic: 16.6 us -> none  [the longest x1 7.16 us: per_device(): totals = totals.at[flat_local].add(on_owned)]
    all_to_all x3 -> x1, starting transfers between devices: 26.3 us -> 10.2 us  [per_device(): lax.all_to_all(outgoing, 'bulk', split_axis=0, concat_axis=0, tiled=True)]
    shift_right_arithmetic x16 -> x0, local copies, waits for them, and re-layouts: 14.7 us -> none  [unpack_bonds(): jnp.right_shift(packed[:, :, None, :], shifts[None, None, :, None])]
    sub x128 -> x0, local copies, waits for them, and re-layouts: 11.4 us -> none  [the longest x80 6.03 us: tile_group(): others[:, 3 + k, :, None] - owned[:, 3 + k, None, :]]
  transfers between devices with their start and end apart: 7 -> 5, of which waited for: 3 -> 2; matrix products, arithmetic and copies ran while one was open for 22% -> 0% of each run, Pallas kernels for 0% -> 20%
where the time goes in v1:
time: 104 us
  Pallas kernels  40.9 us (39%)
  blocking collectives  34.3 us (33%)
  starting transfers between devices  20.6 us (20%)
  local copies, waits for them, and re-layouts  4.91 us (5%)
  waiting for transfers between devices  2.48 us (2%)
    pallas_call x2, Pallas kernels, remote_tiles(): pl.pallas_call(functools.partial(remote_kernel, groups), grid=(1,), out_s...  24.3 us
    all_to_all x1, blocking collectives, per_device(): lax.all_to_all(stacked, 'bulk', split_axis=0, concat_axis=0, tiled=True)  20.4 us
    all_to_all x1, blocking collectives, per_device(): lax.all_to_all(moving, 'bulk', split_axis=0, concat_axis=0, tiled=True)  13.9 us
    pallas_call x1, Pallas kernels, per_device(): pl.pallas_call(local_kernel, out_shape=[shape(4, count, 128), shape(count...  12.4 us
    ppermute x4, starting transfers between devices, from_behind(): lax.ppermute(shard, axis, [(i, (i + by) % peers) for i in range(peers)])  10.4 us
    all_to_all x1, starting transfers between devices, per_device(): lax.all_to_all(outgoing, 'bulk', split_axis=0, concat_axis=0, tiled=True)  10.2 us
    unnamed x26, local copies, waits for them, and re-layouts  4.88 us
  transfers between devices with their start and end apart: 5, of which 2 were waited for; matrix products, arithmetic and copies ran while one was open for 0% of the time, Pallas kernels for 20%

profile of v1, /device:TPU:8, one launch (start us, length us, event | category | flops | bytes accessed | tf_op | source)
XLA Modules:
  0.0 104.0 jit_solution(7518625765020335053)
XLA Ops:
  0.6 0.0 copy-start
  0.6 0.9 copy-done
  1.5 0.0 copy-start.2
  1.5 0.9 copy-done.2
  2.4 0.0 copy-start.5
  2.4 0.7 copy-done.5
  3.1 0.0 copy-start.7
  3.1 0.7 copy-done.7
  3.8 1.6 %pack.1 = (f32[32,24,128]{2,1,0:T(8,128)}, f32[64,8,128]{2,1,0:T(8,128)S(1)}) custom-call(s32[3,1,32]{2,1,0:T(1,128)S(1)} %bitcast.20, s32[1,1,32]{2,1,0:T(1,128)S(1)} %bitcast.22, f32[3,64,128]{2,1,0:T(8,128)S(1)} %bitcast.18, f32[256,128]{1,0:T(8,128)S(1)} %bitcast.16), custom_call_target="tpu_custom_call" | custom-call | tf_op jit(solution)/shard_map/pack/pallas_call | solution.py:354
  5.4 10.2 %all-to-all-start = ((f32[32,24,128]{2,1,0:T(8,128)}), f32[32,24,128]{2,1,0:T(8,128)S(1)}, u32[]{:S(2)}, u32[]{:S(2)}) async-start(f32[32,24,128]{2,1,0:T(8,128)} %get-tuple-element.18), calls=%async_computation | async-start | bytes 786432 | tf_op jit(solution)/shard_map/all_to_all | solution.py:362
  15.5 0.0 copy-start.10
  15.6 1.0 copy-done.10
  16.6 0.0 copy-start.11
  16.6 0.7 copy-done.11
  17.3 0.0 copy-start.9
  17.3 0.0 copy-start.12
  17.3 12.4 %local_tiles.1 = (f32[4,64,128]{2,1,0:T(8,128)S(1)}, bf16[64,48,128]{2,1,0:T(8,128)(2,1)S(1)}) custom-call(s32[2,64]{1,0:T(2,128)S(1)} %bitcast.28, f32[64,8,128]{2,1,0:T(8,128)S(1)} %get-tuple-element.15.points_ref, s32[64,16,128]{2,1,0:T(8,128)S(1)} %bitcast.27), custom_call_target="tpu_custom_call" | custom-call | flops 4000000000 | bytes 2097152 | tf_op jit(solution)/shard_map/local_tiles/pallas_call | solution.py:365
  29.7 0.5 all-to-all-done.early_ref
  30.3 0.0 collective-permute-start.1
  30.3 7.4 %collective-permute-start = (f32[32,8,128]{2,1,0:T(8,128)S(1)}, f32[32,8,128]{2,1,0:T(8,128)S(1)}, u32[]{:S(2)}, u32[]{:S(2)}) collective-permute-start(f32[32,8,128]{2,1,0:T(8,128)S(1)} %get-tuple-element.28), channel_id=1, source_target_pairs={{0,480},{32,0},{64,32},{96,64},{128,96},{160,128},{192,160},{224,1... | collective-permute-start | bytes 393224 | tf_op jit(solution)/shard_map/ppermute | solution.py:22
  37.7 0.0 copy-done.9
  37.7 0.0 copy-done.12
  37.7 8.4 %remote_tiles.2 = (f32[4,64,128]{2,1,0:T(8,128)S(1)}, f32[32,4,128]{2,1,0:T(4,128)S(1)}) custom-call(s32[2,96]{1,0:T(2,128)S(1)} %bitcast.29, f32[4,64,128]{2,1,0:T(8,128)S(1)} %get-tuple-element.16.totals_in_ref, f32[64,8,128]{2,1,0:T(8,128)S(1)} %get-tuple-element.15.points_ref, bf16[64,48,128]{2,1,0:T(8,128)(2,1)S(1)} %get-tuple-element.17.feature_ref, ...), custom_call_target="tpu_custom_call" | custom-call | flops 4000000000 | bytes 2097152 | tf_op jit(solution)/shard_map/remote_tiles/pallas_call | solution.py:316
  46.1 0.0 collective-permute-done.1.rest_1_
  46.1 0.0 collective-permute-done.rest_0_
  46.1 0.0 copy-start.1
  46.1 0.0 copy-start.3
  46.2 0.0 copy-start.4
  46.2 0.0 copy-start.6
  46.2 0.0 copy-start.8
  46.2 15.9 %remote_tiles.3 = (f32[4,64,128]{2,1,0:T(8,128)S(1)}, f32[32,4,128]{2,1,0:T(4,128)S(1)}, f32[32,4,128]{2,1,0:T(4,128)S(1)}) custom-call(s32[2,96]{1,0:T(2,128)S(1)} %bitcast.30, f32[4,64,128]{2,1,0:T(8,128)S(1)} %get-tuple-element.19.totals_in_ref, f32[64,8,128]{2,1,0:T(8,128)S(1)} %get-tuple-element.15.points_ref, ...), custom_call_target="tpu_custom_call" | custom-call | flops 8000000000 | bytes 2097152 | tf_op jit(solution)/shard_map/remote_tiles/pallas_call | solution.py:316
  62.1 0.0 collective-permute-start.2
  62.2 2.9 %collective-permute-start.3 = (f32[32,4,128]{2,1,0:T(4,128)S(1)}, f32[32,4,128]{2,1,0:T(4,128)S(1)}, u32[]{:S(2)}, u32[]{:S(2)}) collective-permute-start(f32[32,4,128]{2,1,0:T(4,128)S(1)} %get-tuple-element.23), channel_id=1, source_target_pairs={{0,480},{32,0},{64,32},{96,64},{128,96},{160,128},{192,160},{224,1... | collective-permute-start | bytes 196616 | tf_op jit(solution)/shard_map/ppermute | solution.py:22
  65.1 1.9 %collective-permute-done.2 = f32[32,4,128]{2,1,0:T(4,128)S(1)} collective-permute-done((f32[32,4,128]{2,1,0:T(4,128)S(1)}, f32[32,4,128]{2,1,0:T(4,128)S(1)}, u32[]{:S(2)}, u32[]{:S(2)}) %collective-permute-start.2) | collective-permute-done | bytes 65568 | tf_op jit(solution)/shard_map/ppermute | solution.py:22
  67.1 0.0 collective-permute-done.3
  67.1 20.4 %all_to_all.15.returned_ref = f32[32,12,128]{2,1,0:T(8,128)S(1)} all-to-all(f32[32,12,128]{2,1,0:T(8,128)S(1)} %pad_maximum_fusion), channel_id=1, replica_groups=mesh['region'=16,'bulk'=32] {'bulk'}, dimensions={0} | all-to-all | bytes 393216 | tf_op jit(solution)/shard_map/all_to_all | solution.py:389
  87.5 0.0 copy-done.1
  87.5 0.0 copy-done.3
  87.5 0.0 copy-done.4
  87.5 0.0 copy-done.6
  87.5 0.0 copy-done.8
  87.5 1.8 %update.1 = (f32[256,128]{1,0:T(8,128)}, f32[3,64,128]{2,1,0:T(8,128)}, f32[32,8,128]{2,1,0:T(8,128)S(1)}) custom-call(s32[3,1,32]{2,1,0:T(1,128)S(1)} %bitcast.21, s32[1,1,32]{2,1,0:T(1,128)S(1)} %bitcast.23, f32[4,64,128]{2,1,0:T(8,128)S(1)} %get-tuple-element.20.totals_ref, f32[32,12,128]{2,1,0:T(8,128)S(1)} %all_to_all.15.returned_ref, ...), custom_call_target="tpu_custom_call" | custom-call | tf_op jit(solution)/shard_map/update/pallas_call | solution.py:390
  89.4 13.9 %all_to_all.16.late_ref = f32[32,8,128]{2,1,0:T(8,128)S(1)} all-to-all(f32[32,8,128]{2,1,0:T(8,128)S(1)} %get-tuple-element.26), channel_id=1, replica_groups=mesh['region'=16,'bulk'=32] {'bulk'}, dimensions={0} | all-to-all | bytes 262144 | tf_op jit(solution)/shard_map/all_to_all | solution.py:399
  103.3 0.7 arrive.1
  (2 shorter events, 0.1 us)
Async XLA Ops:
  0.6 0.9 copy-start
  1.5 0.9 copy-start.2
  2.4 0.7 copy-start.5
  3.1 0.7 copy-start.7
  5.4 24.9 %all-to-all-start = ((f32[32,24,128]{2,1,0:T(8,128)}), f32[32,24,128]{2,1,0:T(8,128)S(1)}, u32[]{:S(2)}, u32[]{:S(2)}) async-start(f32[32,24,128]{2,1,0:T(8,128)} %get-tuple-element.18), calls=%async_computation | async-start | bytes 786432 | tf_op jit(solution)/shard_map/all_to_all | solution.py:362
  15.5 1.0 %copy-start.10 = (s32[1,64,16,128]{3,2,1,0:T(8,128)S(1)}, s32[1,64,16,128]{3,2,1,0:T(8,128)}, u32[]{:S(2)}) copy-start(s32[1,64,16,128]{3,2,1,0:T(8,128)} %param.18) | copy-start | bytes 1572868
  16.6 0.7 copy-start.11
  17.3 20.5 %copy-start.9 = (s32[1,96,2,16,128]{4,3,2,1,0:T(8,128)S(1)}, s32[1,96,2,16,128]{4,3,2,1,0:T(8,128)}, u32[]{:S(2)}) copy-start(s32[1,96,2,16,128]{4,3,2,1,0:T(8,128)} %param.16) | copy-start | bytes 4718596
  17.3 20.5 %copy-start.12 = (s32[1,96,2]{1,2,0:T(2,128)S(1)}, s32[1,96,2]{1,2,0:T(2,128)}, u32[]{:S(2)}) copy-start(s32[1,96,2]{1,2,0:T(2,128)} %param.15) | copy-start | bytes 2308
  30.3 15.8 %collective-permute-start.1 = (f32[32,8,128]{2,1,0:T(8,128)S(1)}, f32[32,8,128]{2,1,0:T(8,128)S(1)}, u32[]{:S(2)}, u32[]{:S(2)}) collective-permute-start(f32[32,8,128]{2,1,0:T(8,128)S(1)} %get-tuple-element.27), channel_id=1, source_target_pairs={{0,32},{32,64},{64,96},{96,128},{128,160},{160,192},{192,224},{224... | collective-permute-start | bytes 393224 | tf_op jit(solution)/shard_map/ppermute | solution.py:22
  30.3 15.8 %collective-permute-start = (f32[32,8,128]{2,1,0:T(8,128)S(1)}, f32[32,8,128]{2,1,0:T(8,128)S(1)}, u32[]{:S(2)}, u32[]{:S(2)}) collective-permute-start(f32[32,8,128]{2,1,0:T(8,128)S(1)} %get-tuple-element.28), channel_id=1, source_target_pairs={{0,480},{32,0},{64,32},{96,64},{128,96},{160,128},{192,160},{224,1... | collective-permute-start | bytes 393224 | tf_op jit(solution)/shard_map/ppermute | solution.py:22
  46.1 41.4 %copy-start.1 = (f32[64,4,128]{2,1,0:T(4,128)S(1)}, f32[64,4,128]{2,1,0:T(4,128)}, u32[]{:S(2)}) copy-start(f32[64,4,128]{2,1,0:T(4,128)} %param.11) | copy-start | bytes 393220
  46.1 41.4 %copy-start.3 = (f32[64,3,128]{2,0,1:T(8,128)S(1)}, f32[64,3,128]{2,0,1:T(8,128)}, u32[]{:S(2)}) copy-start(f32[64,3,128]{2,0,1:T(8,128)} %param.13) | copy-start | bytes 294916
  46.2 41.3 %copy-start.4 = (f32[64,128]{1,0:T(8,128)S(1)}, f32[64,128]{1,0:T(8,128)}, u32[]{:S(2)}) copy-start(f32[64,128]{1,0:T(8,128)} %storage_ref.1) | copy-start | bytes 98308
  46.2 41.3 %copy-start.6 = (s32[1,3,32,1]{2,3,1,0:T(1,128)S(1)}, s32[1,3,32,1]{2,3,1,0:T(1,128)}, u32[]{:S(2)}) copy-start(s32[1,3,32,1]{2,3,1,0:T(1,128)} %param.14) | copy-start | bytes 1156
  46.2 41.3 %copy-start.8 = (s32[1,32,1]{1,2,0:T(1,128)S(1)}, s32[1,32,1]{1,2,0:T(1,128)}, u32[]{:S(2)}) copy-start(s32[1,32,1]{1,2,0:T(1,128)} %param.19) | copy-start | bytes 388
  62.1 4.9 %collective-permute-start.2 = (f32[32,4,128]{2,1,0:T(4,128)S(1)}, f32[32,4,128]{2,1,0:T(4,128)S(1)}, u32[]{:S(2)}, u32[]{:S(2)}) collective-permute-start(f32[32,4,128]{2,1,0:T(4,128)S(1)} %get-tuple-element.21), channel_id=1, source_target_pairs={{0,32},{32,64},{64,96},{96,128},{128,160},{160,192},{192,224},{224... | collective-permute-start | bytes 196616 | tf_op jit(solution)/shard_map/ppermute | solution.py:22
  62.2 4.9 %collective-permute-start.3 = (f32[32,4,128]{2,1,0:T(4,128)S(1)}, f32[32,4,128]{2,1,0:T(4,128)S(1)}, u32[]{:S(2)}, u32[]{:S(2)}) collective-permute-start(f32[32,4,128]{2,1,0:T(4,128)S(1)} %get-tuple-element.23), channel_id=1, source_target_pairs={{0,480},{32,0},{64,32},{96,64},{128,96},{160,128},{192,160},{224,1... | collective-permute-start | bytes 196616 | tf_op jit(solution)/shard_map/ppermute | solution.py:22

commit v2 on v1

--- a/solution.py
+++ b/solution.py
@@ -49,9 +49,10 @@
     return ref[pl.ds(first, count, stride=stride), :]
 
 
-def columns(blocks_ref, turned_ref):
+def turn(blocks, turned_ref):
     for g in range(turned_ref.shape[0]):
-        turned_ref[g] = jnp.transpose(blocks_ref[pl.ds(g * 128, 128), :])
+        group = jnp.concatenate([blocks(16 * g + n) for n in range(16)], axis=0)
+        turned_ref[g] = 0.5 * jnp.transpose(group)
 
 
 def bond_weights(others, owned, words, bits):
@@ -60,11 +61,10 @@
     weight = pltpu.reciprocal(size, approx=True)
     intact = (words & bits) != 0
     high = weight.astype(bf16)
-    high_wide = high.astype(f32)
-    low_wide = weight - high_wide
-    low = low_wide.astype(bf16)
-    intact_high = jnp.where(intact, high_wide, 0.0).astype(bf16)
-    intact_low = jnp.where(intact, low_wide, 0.0).astype(bf16)
+    low = (weight - high.astype(f32)).astype(bf16)
+    none = jnp.zeros((128, 128), bf16)
+    intact_high = jnp.where(intact, high, none)
+    intact_low = jnp.where(intact, low, none)
     return intact_high, high, intact_low, low
 
 
@@ -105,8 +105,8 @@
 
 
 def tile_loop(
-    slots, touch, per_step, owned_of, mask_ref, other_blocks, other_feature, turned_ref, points_ref,
-    feature_ref, sums_ref, weights_ref, other_of, store_other,
+    slots, touch, per_step, owned_of, other_of, other_block, mask_ref, turned_ref, points_ref,
+    feature_ref, sums_ref, weights_ref, other_feature_ref, store_other,
 ):
     bits = jnp.left_shift(1, lax.broadcasted_iota(jnp.int32, (16, 8, 128), 1)).reshape(128, 128)
     steps = slots // per_step
@@ -115,12 +115,20 @@
         for n in range(per_step):
             slot = step * per_step + n
             other = other_of(slot)
-            turned = pltpu.roll(turned_ref[other // 16], lax.rem(128 - 8 * lax.rem(other, 16), 128), 1)
-            others = [jnp.broadcast_to(0.5 * turned[:, k : k + 1], (128, 128)) for k in range(3)]
+            if other_block is not None:
+                other_feature_ref[half, n] = features(other_block(slot))
+            turned = turned_ref[other // 16]
+            lane = 8 * lax.rem(other, 16)
+            others = [
+                jnp.take_along_axis(turned, jnp.full((128, 128), lane + k, jnp.int32), axis=1)
+                for k in range(3)
+            ]
             for e in range(touch):
                 tile = slot * touch + e
                 owned = owned_of(slot, e)
-                words = jnp.broadcast_to(mask_ref[tile][:, None, :], (16, 8, 128)).reshape(128, 128)
+                words = jnp.concatenate(
+                    [mask_ref[tile, pl.ds(j, 8, stride=0), :] for j in range(16)], axis=0
+                )
                 a, b, c, d = bond_weights(others, points_ref[owned], words, bits)
                 at = n * touch + e
                 weights_ref[half, at, 0:128, 0:128] = a
@@ -131,7 +139,10 @@
     def add_up(step, half):
         for n in range(per_step):
             slot = step * per_step + n
-            feature = other_feature(slot)
+            if other_block is not None:
+                feature = other_feature_ref[half, n]
+            else:
+                feature = feature_ref[other_of(slot)]
             on_other = None
             for e in range(touch):
                 owned = owned_of(slot, e)
@@ -147,24 +158,46 @@
     def body(k, carry):
         weigh(2 * k + 1, 1)
         add_up(2 * k, 0)
-        weigh(jnp.minimum(2 * k + 2, steps - 1), 0)
+        weigh(2 * k + 2, 0)
         add_up(2 * k + 1, 1)
         return carry
 
-    lax.fori_loop(0, steps // 2, body, 0)
-
-
-def owned_terms(sums_ref, points_ref, count):
-    rows = sums_ref.reshape(count * 16, 128)
-    sums = [block_rows(rows, r, count, 16) for r in range(12)]
-    flat = points_ref.reshape(count * 8, 128)
-    own = [block_rows(flat, r, count, 8) for r in range(7)]
-    return terms_of(sums, own[0:3], own[3], own[4:7])
-
-
-def pack_kernel(sends_ref, moves_ref, positions_ref, fields_ref, out_ref, points_ref):
+    lax.fori_loop(0, steps // 2 - 1, body, 0)
+    weigh(steps - 1, 1)
+    add_up(steps - 2, 0)
+    add_up(steps - 1, 1)
+
+
+def owned_terms(sums_ref, points, count):
+    rows = sums_ref.reshape(sums_ref.shape[0] * 16, 128)
+    return lambda first: terms_of(
+        [block_rows(rows, first * 16 + r, count, 16) for r in range(12)],
+        [points(r) for r in range(3)],
+        points(3),
+        [points(4 + r) for r in range(3)],
+    )
+
+
+def fetch(copies):
+    for copy in copies:
+        copy.start()
+    for copy in copies:
+        copy.wait()
+
+
+def pack_kernel(
+    sends_any, moves_any, positions_any, fields_any, down_ref, here_ref, up_ref, going_ref, points_ref,
+    sends_ref, moves_ref, positions_ref, fields_ref, sems,
+):
+    pairs = (
+        (positions_any, positions_ref),
+        (fields_any, fields_ref),
+        (sends_any, sends_ref),
+        (moves_any, moves_ref),
+    )
+    fetch([pltpu.make_async_copy(a, b, sems.at[n]) for n, (a, b) in enumerate(pairs)])
     count = positions_ref.shape[1]
-    peers = out_ref.shape[0]
+    peers = here_ref.shape[0]
     flat = points_ref.reshape(count * 8, 128)
     for k in range(3):
         flat[pl.ds(k, count, stride=8), :] = positions_ref[k]
@@ -173,68 +206,110 @@
     flat[pl.ds(7, count, stride=8), :] = jnp.zeros((count, 128), f32)
 
     def one_peer(peer, carry):
+        for o, out in enumerate((down_ref, here_ref, up_ref)):
+            out[peer] = points_ref[sends_ref[o, 0, peer]]
         move = moves_ref[0, 0, peer]
-        live = (move >= 0).astype(f32)
-        moved = points_ref[jnp.maximum(move, 0)] * live
-        for o in range(3):
-            out_ref[peer, 8 * o : 8 * o + 7] = points_ref[sends_ref[o, 0, peer], 0:7]
-            out_ref[peer, 8 * o + 7 : 8 * o + 8] = moved[o : o + 1]
+        block = points_ref[jnp.maximum(move, 0)]
+        going_ref[peer] = jnp.where(move >= 0, block, jnp.zeros_like(block))
         return carry
 
     lax.fori_loop(0, peers, one_peer, 0, unroll=8)
 
 
-def local_kernel(pairs_ref, points_ref, mask_ref, totals_ref, feature_ref, sums_ref, turned_ref, weights_ref):
+def merge_kernel(going_ref, down_ref, here_ref, up_ref, out_ref):
+    last = lax.broadcasted_iota(jnp.int32, (8, 128), 0) == 7
+
+    def one_peer(peer, carry):
+        block = going_ref[peer]
+        for o, part in enumerate((down_ref, here_ref, up_ref)):
+            out_ref[peer, 8 * o : 8 * o + 8] = jnp.where(last, block[o : o + 1], part[peer])
+        return carry
+
+    lax.fori_loop(0, out_ref.shape[0], one_peer, 0, unroll=8)
+
+
+def local_kernel(
+    pairs_ref, points_ref, mask_ref, totals_ref, feature_ref, sums_ref, turned_ref, weights_ref
+):
     count = points_ref.shape[0]
     tiles = mask_ref.shape[0]
     sums_ref[...] = jnp.zeros_like(sums_ref)
-    columns(points_ref.reshape(count * 8, 128), turned_ref)
+    turn(lambda n: points_ref[n], turned_ref)
 
     def one_block(block, carry):
         feature_ref[block] = features(points_ref[block])
         return carry
 
-    lax.fori_loop(0, count, one_block, 0, unroll=4)
+    lax.fori_loop(0, count, one_block, 0, unroll=8)
 
     def store_other(slot, on_other):
         sums_ref[pairs_ref[1, slot]] += on_other
 
     tile_loop(
-        tiles, 1, 4, lambda slot, e: pairs_ref[0, slot], mask_ref, None,
-        lambda slot: feature_ref[pairs_ref[1, slot]], turned_ref, points_ref, feature_ref, sums_ref,
-        weights_ref, lambda slot: pairs_ref[1, slot], store_other,
-    )
-    for k, row in enumerate(owned_terms(sums_ref, points_ref, count)):
+        tiles, 1, 4, lambda slot, e: pairs_ref[0, slot], lambda slot: pairs_ref[1, slot], None,
+        mask_ref, turned_ref, points_ref, feature_ref, sums_ref, weights_ref, None, store_other,
+    )
+    flat = points_ref.reshape(count * 8, 128)
+    terms = owned_terms(sums_ref, lambda r: block_rows(flat, r, count, 8), count)
+    for k, row in enumerate(terms(0)):
         totals_ref[k] = row
 
 
-def remote_kernel(
-    groups, local_ref, totals_in_ref, points_ref, feature_ref, *rest
-):
-    lifted = rest[: len(groups)]
-    masks = rest[len(groups) : 2 * len(groups)]
-    totals_ref = rest[2 * len(groups)]
-    back = rest[2 * len(groups) + 1 : 3 * len(groups) + 1]
-    sums_ref, turned_ref, weights_ref, other_sums = rest[3 * len(groups) + 1 :]
+def remote_kernel(groups, local_ref, totals_in_ref, points_ref, feature_ref, spread_ref, mask_any, *rest):
+    totals_ref = rest[0]
+    back = rest[1 : 1 + len(groups)]
+    (sums_ref, turned_ref, weights_ref, other_feature_ref, other_sums, mask_ref, sems) = rest[
+        1 + len(groups) :
+    ]
     count = points_ref.shape[0]
-    slots = lifted[0].shape[0]
+    peers = spread_ref.shape[0]
+    slots = peers * len(groups)
+    tiles = 2 * peers
+    copies = [
+        pltpu.make_async_copy(
+            mask_any.at[pl.ds(group * tiles, tiles)], mask_ref.at[pl.ds(part * tiles, tiles)], sems.at[part]
+        )
+        for part, group in enumerate(groups)
+    ]
+    for copy in copies:
+        copy.start()
+    first = groups[0]
+    apart = groups[-1] - first
+
+    def group_of(slot):
+        return first + apart * (slot // peers), lax.rem(slot, peers)
+
+    def other_block(slot):
+        group, peer = group_of(slot)
+        return spread_ref[peer, pl.ds(pl.multiple_of(8 * group, 8), 8)]
+
+    def owned_of(slot, e):
+        group, peer = group_of(slot)
+        return local_ref[e, group * peers + peer]
+
     sums_ref[...] = jnp.zeros_like(sums_ref)
+    turn(
+        lambda n: spread_ref[n % peers, 8 * groups[n // peers] : 8 * groups[n // peers] + 8], turned_ref
+    )
+    for copy in copies:
+        copy.wait()
+
+    def store_other(slot, on_other):
+        other_sums[slot] = on_other
+
+    tile_loop(
+        slots, 2, 2, owned_of, lambda slot: slot, other_block, mask_ref, turned_ref, points_ref,
+        feature_ref, sums_ref, weights_ref, other_feature_ref, store_other,
+    )
+    flat = spread_ref.reshape(peers * 24, 128)
     for part, group in enumerate(groups):
-        blocks = lifted[part]
-        columns(blocks.reshape(slots * 8, 128), turned_ref)
-
-        def store_other(slot, on_other):
-            other_sums[slot] = on_other
-
-        tile_loop(
-            slots, 2, 2, lambda slot, e: local_ref[e, group * slots + slot], masks[part], None,
-            lambda slot: features(blocks[slot]), turned_ref, points_ref, feature_ref, sums_ref,
-            weights_ref, lambda slot: slot, store_other,
-        )
-        back_rows = back[part].reshape(slots * 4, 128)
-        for k, row in enumerate(owned_terms(other_sums, blocks, slots)):
-            back_rows[pl.ds(k, slots, stride=4), :] = row
-    for k, row in enumerate(owned_terms(sums_ref, points_ref, count)):
+        terms = owned_terms(other_sums, lambda r: block_rows(flat, 8 * group + r, peers, 24), peers)
+        back_rows = back[part].reshape(peers * 4, 128)
+        for k, row in enumerate(terms(part * peers)):
+            back_rows[pl.ds(k, peers, stride=4), :] = row
+    own = points_ref.reshape(count * 8, 128)
+    terms = owned_terms(sums_ref, lambda r: block_rows(own, r, count, 8), count)
+    for k, row in enumerate(terms(0)):
         totals_ref[k] = totals_in_ref[k] + row
 
 
@@ -248,7 +323,7 @@
 
     def one_peer(peer, carry):
         for o in range(3):
-            sums_ref[sends_ref[o, 0, peer]] += returned_ref[peer, 4 * o : 4 * o + 4]
+            sums_ref[sends_ref[o, 0, peer]] += returned_ref[peer, o]
         return carry
 
     lax.fori_loop(0, peers, one_peer, 0, unroll=4)
@@ -272,7 +347,8 @@
 
     def one_move(peer, carry):
         move = moves_ref[0, 0, peer]
-        moving_ref[peer] = rows_ref[jnp.maximum(move, 0)] * (move >= 0).astype(f32)
+        block = rows_ref[jnp.maximum(move, 0)]
+        moving_ref[peer] = jnp.where(move >= 0, block, jnp.zeros_like(block))
         return carry
 
     lax.fori_loop(0, peers, one_move, 0, unroll=4)
@@ -309,28 +385,50 @@
     return jax.ShapeDtypeStruct(dims, dtype)
 
 
-def remote_tiles(groups, local, totals, points, feature, lifted, mask):
+def anywhere():
+    return pl.BlockSpec(memory_space=pl.ANY)
+
+
+def remote_tiles(groups, local, totals, points, feature, spread, mask):
     count = points.shape[0]
-    slots = lifted[0].shape[0]
-    tiles = 2 * slots
+    peers = spread.shape[0]
+    slots = peers * len(groups)
     return pl.pallas_call(
         functools.partial(remote_kernel, groups),
-        grid=(1,),
-        out_shape=[shape(4, count, 128)] + [shape(slots, 4, 128)] * len(groups),
-        in_specs=[in_smem()]
-        + [in_vmem()] * (3 + len(groups))
-        + [pl.BlockSpec((tiles, 16, 128), functools.partial(lambda g, i: (g, 0, 0), g)) for g in groups],
+        out_shape=[shape(4, count, 128)] + [shape(peers, 4, 128)] * len(groups),
+        in_specs=[in_smem()] + [in_vmem()] * 4 + [anywhere()],
         out_specs=[in_vmem()] * (1 + len(groups)),
         scratch_shapes=[
             pltpu.VMEM((count, 16, 128), f32),
             pltpu.VMEM((slots // 16, 128, 128), f32),
             pltpu.VMEM((2, 4, 256, 256), bf16),
+            pltpu.VMEM((2, 2, 48, 128), bf16),
             pltpu.VMEM((slots, 16, 128), f32),
+            pltpu.VMEM((2 * slots, 16, 128), jnp.int32),
+            pltpu.SemaphoreType.DMA((len(groups),)),
         ],
         compiler_params=params(),
         cost_estimate=cost(len(groups) * 4 * 10**9),
         name="remote_tiles",
-    )(local, totals, points, feature, *lifted, *([mask] * len(groups)))
+    )(local, totals, points, feature, spread, mask)
+
+
+def local_tiles(pairs, points, mask):
+    count = points.shape[0]
+    return pl.pallas_call(
+        local_kernel,
+        out_shape=[shape(4, count, 128), shape(count, 48, 128, dtype=bf16)],
+        in_specs=[in_smem(), in_vmem(), in_vmem()],
+        out_specs=[in_vmem()] * 2,
+        scratch_shapes=[
+            pltpu.VMEM((count, 16, 128), f32),
+            pltpu.VMEM((count // 16, 128, 128), f32),
+            pltpu.VMEM((2, 4, 256, 256), bf16),
+        ],
+        compiler_params=params(),
+        cost_estimate=cost(4 * 10**9),
+        name="local_tiles",
+    )(pairs, points, mask)
 
 
 def per_device(
@@ -351,41 +449,42 @@
     moves = migrate_list.transpose(0, 2, 1)
     rows_first = positions.transpose(1, 0, 2)
     flat_fields = fields.reshape(count * 4, 128)
-    outgoing, points = pl.pallas_call(
+    part = shape(peers, 8, 128)
+    down, here, up, going, points = pl.pallas_call(
         pack_kernel,
-        out_shape=[shape(peers, 24, 128), shape(count, 8, 128)],
-        in_specs=[in_smem(), in_smem(), in_vmem(), in_vmem()],
-        out_specs=[in_vmem()] * 2,
-        compiler_params=params(),
+        out_shape=[part, part, part, part, shape(count, 8, 128)],
+        in_specs=[anywhere()] * 4,
+        out_specs=[in_vmem()] * 5,
+        scratch_shapes=[
+            pltpu.SMEM(sends.shape, jnp.int32),
+            pltpu.SMEM(moves.shape, jnp.int32),
+            pltpu.VMEM(rows_first.shape, f32),
+            pltpu.VMEM(flat_fields.shape, f32),
+            pltpu.SemaphoreType.DMA((4,)),
+        ],
+        compiler_params=pltpu.CompilerParams(vmem_limit_bytes=60 * 1024 * 1024),
         name="pack",
     )(sends, moves, rows_first, flat_fields)
+    down = from_behind(down, "region", -1)
+    up = from_behind(up, "region", 1)
+    outgoing = pl.pallas_call(
+        merge_kernel,
+        out_shape=shape(peers, 24, 128),
+        in_specs=[in_vmem()] * 4,
+        out_specs=in_vmem(),
+        compiler_params=params(),
+        name="merge",
+    )(going, down, here, up)
+    points, outgoing = lax.optimization_barrier((points, outgoing))
     spread = lax.all_to_all(outgoing, "bulk", split_axis=0, concat_axis=0, tiled=True)
-    pairs = local_pairs[0].transpose(1, 0)
-    tiles = local_mask.shape[1]
-    totals, feature = pl.pallas_call(
-        local_kernel,
-        out_shape=[shape(4, count, 128), shape(count, 48, 128, dtype=bf16)],
-        in_specs=[in_smem(), in_vmem(), in_vmem()],
-        out_specs=[in_vmem()] * 2,
-        scratch_shapes=[
-            pltpu.VMEM((count, 16, 128), f32),
-            pltpu.VMEM((count // 16, 128, 128), f32),
-            pltpu.VMEM((2, 4, 256, 256), bf16),
-        ],
-        compiler_params=params(),
-        cost_estimate=cost(4 * 10**9),
-        name="local_tiles",
-    )(pairs, points, local_mask[0])
-    lifted = [
-        from_behind(spread[:, 8 * (offset + 1) : 8 * (offset + 1) + 8], "region", offset)
-        for offset in (-1, 1)
-    ]
+    totals, feature = local_tiles(local_pairs[0].transpose(1, 0), points, local_mask[0])
     local = remote_local[0].transpose(1, 0)
     mask = remote_mask[0].reshape(-1, remote_mask.shape[3], remote_mask.shape[4])
-    totals, here_back = remote_tiles((1,), local, totals, points, feature, [spread[:, 8:16]], mask)
-    totals, down_back, up_back = remote_tiles((0, 2), local, totals, points, feature, lifted, mask)
-    lowered = [from_behind(part, "region", -offset) for part, offset in ((down_back, -1), (up_back, 1))]
-    stacked = jnp.concatenate([lowered[0], here_back, lowered[1]], axis=1)
+    totals, down_back, up_back = remote_tiles((0, 2), local, totals, points, feature, spread, mask)
+    down_back = from_behind(down_back, "region", 1)
+    up_back = from_behind(up_back, "region", -1)
+    totals, here_back = remote_tiles((1,), local, totals, points, feature, spread, mask)
+    stacked = jnp.stack([down_back, here_back, up_back], axis=1)
     returned = lax.all_to_all(stacked, "bulk", split_axis=0, concat_axis=0, tiled=True)
     new_fields, new_velocity, moving = pl.pallas_call(
         update_kernel,

time: 104 us -> 96.1 us (0.924)
  Pallas kernels: 40.9 us -> 30.5 us
  waiting for transfers between devices: 2.48 us -> 9.97 us
  blocking collectives: 34.3 us -> 29.4 us
  local copies, waits for them, and re-layouts: 4.91 us -> 3.41 us
    pallas_call x4 -> x5, Pallas kernels: 38.4 us -> 28 us  [the longest x2 17.9 us: remote_tiles(): pl.pallas_call(functools.partial(remote_kernel, groups), out_shape=[shape...]
    all_to_all x1, blocking collectives: 20.4 us -> 15.6 us  [per_device(): lax.all_to_all(stacked, 'bulk', split_axis=0, concat_axis=0, tiled=True)]
    ppermute x4, waiting for transfers between devices: 1.95 us -> 5.82 us  [from_behind(): lax.ppermute(shard, axis, [(i, (i + by) % peers) for i in range(peers)])]
    all_to_all x1, waiting for transfers between devices: 0.53 us -> 4.16 us  [per_device(): lax.all_to_all(outgoing, 'bulk', split_axis=0, concat_axis=0, tiled=True)]
    unnamed x26 -> x28, local copies, waits for them, and re-layouts: 4.88 us -> 3.41 us
    ppermute x4, starting transfers between devices: 10.4 us -> 11.5 us  [from_behind(): lax.ppermute(shard, axis, [(i, (i + by) % peers) for i in range(peers)])]
  transfers between devices with their start and end apart: 5 -> 5, of which waited for: 2 -> 3; matrix products, arithmetic and copies ran while one was open for 0% -> 0% of each run, Pallas kernels for 20% -> 14%
where the time goes in v2:
time: 96.1 us; the launch traced here: 95.7 us
  Pallas kernels  30.5 us (32%)
  blocking collectives  29.4 us (31%)
  starting transfers between devices  21.6 us (22%)
  waiting for transfers between devices  9.97 us (10%)
  local copies, waits for them, and re-layouts  3.41 us (4%)
    pallas_call x2, Pallas kernels, remote_tiles(): pl.pallas_call(functools.partial(remote_kernel, groups), out_shape=[shape...  17.9 us
    all_to_all x1, blocking collectives, per_device(): lax.all_to_all(stacked, 'bulk', split_axis=0, concat_axis=0, tiled=True)  15.6 us
    all_to_all x1, blocking collectives, per_device(): lax.all_to_all(moving, 'bulk', split_axis=0, concat_axis=0, tiled=True)  13.8 us
    ppermute x4, starting transfers between devices, from_behind(): lax.ppermute(shard, axis, [(i, (i + by) % peers) for i in range(peers)])  11.5 us
    all_to_all x1, starting transfers between devices, per_device(): lax.all_to_all(outgoing, 'bulk', split_axis=0, concat_axis=0, tiled=True)  10.2 us
    pallas_call x1, Pallas kernels, local_tiles(): pl.pallas_call(local_kernel, out_shape=[shape(4, count, 128), shape(count...  7.06 us
    ppermute x4, waiting for transfers between devices, from_behind(): lax.ppermute(shard, axis, [(i, (i + by) % peers) for i in range(peers)])  5.82 us
    all_to_all x1, waiting for transfers between devices, per_device(): lax.all_to_all(outgoing, 'bulk', split_axis=0, concat_axis=0, tiled=True)  4.16 us
  transfers between devices with their start and end apart: 5, of which 3 were waited for; matrix products, arithmetic and copies ran while one was open for 0% of the time, Pallas kernels for 14%

profile of v2, /device:TPU:8, one launch (start us, length us, event | category | flops | bytes accessed | tf_op | source)
XLA Modules:
  0.0 95.7 jit_solution(15442526155852991325)
XLA Ops:
  0.6 0.0 copy-start.10
  0.6 2.2 %pack.1 = (f32[32,8,128]{2,1,0:T(8,128)}, f32[32,8,128]{2,1,0:T(8,128)}, f32[32,8,128]{2,1,0:T(8,128)}, f32[32,8,128]{2,1,0:T(8,128)}, f32[64,8,128]{2,1,0:T(8,128)}) custom-call(s32[3,1,32]{2,1,0:T(1,128)} %bitcast.23, s32[1,1,32]{2,1,0:T(1,128)} %bitcast.25, f32[3,64,128]{2,1,0:T(8,128)} %bitcast.34, f32[256,128]{1,0:T(8,128)} %bitcast.19), custom_call_target="tpu_custom_call" | custom-call | tf_op jit(solution)/shard_map/pack/pallas_call | solution.py:453
  2.8 8.5 %collective-permute-start = (f32[32,8,128]{2,1,0:T(8,128)}, f32[32,8,128]{2,1,0:T(8,128)S(1)}, u32[]{:S(2)}, u32[]{:S(2)}) collective-permute-start(f32[32,8,128]{2,1,0:T(8,128)} %get-tuple-element.22), channel_id=1, source_target_pairs={{0,480},{32,0},{64,32},{96,64},{128,96},{160,128},{192,160},{224,1... | collective-permute-start | bytes 393224 | tf_op jit(solution)/shard_map/ppermute | solution.py:22
  11.3 0.0 collective-permute-start.1
  11.3 2.8 %collective-permute-done.down_ref = f32[32,8,128]{2,1,0:T(8,128)S(1)} collective-permute-done((f32[32,8,128]{2,1,0:T(8,128)}, f32[32,8,128]{2,1,0:T(8,128)S(1)}, u32[]{:S(2)}, u32[]{:S(2)}) %collective-permute-start) | collective-permute-done | bytes 131104 | tf_op jit(solution)/shard_map/ppermute | solution.py:22
  14.1 3.0 %collective-permute-done.1.up_ref = f32[32,8,128]{2,1,0:T(8,128)S(1)} collective-permute-done((f32[32,8,128]{2,1,0:T(8,128)}, f32[32,8,128]{2,1,0:T(8,128)S(1)}, u32[]{:S(2)}, u32[]{:S(2)}) %collective-permute-start.1) | collective-permute-done | bytes 131104 | tf_op jit(solution)/shard_map/ppermute | solution.py:22
  17.1 0.0 copy-start.1
  17.1 0.9 copy-done.1
  18.0 0.0 copy-start.2
  18.0 0.9 copy-done.2
  18.9 0.0 copy-start.8
  18.9 0.0 copy-start.9
  18.9 0.8 merge.1
  19.7 10.2 %all-to-all-start = ((f32[32,24,128]{2,1,0:T(8,128)}), f32[32,24,128]{2,1,0:T(8,128)S(1)}, u32[]{:S(2)}, u32[]{:S(2)}) async-start(f32[32,24,128]{2,1,0:T(8,128)} %merge.1), calls=%async_computation | async-start | bytes 786432 | tf_op jit(solution)/shard_map/all_to_all | solution.py:479
  29.9 0.0 copy-done.10
  29.9 0.0 copy-done.8
  29.9 0.0 copy-done.9
  29.9 0.0 copy-start.7
  30.0 0.0 copy-start.11
  30.0 7.1 %local_tiles.1 = (f32[4,64,128]{2,1,0:T(8,128)S(1)}, bf16[64,48,128]{2,1,0:T(8,128)(2,1)S(1)}) custom-call(s32[2,64]{1,0:T(2,128)S(1)} %bitcast.30, f32[64,8,128]{2,1,0:T(8,128)S(1)} %copy-done.9, s32[64,16,128]{2,1,0:T(8,128)S(1)} %bitcast.29), custom_call_target="tpu_custom_call" | custom-call | flops 4000000000 | bytes 2097152 | tf_op jit(solution)/shard_map/local_tiles/pallas_call | solution.py:418
  37.0 0.0 copy-start.12
  37.0 0.6 copy-done.12
  37.7 4.2 %all-to-all-done.spread_ref.early_ref = f32[32,24,128]{2,1,0:T(8,128)S(1)} async-done(((f32[32,24,128]{2,1,0:T(8,128)}), f32[32,24,128]{2,1,0:T(8,128)S(1)}, u32[]{:S(2)}, u32[]{:S(2)}) %all-to-all-start) | async-done | bytes 393248 | tf_op jit(solution)/shard_map/all_to_all | solution.py:479
  41.8 0.0 copy-done.7
  41.9 0.0 copy-done.11
  41.9 0.0 copy-start.13
  41.9 0.9 copy-done.13
  42.8 11.6 %remote_tiles.2 = (f32[4,64,128]{2,1,0:T(8,128)S(1)}, f32[32,4,128]{2,1,0:T(4,128)S(1)}, f32[32,4,128]{2,1,0:T(4,128)S(1)}) custom-call(s32[2,96]{1,0:T(2,128)S(1)} %bitcast.31, f32[4,64,128]{2,1,0:T(8,128)S(1)} %copy-done.13, f32[64,8,128]{2,1,0:T(8,128)S(1)} %copy-done.9, bf16[64,48,128]{2,1,0:T(8,128)(2,1)S(1)} %get-tuple-element.27.feature_ref, ...), custom_call_target="tpu_custom_call" | custom-call | flops 8000000000 | bytes 2097152 | tf_op jit(solution)/shard_map/remote_tiles/pallas_call | solution.py:396
  54.4 0.0 collective-permute-start.2
  54.4 2.9 %collective-permute-start.3 = (f32[32,4,128]{2,1,0:T(4,128)S(1)}, f32[32,4,128]{2,1,0:T(4,128)S(1)}, u32[]{:S(2)}, u32[]{:S(2)}) collective-permute-start(f32[32,4,128]{2,1,0:T(4,128)S(1)} %get-tuple-element.33), channel_id=1, source_target_pairs={{0,480},{32,0},{64,32},{96,64},{128,96},{160,128},{192,160},{224,1... | collective-permute-start | bytes 196616 | tf_op jit(solution)/shard_map/ppermute | solution.py:22
  57.4 0.0 copy-start
  57.4 0.0 copy-start.3
  57.4 0.0 copy-start.4
  57.4 0.0 copy-start.5
  57.4 0.0 copy-start.6
  57.4 6.3 %remote_tiles.3 = (f32[4,64,128]{2,1,0:T(8,128)S(1)}, f32[32,4,128]{2,1,0:T(4,128)S(1)}) custom-call(s32[2,96]{1,0:T(2,128)S(1)} %bitcast.32, f32[4,64,128]{2,1,0:T(8,128)S(1)} %get-tuple-element.29.totals_in_ref, f32[64,8,128]{2,1,0:T(8,128)S(1)} %copy-done.9, bf16[64,48,128]{2,1,0:T(8,128)(2,1)S(1)} %get-tuple-element.27.feature_ref, ...), custom_call_target="tpu_custom_call" | custom-call | flops 4000000000 | bytes 2097152 | tf_op jit(solution)/shard_map/remote_tiles/pallas_call | solution.py:396
  63.7 0.0 collective-permute-done.2
  63.7 0.0 collective-permute-done.3
  63.8 15.6 %all_to_all.15.returned_ref = f32[32,3,4,128]{3,2,1,0:T(4,128)S(1)} all-to-all(f32[32,3,4,128]{3,2,1,0:T(4,128)S(1)} %pad_maximum_fusion), channel_id=1, replica_groups=mesh['region'=16,'bulk'=32] {'bulk'}, dimensions={0} | all-to-all | bytes 393216 | tf_op jit(solution)/shard_map/all_to_all | solution.py:488
  79.4 0.0 copy-done
  79.4 0.0 copy-done.3
  79.4 0.0 copy-done.4
  79.4 0.0 copy-done.5
  79.4 0.0 copy-done.6
  79.4 1.8 %update.1 = (f32[256,128]{1,0:T(8,128)}, f32[3,64,128]{2,1,0:T(8,128)}, f32[32,8,128]{2,1,0:T(8,128)S(1)}) custom-call(s32[3,1,32]{2,1,0:T(1,128)S(1)} %bitcast.24, s32[1,1,32]{2,1,0:T(1,128)S(1)} %bitcast.26, f32[4,64,128]{2,1,0:T(8,128)S(1)} %get-tuple-element.30.totals_ref, f32[32,3,4,128]{3,2,1,0:T(4,128)S(1)} %all_to_all.15.returned_ref, ...), custom_call_target="tpu_custom_call" | custom-call | tf_op jit(solution)/shard_map/update/pallas_call | solution.py:489
  81.3 13.8 %all_to_all.16.late_ref = f32[32,8,128]{2,1,0:T(8,128)S(1)} all-to-all(f32[32,8,128]{2,1,0:T(8,128)S(1)} %get-tuple-element.36), channel_id=1, replica_groups=mesh['region'=16,'bulk'=32] {'bulk'}, dimensions={0} | all-to-all | bytes 262144 | tf_op jit(solution)/shard_map/all_to_all | solution.py:498
  95.0 0.7 arrive.1
  (1 shorter events, 0.0 us)
Async XLA Ops:
  0.6 29.3 %copy-start.10 = (s32[1,64,2]{1,2,0:T(2,128)S(1)}, s32[1,64,2]{1,2,0:T(2,128)}, u32[]{:S(2)}) copy-start(s32[1,64,2]{1,2,0:T(2,128)} %param.17) | copy-start | bytes 1540
  2.8 11.3 %collective-permute-start = (f32[32,8,128]{2,1,0:T(8,128)}, f32[32,8,128]{2,1,0:T(8,128)S(1)}, u32[]{:S(2)}, u32[]{:S(2)}) collective-permute-start(f32[32,8,128]{2,1,0:T(8,128)} %get-tuple-element.22), channel_id=1, source_target_pairs={{0,480},{32,0},{64,32},{96,64},{128,96},{160,128},{192,160},{224,1... | collective-permute-start | bytes 393224 | tf_op jit(solution)/shard_map/ppermute | solution.py:22
  11.3 5.8 %collective-permute-start.1 = (f32[32,8,128]{2,1,0:T(8,128)}, f32[32,8,128]{2,1,0:T(8,128)S(1)}, u32[]{:S(2)}, u32[]{:S(2)}) collective-permute-start(f32[32,8,128]{2,1,0:T(8,128)} %get-tuple-element.24), channel_id=1, source_target_pairs={{0,32},{32,64},{64,96},{96,128},{128,160},{160,192},{192,224},{224... | collective-permute-start | bytes 393224 | tf_op jit(solution)/shard_map/ppermute | solution.py:22
  17.1 0.9 copy-start.1
  18.0 0.9 copy-start.2
  18.9 11.0 %copy-start.8 = (s32[1,64,16,128]{3,2,1,0:T(8,128)S(1)}, s32[1,64,16,128]{3,2,1,0:T(8,128)}, u32[]{:S(2)}) copy-start(s32[1,64,16,128]{3,2,1,0:T(8,128)} %param.18) | copy-start | bytes 1572868
  18.9 11.0 %copy-start.9 = (f32[64,8,128]{2,1,0:T(8,128)S(1)}, f32[64,8,128]{2,1,0:T(8,128)}, u32[]{:S(2)}) copy-start(f32[64,8,128]{2,1,0:T(8,128)} %get-tuple-element.25.points_ref) | copy-start | bytes 786436
  19.7 22.1 %all-to-all-start = ((f32[32,24,128]{2,1,0:T(8,128)}), f32[32,24,128]{2,1,0:T(8,128)S(1)}, u32[]{:S(2)}, u32[]{:S(2)}) async-start(f32[32,24,128]{2,1,0:T(8,128)} %merge.1), calls=%async_computation | async-start | bytes 786432 | tf_op jit(solution)/shard_map/all_to_all | solution.py:479
  29.9 11.9 %copy-start.7 = (s32[1,96,2,16,128]{4,3,2,1,0:T(8,128)S(1)}, s32[1,96,2,16,128]{4,3,2,1,0:T(8,128)}, u32[]{:S(2)}) copy-start(s32[1,96,2,16,128]{4,3,2,1,0:T(8,128)} %param.16) | copy-start | bytes 4718596
  30.0 11.9 %copy-start.11 = (s32[1,96,2]{1,2,0:T(2,128)S(1)}, s32[1,96,2]{1,2,0:T(2,128)}, u32[]{:S(2)}) copy-start(s32[1,96,2]{1,2,0:T(2,128)} %param.15) | copy-start | bytes 2308
  37.0 0.7 copy-start.12
  41.9 0.9 copy-start.13
  54.4 9.3 %collective-permute-start.2 = (f32[32,4,128]{2,1,0:T(4,128)S(1)}, f32[32,4,128]{2,1,0:T(4,128)S(1)}, u32[]{:S(2)}, u32[]{:S(2)}) collective-permute-start(f32[32,4,128]{2,1,0:T(4,128)S(1)} %get-tuple-element.31), channel_id=1, source_target_pairs={{0,32},{32,64},{64,96},{96,128},{128,160},{160,192},{192,224},{224... | collective-permute-start | bytes 196616 | tf_op jit(solution)/shard_map/ppermute | solution.py:22
  54.4 9.3 %collective-permute-start.3 = (f32[32,4,128]{2,1,0:T(4,128)S(1)}, f32[32,4,128]{2,1,0:T(4,128)S(1)}, u32[]{:S(2)}, u32[]{:S(2)}) collective-permute-start(f32[32,4,128]{2,1,0:T(4,128)S(1)} %get-tuple-element.33), channel_id=1, source_target_pairs={{0,480},{32,0},{64,32},{96,64},{128,96},{160,128},{192,160},{224,1... | collective-permute-start | bytes 196616 | tf_op jit(solution)/shard_map/ppermute | solution.py:22
  57.4 22.0 %copy-start = (f32[64,4,128]{2,1,0:T(4,128)S(1)}, f32[64,4,128]{2,1,0:T(4,128)}, u32[]{:S(2)}) copy-start(f32[64,4,128]{2,1,0:T(4,128)} %param.11) | copy-start | bytes 393220
  57.4 22.0 %copy-start.3 = (f32[64,3,128]{2,0,1:T(8,128)S(1)}, f32[64,3,128]{2,0,1:T(8,128)}, u32[]{:S(2)}) copy-start(f32[64,3,128]{2,0,1:T(8,128)} %param.13) | copy-start | bytes 294916
  57.4 22.0 %copy-start.4 = (f32[64,128]{1,0:T(8,128)S(1)}, f32[64,128]{1,0:T(8,128)}, u32[]{:S(2)}) copy-start(f32[64,128]{1,0:T(8,128)} %storage_ref.1) | copy-start | bytes 98308
  57.4 22.1 %copy-start.5 = (s32[1,3,32,1]{2,3,1,0:T(1,128)S(1)}, s32[1,3,32,1]{2,3,1,0:T(1,128)}, u32[]{:S(2)}) copy-start(s32[1,3,32,1]{2,3,1,0:T(1,128)} %param.14) | copy-start | bytes 1156
  57.4 22.1 %copy-start.6 = (s32[1,32,1]{1,2,0:T(1,128)S(1)}, s32[1,32,1]{1,2,0:T(1,128)}, u32[]{:S(2)}) copy-start(s32[1,32,1]{1,2,0:T(1,128)} %param.19) | copy-start | bytes 388

commit v3 on v2

--- a/solution.py
+++ b/solution.py
@@ -186,7 +186,7 @@
 
 
 def pack_kernel(
-    sends_any, moves_any, positions_any, fields_any, down_ref, here_ref, up_ref, going_ref, points_ref,
+    sends_any, moves_any, positions_any, fields_any, out_ref, points_ref,
     sends_ref, moves_ref, positions_ref, fields_ref, sems,
 ):
     pairs = (
@@ -197,32 +197,21 @@
     )
     fetch([pltpu.make_async_copy(a, b, sems.at[n]) for n, (a, b) in enumerate(pairs)])
     count = positions_ref.shape[1]
-    peers = here_ref.shape[0]
     flat = points_ref.reshape(count * 8, 128)
     for k in range(3):
         flat[pl.ds(k, count, stride=8), :] = positions_ref[k]
         flat[pl.ds(4 + k, count, stride=8), :] = block_rows(fields_ref, k, count, 4)
     flat[pl.ds(3, count, stride=8), :] = block_rows(fields_ref, 3, count, 4)
     flat[pl.ds(7, count, stride=8), :] = jnp.zeros((count, 128), f32)
+    last = lax.broadcasted_iota(jnp.int32, (8, 128), 0) == 7
 
     def one_peer(peer, carry):
-        for o, out in enumerate((down_ref, here_ref, up_ref)):
-            out[peer] = points_ref[sends_ref[o, 0, peer]]
         move = moves_ref[0, 0, peer]
-        block = points_ref[jnp.maximum(move, 0)]
-        going_ref[peer] = jnp.where(move >= 0, block, jnp.zeros_like(block))
-        return carry
-
-    lax.fori_loop(0, peers, one_peer, 0, unroll=8)
-
-
-def merge_kernel(going_ref, down_ref, here_ref, up_ref, out_ref):
-    last = lax.broadcasted_iota(jnp.int32, (8, 128), 0) == 7
-
-    def one_peer(peer, carry):
-        block = going_ref[peer]
-        for o, part in enumerate((down_ref, here_ref, up_ref)):
-            out_ref[peer, 8 * o : 8 * o + 8] = jnp.where(last, block[o : o + 1], part[peer])
+        moved = points_ref[jnp.maximum(move, 0)]
+        moved = jnp.where(move >= 0, moved, jnp.zeros_like(moved))
+        for o in range(3):
+            block = points_ref[sends_ref[o, 0, peer]]
+            out_ref[peer, 8 * o : 8 * o + 8] = jnp.where(last, moved[o : o + 1], block)
         return carry
 
     lax.fori_loop(0, out_ref.shape[0], one_peer, 0, unroll=8)
@@ -255,62 +244,64 @@
         totals_ref[k] = row
 
 
-def remote_kernel(groups, local_ref, totals_in_ref, points_ref, feature_ref, spread_ref, mask_any, *rest):
-    totals_ref = rest[0]
-    back = rest[1 : 1 + len(groups)]
-    (sums_ref, turned_ref, weights_ref, other_feature_ref, other_sums, mask_ref, sems) = rest[
-        1 + len(groups) :
-    ]
+def remote_kernel(parts, adds, earlier, local_ref, points_ref, feature_ref, mask_any, *rest):
+    sources, rest = rest[: len(parts)], rest[len(parts) :]
+    add_refs, rest = rest[:adds], rest[adds:]
+    earlier_refs, rest = rest[:earlier], rest[earlier:]
+    totals_ref, rest = rest[0], rest[1:]
+    back, rest = rest[: len(parts)], rest[len(parts) :]
+    (
+        sums_ref, turned_ref, weights_ref, other_feature_ref, other_sums, blocks_ref, mask_ref, sems,
+    ) = rest
     count = points_ref.shape[0]
-    peers = spread_ref.shape[0]
-    slots = peers * len(groups)
-    tiles = 2 * peers
+    per_part = parts[0][3]
+    slots = per_part * len(parts)
+    starts = [group * first_of_group + first for group, _, first, _, first_of_group in parts]
     copies = [
         pltpu.make_async_copy(
-            mask_any.at[pl.ds(group * tiles, tiles)], mask_ref.at[pl.ds(part * tiles, tiles)], sems.at[part]
+            mask_any.at[pl.ds(2 * start, 2 * per_part)],
+            mask_ref.at[pl.ds(2 * n * per_part, 2 * per_part)],
+            sems.at[n],
         )
-        for part, group in enumerate(groups)
+        for n, start in enumerate(starts)
     ]
     for copy in copies:
         copy.start()
-    first = groups[0]
-    apart = groups[-1] - first
-
-    def group_of(slot):
-        return first + apart * (slot // peers), lax.rem(slot, peers)
-
-    def other_block(slot):
-        group, peer = group_of(slot)
-        return spread_ref[peer, pl.ds(pl.multiple_of(8 * group, 8), 8)]
-
-    def owned_of(slot, e):
-        group, peer = group_of(slot)
-        return local_ref[e, group * peers + peer]
-
+    for n, (_, row, first, _, _) in enumerate(parts):
+        for m in range(per_part):
+            blocks_ref[n * per_part + m] = sources[n][first + m, row : row + 8]
+    turn(lambda n: blocks_ref[n], turned_ref)
     sums_ref[...] = jnp.zeros_like(sums_ref)
-    turn(
-        lambda n: spread_ref[n % peers, 8 * groups[n // peers] : 8 * groups[n // peers] + 8], turned_ref
-    )
     for copy in copies:
         copy.wait()
+    gap = starts[-1] - starts[0] - per_part
+
+    def owned_of(slot, e):
+        return local_ref[e, slot + starts[0] + gap * (slot // per_part)]
 
     def store_other(slot, on_other):
         other_sums[slot] = on_other
 
     tile_loop(
-        slots, 2, 2, owned_of, lambda slot: slot, other_block, mask_ref, turned_ref, points_ref,
-        feature_ref, sums_ref, weights_ref, other_feature_ref, store_other,
-    )
-    flat = spread_ref.reshape(peers * 24, 128)
-    for part, group in enumerate(groups):
-        terms = owned_terms(other_sums, lambda r: block_rows(flat, 8 * group + r, peers, 24), peers)
-        back_rows = back[part].reshape(peers * 4, 128)
-        for k, row in enumerate(terms(part * peers)):
-            back_rows[pl.ds(k, peers, stride=4), :] = row
+        slots, 2, 2, owned_of, lambda slot: slot, lambda slot: blocks_ref[slot], mask_ref, turned_ref,
+        points_ref, feature_ref, sums_ref, weights_ref, other_feature_ref, store_other,
+    )
+    flat = blocks_ref.reshape(slots * 8, 128)
+    for n in range(len(parts)):
+        base = n * per_part
+        terms = owned_terms(other_sums, lambda r: block_rows(flat, 8 * base + r, per_part, 8), per_part)
+        before = back[n].shape[0] - per_part
+        if before:
+            back[n][0:before] = earlier_refs[n][...]
+        rows = back[n].reshape(back[n].shape[0] * 4, 128)
+        for k, row in enumerate(terms(base)):
+            rows[pl.ds(4 * before + k, per_part, stride=4), :] = row
     own = points_ref.reshape(count * 8, 128)
     terms = owned_terms(sums_ref, lambda r: block_rows(own, r, count, 8), count)
     for k, row in enumerate(terms(0)):
-        totals_ref[k] = totals_in_ref[k] + row
+        for add in add_refs:
+            row = row + add[k]
+        totals_ref[k] = row
 
 
 def update_kernel(
@@ -389,28 +380,31 @@
     return pl.BlockSpec(memory_space=pl.ANY)
 
 
-def remote_tiles(groups, local, totals, points, feature, spread, mask):
+def remote_tiles(parts, local, points, feature, mask, sources, adds=(), earlier=()):
     count = points.shape[0]
-    peers = spread.shape[0]
-    slots = peers * len(groups)
+    per_part = parts[0][3]
+    slots = per_part * len(parts)
+    before = earlier[0].shape[0] if earlier else 0
     return pl.pallas_call(
-        functools.partial(remote_kernel, groups),
-        out_shape=[shape(4, count, 128)] + [shape(peers, 4, 128)] * len(groups),
-        in_specs=[in_smem()] + [in_vmem()] * 4 + [anywhere()],
-        out_specs=[in_vmem()] * (1 + len(groups)),
+        functools.partial(remote_kernel, parts, len(adds), len(earlier)),
+        out_shape=[shape(4, count, 128)] + [shape(before + per_part, 4, 128)] * len(parts),
+        in_specs=[in_smem(), in_vmem(), in_vmem(), anywhere()]
+        + [in_vmem()] * (len(sources) + len(adds) + len(earlier)),
+        out_specs=[in_vmem()] * (1 + len(parts)),
         scratch_shapes=[
             pltpu.VMEM((count, 16, 128), f32),
             pltpu.VMEM((slots // 16, 128, 128), f32),
             pltpu.VMEM((2, 4, 256, 256), bf16),
             pltpu.VMEM((2, 2, 48, 128), bf16),
             pltpu.VMEM((slots, 16, 128), f32),
+            pltpu.VMEM((slots, 8, 128), f32),
             pltpu.VMEM((2 * slots, 16, 128), jnp.int32),
-            pltpu.SemaphoreType.DMA((len(groups),)),
+            pltpu.SemaphoreType.DMA((len(parts),)),
         ],
         compiler_params=params(),
-        cost_estimate=cost(len(groups) * 4 * 10**9),
+        cost_estimate=cost(slots * 10**8),
         name="remote_tiles",
-    )(local, totals, points, feature, spread, mask)
+    )(local, points, feature, mask, *sources, *adds, *earlier)
 
 
 def local_tiles(pairs, points, mask):
@@ -449,12 +443,11 @@
     moves = migrate_list.transpose(0, 2, 1)
     rows_first = positions.transpose(1, 0, 2)
     flat_fields = fields.reshape(count * 4, 128)
-    part = shape(peers, 8, 128)
-    down, here, up, going, points = pl.pallas_call(
+    outgoing, points = pl.pallas_call(
         pack_kernel,
-        out_shape=[part, part, part, part, shape(count, 8, 128)],
+        out_shape=[shape(peers, 24, 128), shape(count, 8, 128)],
         in_specs=[anywhere()] * 4,
-        out_specs=[in_vmem()] * 5,
+        out_specs=[in_vmem()] * 2,
         scratch_shapes=[
             pltpu.SMEM(sends.shape, jnp.int32),
             pltpu.SMEM(moves.shape, jnp.int32),
@@ -465,25 +458,25 @@
         compiler_params=pltpu.CompilerParams(vmem_limit_bytes=60 * 1024 * 1024),
         name="pack",
     )(sends, moves, rows_first, flat_fields)
-    down = from_behind(down, "region", -1)
-    up = from_behind(up, "region", 1)
-    outgoing = pl.pallas_call(
-        merge_kernel,
-        out_shape=shape(peers, 24, 128),
-        in_specs=[in_vmem()] * 4,
-        out_specs=in_vmem(),
-        compiler_params=params(),
-        name="merge",
-    )(going, down, here, up)
-    points, outgoing = lax.optimization_barrier((points, outgoing))
     spread = lax.all_to_all(outgoing, "bulk", split_axis=0, concat_axis=0, tiled=True)
-    totals, feature = local_tiles(local_pairs[0].transpose(1, 0), points, local_mask[0])
+    local_totals, feature = local_tiles(local_pairs[0].transpose(1, 0), points, local_mask[0])
+    spread, feature = lax.optimization_barrier((spread, feature))
     local = remote_local[0].transpose(1, 0)
     mask = remote_mask[0].reshape(-1, remote_mask.shape[3], remote_mask.shape[4])
-    totals, down_back, up_back = remote_tiles((0, 2), local, totals, points, feature, spread, mask)
+    tile_args = (local, points, feature, mask)
+    down = from_behind(spread[:, 0:8], "region", -1)
+    up = from_behind(spread[:, 16:24], "region", 1)
+    half = peers // 2
+    first_totals, first_back = remote_tiles(((1, 8, 0, half, peers),), *tile_args, [spread])
+    far_totals, down_back, up_back = remote_tiles(
+        ((0, 0, 0, peers, peers), (2, 0, 0, peers, peers)), *tile_args, [down, up]
+    )
     down_back = from_behind(down_back, "region", 1)
     up_back = from_behind(up_back, "region", -1)
-    totals, here_back = remote_tiles((1,), local, totals, points, feature, spread, mask)
+    totals, here_back = remote_tiles(
+        ((1, 8, half, half, peers),), *tile_args, [spread],
+        [local_totals, first_totals, far_totals], [first_back],
+    )
     stacked = jnp.stack([down_back, here_back, up_back], axis=1)
     returned = lax.all_to_all(stacked, "bulk", split_axis=0, concat_axis=0, tiled=True)
     new_fields, new_velocity, moving = pl.pallas_call(

time: 96.1 us -> 91.2 us (0.949)
  starting transfers between devices: 21.6 us -> 18.8 us
  waiting for transfers between devices: 9.97 us -> 7.43 us
  blocking collectives: 29.4 us -> 30.4 us
    ppermute x4, waiting for transfers between devices: 5.82 us -> 2.46 us  [from_behind(): lax.ppermute(shard, axis, [(i, (i + by) % peers) for i in range(peers)])]
    ppermute x4, starting transfers between devices: 11.5 us -> 8.64 us  [from_behind(): lax.ppermute(shard, axis, [(i, (i + by) % peers) for i in range(peers)])]
    unnamed x28 -> x22, local copies, waits for them, and re-layouts: 3.41 us -> 2.7 us
  transfers between devices with their start and end apart: 5 -> 5, of which waited for: 3 -> 2; matrix products, arithmetic and copies ran while one was open for 0% -> 0% of each run, Pallas kernels for 14% -> 16%
where the time goes in v3:
time: 91.2 us; the launch traced here: 90.9 us
  Pallas kernels  30.7 us (34%)
  blocking collectives  30.4 us (33%)
  starting transfers between devices  18.8 us (21%)
  waiting for transfers between devices  7.43 us (8%)
  local copies, waits for them, and re-layouts  2.71 us (3%)
    pallas_call x3, Pallas kernels, remote_tiles(): pl.pallas_call(functools.partial(remote_kernel, parts, len(adds), len(ear...  19 us
    all_to_all x1, blocking collectives, per_device(): lax.all_to_all(stacked, 'bulk', split_axis=0, concat_axis=0, tiled=True)  16.5 us
    all_to_all x1, blocking collectives, per_device(): lax.all_to_all(moving, 'bulk', split_axis=0, concat_axis=0, tiled=True)  13.8 us
    all_to_all x1, starting transfers between devices, per_device(): lax.all_to_all(outgoing, 'bulk', split_axis=0, concat_axis=0, tiled=True)  10.2 us
    ppermute x4, starting transfers between devices, from_behind(): lax.ppermute(shard, axis, [(i, (i + by) % peers) for i in range(peers)])  8.64 us
    pallas_call x1, Pallas kernels, local_tiles(): pl.pallas_call(local_kernel, out_shape=[shape(4, count, 128), shape(count...  7.05 us
    all_to_all x1, waiting for transfers between devices, per_device(): lax.all_to_all(outgoing, 'bulk', split_axis=0, concat_axis=0, tiled=True)  4.97 us
    unnamed x22, local copies, waits for them, and re-layouts  2.7 us
  transfers between devices with their start and end apart: 5, of which 2 were waited for; matrix products, arithmetic and copies ran while one was open for 0% of the time, Pallas kernels for 16%

profile of v3, /device:TPU:8, one launch (start us, length us, event | category | flops | bytes accessed | tf_op | source)
XLA Modules:
  0.0 90.9 jit_solution(4531924114028300262)
XLA Ops:
  0.6 2.2 %pack.1 = (f32[32,24,128]{2,1,0:T(8,128)}, f32[64,8,128]{2,1,0:T(8,128)}) custom-call(s32[3,1,32]{2,1,0:T(1,128)} %bitcast.23, s32[1,1,32]{2,1,0:T(1,128)} %bitcast.25, f32[3,64,128]{2,1,0:T(8,128)} %bitcast.36, f32[256,128]{1,0:T(8,128)} %bitcast.19), custom_call_target="tpu_custom_call" | custom-call | tf_op jit(solution)/shard_map/pack/pallas_call | solution.py:446
  2.8 10.2 %all-to-all-start = ((f32[32,24,128]{2,1,0:T(8,128)}), f32[32,24,128]{2,1,0:T(8,128)S(1)}, u32[]{:S(2)}, u32[]{:S(2)}) async-start(f32[32,24,128]{2,1,0:T(8,128)} %get-tuple-element.20), calls=%async_computation | async-start | bytes 786432 | tf_op jit(solution)/shard_map/all_to_all | solution.py:461
  13.0 0.0 copy-start.6
  13.0 1.0 %copy-done.6 = s32[1,64,16,128]{3,2,1,0:T(8,128)S(1)} copy-done((s32[1,64,16,128]{3,2,1,0:T(8,128)S(1)}, s32[1,64,16,128]{3,2,1,0:T(8,128)}, u32[]{:S(2)}) %copy-start.6) | copy-done | bytes 524312
  14.0 0.0 copy-start.7
  14.0 0.9 %copy-done.7 = f32[64,8,128]{2,1,0:T(8,128)S(1)} copy-done((f32[64,8,128]{2,1,0:T(8,128)S(1)}, f32[64,8,128]{2,1,0:T(8,128)}, u32[]{:S(2)}) %copy-start.7) | copy-done | bytes 262168
  15.0 0.0 copy-start.9
  15.0 0.7 copy-done.9
  15.6 0.0 copy-start.5
  15.7 0.0 copy-start.8
  15.7 0.0 copy-start.10
  15.7 7.1 %local_tiles.1 = (f32[4,64,128]{2,1,0:T(8,128)S(1)}, bf16[64,48,128]{2,1,0:T(8,128)(2,1)S(1)}) custom-call(s32[2,64]{1,0:T(2,128)S(1)} %bitcast.31, f32[64,8,128]{2,1,0:T(8,128)S(1)} %copy-done.7, s32[64,16,128]{2,1,0:T(8,128)S(1)} %bitcast.30), custom_call_target="tpu_custom_call" | custom-call | flops 4000000000 | bytes 2097152 | tf_op jit(solution)/shard_map/local_tiles/pallas_call | solution.py:412
  22.7 5.0 %all-to-all-done.rest_0_.early_ref = f32[32,24,128]{2,1,0:T(8,128)S(1)} async-done(((f32[32,24,128]{2,1,0:T(8,128)}), f32[32,24,128]{2,1,0:T(8,128)S(1)}, u32[]{:S(2)}, u32[]{:S(2)}) %all-to-all-start) | async-done | bytes 393248 | tf_op jit(solution)/shard_map/all_to_all | solution.py:461
  27.7 5.7 %collective-permute-start = (f32[32,8,128]{2,1,0:T(8,128)S(1)}, f32[32,8,128]{2,1,0:T(8,128)S(1)}, u32[]{:S(2)}, u32[]{:S(2)}) collective-permute-start(f32[32,8,128]{2,1,0:T(8,128)S(1)} %get-tuple-element.36), channel_id=1, source_target_pairs={{0,480},{32,0},{64,32},{96,64},{128,96},{160,128},{192,160},{224,1... | collective-permute-start | bytes 393224 | tf_op jit(solution)/shard_map/ppermute | solution.py:22
  33.4 0.0 collective-permute-start.1
  33.4 0.0 copy-done.5
  33.4 0.0 copy-done.8
  33.4 0.0 copy-done.10
  33.4 3.6 %remote_tiles.3 = (f32[4,64,128]{2,1,0:T(8,128)S(1)}, f32[16,4,128]{2,1,0:T(4,128)S(1)}) custom-call(s32[2,96]{1,0:T(2,128)S(1)} %bitcast.32, f32[64,8,128]{2,1,0:T(8,128)S(1)} %copy-done.8, bf16[64,48,128]{2,1,0:T(8,128)(2,1)S(1)} %get-tuple-element.22.feature_ref, s32[192,16,128]{2,1,0:T(8,128)S(1)} %bitcast.27, ...), custom_call_target="tpu_custom_call" | custom-call | flops 1600000000 | bytes 2097152 | tf_op jit(solution)/shard_map/remote_tiles/pallas_call | solution.py:388
  37.1 0.0 collective-permute-done.rest_0_
  37.1 2.5 %collective-permute-done.1.rest_1_ = f32[32,8,128]{2,1,0:T(8,128)S(1)} collective-permute-done((f32[32,8,128]{2,1,0:T(8,128)S(1)}, f32[32,8,128]{2,1,0:T(8,128)S(1)}, u32[]{:S(2)}, u32[]{:S(2)}) %collective-permute-start.1) | collective-permute-done | bytes 131104 | tf_op jit(solution)/shard_map/ppermute | solution.py:22
  39.5 11.6 %remote_tiles.4 = (f32[4,64,128]{2,1,0:T(8,128)S(1)}, f32[32,4,128]{2,1,0:T(4,128)S(1)}, f32[32,4,128]{2,1,0:T(4,128)S(1)}) custom-call(s32[2,96]{1,0:T(2,128)S(1)} %bitcast.33, f32[64,8,128]{2,1,0:T(8,128)S(1)} %copy-done.8, bf16[64,48,128]{2,1,0:T(8,128)(2,1)S(1)} %get-tuple-element.22.feature_ref, s32[192,16,128]{2,1,0:T(8,128)S(1)} %bitcast.28, ...), custom_call_target="tpu_custom_call" | custom-call | flops 6400000000 | bytes 2097152 | tf_op jit(solution)/shard_map/remote_tiles/pallas_call | solution.py:388
  51.2 0.0 collective-permute-start.2
  51.2 2.9 %collective-permute-start.3 = (f32[32,4,128]{2,1,0:T(4,128)S(1)}, f32[32,4,128]{2,1,0:T(4,128)S(1)}, u32[]{:S(2)}, u32[]{:S(2)}) collective-permute-start(f32[32,4,128]{2,1,0:T(4,128)S(1)} %get-tuple-element.31), channel_id=1, source_target_pairs={{0,480},{32,0},{64,32},{96,64},{128,96},{160,128},{192,160},{224,1... | collective-permute-start | bytes 196616 | tf_op jit(solution)/shard_map/ppermute | solution.py:22
  54.1 0.0 copy-start
  54.1 0.0 copy-start.1
  54.1 0.0 copy-start.2
  54.1 0.0 copy-start.3
  54.2 0.0 copy-start.4
  54.2 3.7 %remote_tiles.5 = (f32[4,64,128]{2,1,0:T(8,128)S(1)}, f32[32,4,128]{2,1,0:T(4,128)S(1)}) custom-call(s32[2,96]{1,0:T(2,128)S(1)} %bitcast.34, f32[64,8,128]{2,1,0:T(8,128)S(1)} %copy-done.8, bf16[64,48,128]{2,1,0:T(8,128)(2,1)S(1)} %get-tuple-element.22.feature_ref, s32[192,16,128]{2,1,0:T(8,128)S(1)} %bitcast.29, ...), custom_call_target="tpu_custom_call" | custom-call | flops 1600000000 | bytes 2097152 | tf_op jit(solution)/shard_map/remote_tiles/pallas_call | solution.py:388
  57.8 0.0 collective-permute-done.2
  57.8 0.0 collective-permute-done.3
  57.9 16.5 %all_to_all.15.returned_ref = f32[32,3,4,128]{3,2,1,0:T(4,128)S(1)} all-to-all(f32[32,3,4,128]{3,2,1,0:T(4,128)S(1)} %pad_maximum_fusion), channel_id=1, replica_groups=mesh['region'=16,'bulk'=32] {'bulk'}, dimensions={0} | all-to-all | bytes 393216 | tf_op jit(solution)/shard_map/all_to_all | solution.py:481
  74.5 0.0 copy-done
  74.5 0.0 copy-done.1
  74.5 0.0 copy-done.2
  74.5 0.0 copy-done.3
  74.5 0.0 copy-done.4
  74.5 1.8 %update.1 = (f32[256,128]{1,0:T(8,128)}, f32[3,64,128]{2,1,0:T(8,128)}, f32[32,8,128]{2,1,0:T(8,128)S(1)}) custom-call(s32[3,1,32]{2,1,0:T(1,128)S(1)} %bitcast.24, s32[1,1,32]{2,1,0:T(1,128)S(1)} %bitcast.26, f32[4,64,128]{2,1,0:T(8,128)S(1)} %get-tuple-element.28.totals_ref, f32[32,3,4,128]{3,2,1,0:T(4,128)S(1)} %all_to_all.15.returned_ref, ...), custom_call_target="tpu_custom_call" | custom-call | tf_op jit(solution)/shard_map/update/pallas_call | solution.py:482
  76.3 13.8 %all_to_all.16.late_ref = f32[32,8,128]{2,1,0:T(8,128)S(1)} all-to-all(f32[32,8,128]{2,1,0:T(8,128)S(1)} %get-tuple-element.34), channel_id=1, replica_groups=mesh['region'=16,'bulk'=32] {'bulk'}, dimensions={0} | all-to-all | bytes 262144 | tf_op jit(solution)/shard_map/all_to_all | solution.py:491
  90.1 0.7 arrive.1
  (2 shorter events, 0.1 us)
Async XLA Ops:
  2.8 24.9 %all-to-all-start = ((f32[32,24,128]{2,1,0:T(8,128)}), f32[32,24,128]{2,1,0:T(8,128)S(1)}, u32[]{:S(2)}, u32[]{:S(2)}) async-start(f32[32,24,128]{2,1,0:T(8,128)} %get-tuple-element.20), calls=%async_computation | async-start | bytes 786432 | tf_op jit(solution)/shard_map/all_to_all | solution.py:461
  13.0 1.0 %copy-start.6 = (s32[1,64,16,128]{3,2,1,0:T(8,128)S(1)}, s32[1,64,16,128]{3,2,1,0:T(8,128)}, u32[]{:S(2)}) copy-start(s32[1,64,16,128]{3,2,1,0:T(8,128)} %param.18) | copy-start | bytes 1572868
  14.0 0.9 %copy-start.7 = (f32[64,8,128]{2,1,0:T(8,128)S(1)}, f32[64,8,128]{2,1,0:T(8,128)}, u32[]{:S(2)}) copy-start(f32[64,8,128]{2,1,0:T(8,128)} %get-tuple-element.19.points_ref) | copy-start | bytes 786436
  15.0 0.7 copy-start.9
  15.6 17.7 %copy-start.5 = (s32[1,96,2,16,128]{4,3,2,1,0:T(8,128)S(1)}, s32[1,96,2,16,128]{4,3,2,1,0:T(8,128)}, u32[]{:S(2)}) copy-start(s32[1,96,2,16,128]{4,3,2,1,0:T(8,128)} %param.16) | copy-start | bytes 4718596
  15.7 17.7 %copy-start.8 = (f32[64,8,128]{2,1,0:T(8,128)S(1)}, f32[64,8,128]{2,1,0:T(8,128)}, u32[]{:S(2)}) copy-start(f32[64,8,128]{2,1,0:T(8,128)} %get-tuple-element.19.points_ref) | copy-start | bytes 786436
  15.7 17.7 %copy-start.10 = (s32[1,96,2]{1,2,0:T(2,128)S(1)}, s32[1,96,2]{1,2,0:T(2,128)}, u32[]{:S(2)}) copy-start(s32[1,96,2]{1,2,0:T(2,128)} %param.15) | copy-start | bytes 2308
  27.7 9.4 %collective-permute-start = (f32[32,8,128]{2,1,0:T(8,128)S(1)}, f32[32,8,128]{2,1,0:T(8,128)S(1)}, u32[]{:S(2)}, u32[]{:S(2)}) collective-permute-start(f32[32,8,128]{2,1,0:T(8,128)S(1)} %get-tuple-element.36), channel_id=1, source_target_pairs={{0,480},{32,0},{64,32},{96,64},{128,96},{160,128},{192,160},{224,1... | collective-permute-start | bytes 393224 | tf_op jit(solution)/shard_map/ppermute | solution.py:22
  33.4 6.1 %collective-permute-start.1 = (f32[32,8,128]{2,1,0:T(8,128)S(1)}, f32[32,8,128]{2,1,0:T(8,128)S(1)}, u32[]{:S(2)}, u32[]{:S(2)}) collective-permute-start(f32[32,8,128]{2,1,0:T(8,128)S(1)} %get-tuple-element.35), channel_id=1, source_target_pairs={{0,32},{32,64},{64,96},{96,128},{128,160},{160,192},{192,224},{224... | collective-permute-start | bytes 393224 | tf_op jit(solution)/shard_map/ppermute | solution.py:22
  51.2 6.7 %collective-permute-start.2 = (f32[32,4,128]{2,1,0:T(4,128)S(1)}, f32[32,4,128]{2,1,0:T(4,128)S(1)}, u32[]{:S(2)}, u32[]{:S(2)}) collective-permute-start(f32[32,4,128]{2,1,0:T(4,128)S(1)} %get-tuple-element.29), channel_id=1, source_target_pairs={{0,32},{32,64},{64,96},{96,128},{128,160},{160,192},{192,224},{224... | collective-permute-start | bytes 196616 | tf_op jit(solution)/shard_map/ppermute | solution.py:22
  51.2 6.7 %collective-permute-start.3 = (f32[32,4,128]{2,1,0:T(4,128)S(1)}, f32[32,4,128]{2,1,0:T(4,128)S(1)}, u32[]{:S(2)}, u32[]{:S(2)}) collective-permute-start(f32[32,4,128]{2,1,0:T(4,128)S(1)} %get-tuple-element.31), channel_id=1, source_target_pairs={{0,480},{32,0},{64,32},{96,64},{128,96},{160,128},{192,160},{224,1... | collective-permute-start | bytes 196616 | tf_op jit(solution)/shard_map/ppermute | solution.py:22
  54.1 20.3 %copy-start = (f32[64,4,128]{2,1,0:T(4,128)S(1)}, f32[64,4,128]{2,1,0:T(4,128)}, u32[]{:S(2)}) copy-start(f32[64,4,128]{2,1,0:T(4,128)} %param.11) | copy-start | bytes 393220
  54.1 20.3 %copy-start.1 = (f32[64,3,128]{2,0,1:T(8,128)S(1)}, f32[64,3,128]{2,0,1:T(8,128)}, u32[]{:S(2)}) copy-start(f32[64,3,128]{2,0,1:T(8,128)} %param.13) | copy-start | bytes 294916
  54.1 20.3 %copy-start.2 = (f32[64,128]{1,0:T(8,128)S(1)}, f32[64,128]{1,0:T(8,128)}, u32[]{:S(2)}) copy-start(f32[64,128]{1,0:T(8,128)} %storage_ref.1) | copy-start | bytes 98308
  54.1 20.3 %copy-start.3 = (s32[1,3,32,1]{2,3,1,0:T(1,128)S(1)}, s32[1,3,32,1]{2,3,1,0:T(1,128)}, u32[]{:S(2)}) copy-start(s32[1,3,32,1]{2,3,1,0:T(1,128)} %param.14) | copy-start | bytes 1156
  54.2 20.3 %copy-start.4 = (s32[1,32,1]{1,2,0:T(1,128)S(1)}, s32[1,32,1]{1,2,0:T(1,128)}, u32[]{:S(2)}) copy-start(s32[1,32,1]{1,2,0:T(1,128)} %param.19) | copy-start | bytes 388

commit v4 on v3

--- a/solution.py
+++ b/solution.py
@@ -105,7 +105,7 @@
 
 
 def tile_loop(
-    slots, touch, per_step, owned_of, other_of, other_block, mask_ref, turned_ref, points_ref,
+    slots, touch, per_step, owned_of, other_of, other_block, words_of, turned_ref, points_ref,
     feature_ref, sums_ref, weights_ref, other_feature_ref, store_other,
 ):
     bits = jnp.left_shift(1, lax.broadcasted_iota(jnp.int32, (16, 8, 128), 1)).reshape(128, 128)
@@ -124,12 +124,8 @@
                 for k in range(3)
             ]
             for e in range(touch):
-                tile = slot * touch + e
                 owned = owned_of(slot, e)
-                words = jnp.concatenate(
-                    [mask_ref[tile, pl.ds(j, 8, stride=0), :] for j in range(16)], axis=0
-                )
-                a, b, c, d = bond_weights(others, points_ref[owned], words, bits)
+                a, b, c, d = bond_weights(others, points_ref[owned], words_of(slot, e), bits)
                 at = n * touch + e
                 weights_ref[half, at, 0:128, 0:128] = a
                 weights_ref[half, at, 0:128, 128:256] = b
@@ -168,14 +164,19 @@
     add_up(steps - 1, 1)
 
 
-def owned_terms(sums_ref, points, count):
-    rows = sums_ref.reshape(sums_ref.shape[0] * 16, 128)
-    return lambda first: terms_of(
-        [block_rows(rows, first * 16 + r, count, 16) for r in range(12)],
-        [points(r) for r in range(3)],
-        points(3),
-        [points(4 + r) for r in range(3)],
-    )
+def block_terms(sums_ref, first, blocks_ref, count, put):
+    sums = sums_ref.reshape(sums_ref.shape[0] * 16, 128)
+    rows = blocks_ref.reshape(blocks_ref.shape[0] * 8, 128)
+    for n in range(0, count, 16):
+        own = [block_rows(rows, 8 * (first + n) + r, 16, 8) for r in range(7)]
+        terms = terms_of(
+            [block_rows(sums, 16 * (first + n) + r, 16, 16) for r in range(12)],
+            own[0:3],
+            own[3],
+            own[4:7],
+        )
+        for k, row in enumerate(terms):
+            put(k, n, row)
 
 
 def fetch(copies):
@@ -231,97 +232,102 @@
 
     lax.fori_loop(0, count, one_block, 0, unroll=8)
 
+    def words_of(slot, e):
+        return jnp.concatenate([mask_ref[slot, pl.ds(j, 8, stride=0), :] for j in range(16)], axis=0)
+
     def store_other(slot, on_other):
         sums_ref[pairs_ref[1, slot]] += on_other
 
     tile_loop(
         tiles, 1, 4, lambda slot, e: pairs_ref[0, slot], lambda slot: pairs_ref[1, slot], None,
-        mask_ref, turned_ref, points_ref, feature_ref, sums_ref, weights_ref, None, store_other,
-    )
-    flat = points_ref.reshape(count * 8, 128)
-    terms = owned_terms(sums_ref, lambda r: block_rows(flat, r, count, 8), count)
-    for k, row in enumerate(terms(0)):
-        totals_ref[k] = row
-
-
-def remote_kernel(parts, adds, earlier, local_ref, points_ref, feature_ref, mask_any, *rest):
+        words_of, turned_ref, points_ref, feature_ref, sums_ref, weights_ref, None, store_other,
+    )
+
+    def put(k, n, row):
+        totals_ref[k, n : n + 16] = row
+
+    block_terms(sums_ref, 0, points_ref, count, put)
+
+
+def remote_kernel(parts, adds, earlier, local_ref, points_ref, feature_ref, mask_ref, *rest):
     sources, rest = rest[: len(parts)], rest[len(parts) :]
     add_refs, rest = rest[:adds], rest[adds:]
     earlier_refs, rest = rest[:earlier], rest[earlier:]
     totals_ref, rest = rest[0], rest[1:]
     back, rest = rest[: len(parts)], rest[len(parts) :]
-    (
-        sums_ref, turned_ref, weights_ref, other_feature_ref, other_sums, blocks_ref, mask_ref, sems,
-    ) = rest
+    sums_ref, turned_ref, weights_ref, other_feature_ref, other_sums, blocks_ref = rest
     count = points_ref.shape[0]
     per_part = parts[0][3]
     slots = per_part * len(parts)
     starts = [group * first_of_group + first for group, _, first, _, first_of_group in parts]
-    copies = [
-        pltpu.make_async_copy(
-            mask_any.at[pl.ds(2 * start, 2 * per_part)],
-            mask_ref.at[pl.ds(2 * n * per_part, 2 * per_part)],
-            sems.at[n],
-        )
-        for n, start in enumerate(starts)
-    ]
-    for copy in copies:
-        copy.start()
     for n, (_, row, first, _, _) in enumerate(parts):
         for m in range(per_part):
             blocks_ref[n * per_part + m] = sources[n][first + m, row : row + 8]
     turn(lambda n: blocks_ref[n], turned_ref)
     sums_ref[...] = jnp.zeros_like(sums_ref)
-    for copy in copies:
-        copy.wait()
     gap = starts[-1] - starts[0] - per_part
 
+    def entry(slot):
+        return slot + starts[0] + gap * (slot // per_part)
+
     def owned_of(slot, e):
-        return local_ref[e, slot + starts[0] + gap * (slot // per_part)]
+        return local_ref[e, entry(slot)]
+
+    def words_of(slot, e):
+        tile = 2 * entry(slot) + e
+        return jnp.concatenate([mask_ref[tile, pl.ds(j, 8, stride=0), :] for j in range(16)], axis=0)
 
     def store_other(slot, on_other):
         other_sums[slot] = on_other
 
     tile_loop(
-        slots, 2, 2, owned_of, lambda slot: slot, lambda slot: blocks_ref[slot], mask_ref, turned_ref,
+        slots, 2, 2, owned_of, lambda slot: slot, lambda slot: blocks_ref[slot], words_of, turned_ref,
         points_ref, feature_ref, sums_ref, weights_ref, other_feature_ref, store_other,
     )
-    flat = blocks_ref.reshape(slots * 8, 128)
-    for n in range(len(parts)):
-        base = n * per_part
-        terms = owned_terms(other_sums, lambda r: block_rows(flat, 8 * base + r, per_part, 8), per_part)
-        before = back[n].shape[0] - per_part
+    for part in range(len(parts)):
+        before = back[part].shape[0] - per_part
         if before:
-            back[n][0:before] = earlier_refs[n][...]
-        rows = back[n].reshape(back[n].shape[0] * 4, 128)
-        for k, row in enumerate(terms(base)):
-            rows[pl.ds(4 * before + k, per_part, stride=4), :] = row
-    own = points_ref.reshape(count * 8, 128)
-    terms = owned_terms(sums_ref, lambda r: block_rows(own, r, count, 8), count)
-    for k, row in enumerate(terms(0)):
+            back[part][0:before] = earlier_refs[part][...]
+        rows = back[part].reshape(back[part].shape[0] * 4, 128)
+
+        def put_back(k, n, row):
+            rows[pl.ds(4 * (before + n) + k, 16, stride=4), :] = row
+
+        block_terms(other_sums, part * per_part, blocks_ref, per_part, put_back)
+
+    def put(k, n, row):
         for add in add_refs:
-            row = row + add[k]
-        totals_ref[k] = row
+            row = row + add[k, n : n + 16]
+        totals_ref[k, n : n + 16] = row
+
+    block_terms(sums_ref, 0, points_ref, count, put)
 
 
 def update_kernel(
     sends_ref, moves_ref, totals_ref, returned_ref, fields_ref, velocity_ref, storage_ref,
-    new_fields_ref, new_velocity_ref, moving_ref, sums_ref, rows_ref,
+    new_fields_ref, new_velocity_ref, moving_ref, down_ref, here_ref, up_ref, rows_ref,
 ):
     count = storage_ref.shape[0]
     peers = returned_ref.shape[0]
-    sums_ref[...] = jnp.zeros_like(sums_ref)
+    sums_refs = (down_ref, here_ref, up_ref)
+    for sums_ref in sums_refs:
+        sums_ref[...] = jnp.zeros_like(sums_ref)
 
     def one_peer(peer, carry):
-        for o in range(3):
+        for o, sums_ref in enumerate(sums_refs):
             sums_ref[sends_ref[o, 0, peer]] += returned_ref[peer, o]
         return carry
 
-    lax.fori_loop(0, peers, one_peer, 0, unroll=4)
-    sums = sums_ref.reshape(count * 4, 128)
+    lax.fori_loop(0, peers, one_peer, 0, unroll=8)
+    flats = [sums_ref.reshape(count * 4, 128) for sums_ref in sums_refs]
+
+    def total(k):
+        down, here, up = (block_rows(flat, k, count, 4) for flat in flats)
+        return totals_ref[k] + (down + here + up)
+
     rows = rows_ref.reshape(count * 8, 128)
     for k in range(3):
-        speed = velocity_ref[k] + time_step * (totals_ref[k] + block_rows(sums, k, count, 4))
+        speed = velocity_ref[k] + time_step * total(k)
         moved = block_rows(fields_ref, k, count, 4) + time_step * speed
         new_velocity_ref[k] = speed
         new_fields_ref[pl.ds(k, count, stride=4), :] = moved
@@ -330,7 +336,7 @@
     stored = storage_ref[...]
     pressure = (
         block_rows(fields_ref, 3, count, 4)
-        + time_step * (totals_ref[3] + block_rows(sums, 3, count, 4)) / stored
+        + time_step * total(3) / stored
     )
     new_fields_ref[pl.ds(3, count, stride=4), :] = pressure
     rows[pl.ds(3, count, stride=8), :] = pressure
@@ -388,8 +394,7 @@
     return pl.pallas_call(
         functools.partial(remote_kernel, parts, len(adds), len(earlier)),
         out_shape=[shape(4, count, 128)] + [shape(before + per_part, 4, 128)] * len(parts),
-        in_specs=[in_smem(), in_vmem(), in_vmem(), anywhere()]
-        + [in_vmem()] * (len(sources) + len(adds) + len(earlier)),
+        in_specs=[in_smem()] + [in_vmem()] * (3 + len(sources) + len(adds) + len(earlier)),
         out_specs=[in_vmem()] * (1 + len(parts)),
         scratch_shapes=[
             pltpu.VMEM((count, 16, 128), f32),
@@ -398,8 +403,6 @@
             pltpu.VMEM((2, 2, 48, 128), bf16),
             pltpu.VMEM((slots, 16, 128), f32),
             pltpu.VMEM((slots, 8, 128), f32),
-            pltpu.VMEM((2 * slots, 16, 128), jnp.int32),
-            pltpu.SemaphoreType.DMA((len(parts),)),
         ],
         compiler_params=params(),
         cost_estimate=cost(slots * 10**8),
@@ -484,7 +487,7 @@
         out_shape=[shape(count * 4, 128), shape(3, count, 128), shape(peers, 8, 128)],
         in_specs=[in_smem()] * 2 + [in_vmem()] * 5,
         out_specs=[in_vmem()] * 3,
-        scratch_shapes=[pltpu.VMEM((count, 4, 128), f32), pltpu.VMEM((count, 8, 128), f32)],
+        scratch_shapes=[pltpu.VMEM((count, 4, 128), f32)] * 3 + [pltpu.VMEM((count, 8, 128), f32)],
         compiler_params=params(),
         name="update",
     )(sends, moves, totals, returned, flat_fields, velocity.transpose(1, 0, 2), storage)

time: 91.2 us -> 90.8 us (level)
  no operation moved by 1% of the time
where the time goes in v4:
time: 90.8 us; the launch traced here: 90.4 us
  Pallas kernels  30.3 us (33%)
  blocking collectives  30.2 us (33%)
  starting transfers between devices  18.8 us (21%)
  waiting for transfers between devices  7.54 us (8%)
  local copies, waits for them, and re-layouts  2.71 us (3%)
    pallas_call x3, Pallas kernels, remote_tiles(): pl.pallas_call(functools.partial(remote_kernel, parts, len(adds), len(ear...  18.8 us
    all_to_all x1, blocking collectives, per_device(): lax.all_to_all(stacked, 'bulk', split_axis=0, concat_axis=0, tiled=True)  16.5 us
    all_to_all x1, blocking collectives, per_device(): lax.all_to_all(moving, 'bulk', split_axis=0, concat_axis=0, tiled=True)  13.8 us
    all_to_all x1, starting transfers between devices, per_device(): lax.all_to_all(outgoing, 'bulk', split_axis=0, concat_axis=0, tiled=True)  10.2 us
    ppermute x4, starting transfers between devices, from_behind(): lax.ppermute(shard, axis, [(i, (i + by) % peers) for i in range(peers)])  8.64 us
    pallas_call x1, Pallas kernels, local_tiles(): pl.pallas_call(local_kernel, out_shape=[shape(4, count, 128), shape(count...  6.98 us
    all_to_all x1, waiting for transfers between devices, per_device(): lax.all_to_all(outgoing, 'bulk', split_axis=0, concat_axis=0, tiled=True)  5.04 us
    unnamed x22, local copies, waits for them, and re-layouts  2.7 us
  transfers between devices with their start and end apart: 5, of which 2 were waited for; matrix products, arithmetic and copies ran while one was open for 0% of the time, Pallas kernels for 16%

profile of v4, /device:TPU:8, one launch (start us, length us, event | category | flops | bytes accessed | tf_op | source)
XLA Modules:
  0.0 90.4 jit_solution(17010546680720623737)
XLA Ops:
  0.6 2.2 %pack.1 = (f32[32,24,128]{2,1,0:T(8,128)}, f32[64,8,128]{2,1,0:T(8,128)}) custom-call(s32[3,1,32]{2,1,0:T(1,128)} %bitcast.23, s32[1,1,32]{2,1,0:T(1,128)} %bitcast.25, f32[3,64,128]{2,1,0:T(8,128)} %bitcast.36, f32[256,128]{1,0:T(8,128)} %bitcast.19), custom_call_target="tpu_custom_call" | custom-call | tf_op jit(solution)/shard_map/pack/pallas_call | solution.py:449
  2.8 10.2 %all-to-all-start = ((f32[32,24,128]{2,1,0:T(8,128)}), f32[32,24,128]{2,1,0:T(8,128)S(1)}, u32[]{:S(2)}, u32[]{:S(2)}) async-start(f32[32,24,128]{2,1,0:T(8,128)} %get-tuple-element.20), calls=%async_computation | async-start | bytes 786432 | tf_op jit(solution)/shard_map/all_to_all | solution.py:464
  13.0 0.0 copy-start.6
  13.0 1.0 %copy-done.6 = s32[1,64,16,128]{3,2,1,0:T(8,128)S(1)} copy-done((s32[1,64,16,128]{3,2,1,0:T(8,128)S(1)}, s32[1,64,16,128]{3,2,1,0:T(8,128)}, u32[]{:S(2)}) %copy-start.6) | copy-done | bytes 524312
  14.0 0.0 copy-start.7
  14.0 0.9 %copy-done.7 = f32[64,8,128]{2,1,0:T(8,128)S(1)} copy-done((f32[64,8,128]{2,1,0:T(8,128)S(1)}, f32[64,8,128]{2,1,0:T(8,128)}, u32[]{:S(2)}) %copy-start.7) | copy-done | bytes 262168
  15.0 0.0 copy-start.9
  15.0 0.7 copy-done.9
  15.6 0.0 copy-start.5
  15.7 0.0 copy-start.8
  15.7 0.0 copy-start.10
  15.7 7.0 %local_tiles.1 = (f32[4,64,128]{2,1,0:T(8,128)S(1)}, bf16[64,48,128]{2,1,0:T(8,128)(2,1)S(1)}) custom-call(s32[2,64]{1,0:T(2,128)S(1)} %bitcast.31, f32[64,8,128]{2,1,0:T(8,128)S(1)} %copy-done.7, s32[64,16,128]{2,1,0:T(8,128)S(1)} %bitcast.30), custom_call_target="tpu_custom_call" | custom-call | flops 4000000000 | bytes 2097152 | tf_op jit(solution)/shard_map/local_tiles/pallas_call | solution.py:415
  22.6 5.0 %all-to-all-done.rest_0_.early_ref = f32[32,24,128]{2,1,0:T(8,128)S(1)} async-done(((f32[32,24,128]{2,1,0:T(8,128)}), f32[32,24,128]{2,1,0:T(8,128)S(1)}, u32[]{:S(2)}, u32[]{:S(2)}) %all-to-all-start) | async-done | bytes 393248 | tf_op jit(solution)/shard_map/all_to_all | solution.py:464
  27.7 5.7 %collective-permute-start = (f32[32,8,128]{2,1,0:T(8,128)S(1)}, f32[32,8,128]{2,1,0:T(8,128)S(1)}, u32[]{:S(2)}, u32[]{:S(2)}) collective-permute-start(f32[32,8,128]{2,1,0:T(8,128)S(1)} %get-tuple-element.36), channel_id=1, source_target_pairs={{0,480},{32,0},{64,32},{96,64},{128,96},{160,128},{192,160},{224,1... | collective-permute-start | bytes 393224 | tf_op jit(solution)/shard_map/ppermute | solution.py:22
  33.4 0.0 collective-permute-start.1
  33.4 0.0 copy-done.5
  33.4 0.0 copy-done.8
  33.4 0.0 copy-done.10
  33.4 3.6 %remote_tiles.3 = (f32[4,64,128]{2,1,0:T(8,128)S(1)}, f32[16,4,128]{2,1,0:T(4,128)S(1)}) custom-call(s32[2,96]{1,0:T(2,128)S(1)} %bitcast.32, f32[64,8,128]{2,1,0:T(8,128)S(1)} %copy-done.8, bf16[64,48,128]{2,1,0:T(8,128)(2,1)S(1)} %get-tuple-element.22.feature_ref, s32[192,16,128]{2,1,0:T(8,128)S(1)} %bitcast.27, ...), custom_call_target="tpu_custom_call" | custom-call | flops 1600000000 | bytes 2097152 | tf_op jit(solution)/shard_map/remote_tiles/pallas_call | solution.py:394
  37.0 0.0 collective-permute-done.rest_0_
  37.0 2.5 %collective-permute-done.1.rest_1_ = f32[32,8,128]{2,1,0:T(8,128)S(1)} collective-permute-done((f32[32,8,128]{2,1,0:T(8,128)S(1)}, f32[32,8,128]{2,1,0:T(8,128)S(1)}, u32[]{:S(2)}, u32[]{:S(2)}) %collective-permute-start.1) | collective-permute-done | bytes 131104 | tf_op jit(solution)/shard_map/ppermute | solution.py:22
  39.5 11.5 %remote_tiles.4 = (f32[4,64,128]{2,1,0:T(8,128)S(1)}, f32[32,4,128]{2,1,0:T(4,128)S(1)}, f32[32,4,128]{2,1,0:T(4,128)S(1)}) custom-call(s32[2,96]{1,0:T(2,128)S(1)} %bitcast.33, f32[64,8,128]{2,1,0:T(8,128)S(1)} %copy-done.8, bf16[64,48,128]{2,1,0:T(8,128)(2,1)S(1)} %get-tuple-element.22.feature_ref, s32[192,16,128]{2,1,0:T(8,128)S(1)} %bitcast.28, ...), custom_call_target="tpu_custom_call" | custom-call | flops 6400000000 | bytes 2097152 | tf_op jit(solution)/shard_map/remote_tiles/pallas_call | solution.py:394
  51.1 0.0 collective-permute-start.2
  51.1 2.9 %collective-permute-start.3 = (f32[32,4,128]{2,1,0:T(4,128)S(1)}, f32[32,4,128]{2,1,0:T(4,128)S(1)}, u32[]{:S(2)}, u32[]{:S(2)}) collective-permute-start(f32[32,4,128]{2,1,0:T(4,128)S(1)} %get-tuple-element.31), channel_id=1, source_target_pairs={{0,480},{32,0},{64,32},{96,64},{128,96},{160,128},{192,160},{224,1... | collective-permute-start | bytes 196616 | tf_op jit(solution)/shard_map/ppermute | solution.py:22
  54.0 0.0 copy-start
  54.0 0.0 copy-start.1
  54.0 0.0 copy-start.2
  54.0 0.0 copy-start.3
  54.1 0.0 copy-start.4
  54.1 3.6 %remote_tiles.5 = (f32[4,64,128]{2,1,0:T(8,128)S(1)}, f32[32,4,128]{2,1,0:T(4,128)S(1)}) custom-call(s32[2,96]{1,0:T(2,128)S(1)} %bitcast.34, f32[64,8,128]{2,1,0:T(8,128)S(1)} %copy-done.8, bf16[64,48,128]{2,1,0:T(8,128)(2,1)S(1)} %get-tuple-element.22.feature_ref, s32[192,16,128]{2,1,0:T(8,128)S(1)} %bitcast.29, ...), custom_call_target="tpu_custom_call" | custom-call | flops 1600000000 | bytes 2097152 | tf_op jit(solution)/shard_map/remote_tiles/pallas_call | solution.py:394
  57.7 0.0 collective-permute-done.2
  57.7 0.0 collective-permute-done.3
  57.8 16.5 %all_to_all.15.returned_ref = f32[32,3,4,128]{3,2,1,0:T(4,128)S(1)} all-to-all(f32[32,3,4,128]{3,2,1,0:T(4,128)S(1)} %pad_maximum_fusion), channel_id=1, replica_groups=mesh['region'=16,'bulk'=32] {'bulk'}, dimensions={0} | all-to-all | bytes 393216 | tf_op jit(solution)/shard_map/all_to_all | solution.py:484
  74.2 0.0 copy-done
  74.2 0.0 copy-done.1
  74.2 0.0 copy-done.2
  74.3 0.0 copy-done.3
  74.3 0.0 copy-done.4
  74.3 1.7 %update.1 = (f32[256,128]{1,0:T(8,128)}, f32[3,64,128]{2,1,0:T(8,128)}, f32[32,8,128]{2,1,0:T(8,128)S(1)}) custom-call(s32[3,1,32]{2,1,0:T(1,128)S(1)} %bitcast.24, s32[1,1,32]{2,1,0:T(1,128)S(1)} %bitcast.26, f32[4,64,128]{2,1,0:T(8,128)S(1)} %get-tuple-element.28.totals_ref, f32[32,3,4,128]{3,2,1,0:T(4,128)S(1)} %all_to_all.15.returned_ref, ...), custom_call_target="tpu_custom_call" | custom-call | tf_op jit(solution)/shard_map/update/pallas_call | solution.py:485
  76.0 13.8 %all_to_all.16.late_ref = f32[32,8,128]{2,1,0:T(8,128)S(1)} all-to-all(f32[32,8,128]{2,1,0:T(8,128)S(1)} %get-tuple-element.34), channel_id=1, replica_groups=mesh['region'=16,'bulk'=32] {'bulk'}, dimensions={0} | all-to-all | bytes 262144 | tf_op jit(solution)/shard_map/all_to_all | solution.py:494
  89.7 0.7 arrive.1
  (2 shorter events, 0.1 us)
Async XLA Ops:
  2.8 24.9 %all-to-all-start = ((f32[32,24,128]{2,1,0:T(8,128)}), f32[32,24,128]{2,1,0:T(8,128)S(1)}, u32[]{:S(2)}, u32[]{:S(2)}) async-start(f32[32,24,128]{2,1,0:T(8,128)} %get-tuple-element.20), calls=%async_computation | async-start | bytes 786432 | tf_op jit(solution)/shard_map/all_to_all | solution.py:464
  13.0 1.0 %copy-start.6 = (s32[1,64,16,128]{3,2,1,0:T(8,128)S(1)}, s32[1,64,16,128]{3,2,1,0:T(8,128)}, u32[]{:S(2)}) copy-start(s32[1,64,16,128]{3,2,1,0:T(8,128)} %param.18) | copy-start | bytes 1572868
  14.0 0.9 %copy-start.7 = (f32[64,8,128]{2,1,0:T(8,128)S(1)}, f32[64,8,128]{2,1,0:T(8,128)}, u32[]{:S(2)}) copy-start(f32[64,8,128]{2,1,0:T(8,128)} %get-tuple-element.19.points_ref) | copy-start | bytes 786436
  15.0 0.7 copy-start.9
  15.6 17.7 %copy-start.5 = (s32[1,96,2,16,128]{4,3,2,1,0:T(8,128)S(1)}, s32[1,96,2,16,128]{4,3,2,1,0:T(8,128)}, u32[]{:S(2)}) copy-start(s32[1,96,2,16,128]{4,3,2,1,0:T(8,128)} %param.16) | copy-start | bytes 4718596
  15.7 17.7 %copy-start.8 = (f32[64,8,128]{2,1,0:T(8,128)S(1)}, f32[64,8,128]{2,1,0:T(8,128)}, u32[]{:S(2)}) copy-start(f32[64,8,128]{2,1,0:T(8,128)} %get-tuple-element.19.points_ref) | copy-start | bytes 786436
  15.7 17.7 %copy-start.10 = (s32[1,96,2]{1,2,0:T(2,128)S(1)}, s32[1,96,2]{1,2,0:T(2,128)}, u32[]{:S(2)}) copy-start(s32[1,96,2]{1,2,0:T(2,128)} %param.15) | copy-start | bytes 2308
  27.7 9.3 %collective-permute-start = (f32[32,8,128]{2,1,0:T(8,128)S(1)}, f32[32,8,128]{2,1,0:T(8,128)S(1)}, u32[]{:S(2)}, u32[]{:S(2)}) collective-permute-start(f32[32,8,128]{2,1,0:T(8,128)S(1)} %get-tuple-element.36), channel_id=1, source_target_pairs={{0,480},{32,0},{64,32},{96,64},{128,96},{160,128},{192,160},{224,1... | collective-permute-start | bytes 393224 | tf_op jit(solution)/shard_map/ppermute | solution.py:22
  33.4 6.1 %collective-permute-start.1 = (f32[32,8,128]{2,1,0:T(8,128)S(1)}, f32[32,8,128]{2,1,0:T(8,128)S(1)}, u32[]{:S(2)}, u32[]{:S(2)}) collective-permute-start(f32[32,8,128]{2,1,0:T(8,128)S(1)} %get-tuple-element.35), channel_id=1, source_target_pairs={{0,32},{32,64},{64,96},{96,128},{128,160},{160,192},{192,224},{224... | collective-permute-start | bytes 393224 | tf_op jit(solution)/shard_map/ppermute | solution.py:22
  51.1 6.6 %collective-permute-start.2 = (f32[32,4,128]{2,1,0:T(4,128)S(1)}, f32[32,4,128]{2,1,0:T(4,128)S(1)}, u32[]{:S(2)}, u32[]{:S(2)}) collective-permute-start(f32[32,4,128]{2,1,0:T(4,128)S(1)} %get-tuple-element.29), channel_id=1, source_target_pairs={{0,32},{32,64},{64,96},{96,128},{128,160},{160,192},{192,224},{224... | collective-permute-start | bytes 196616 | tf_op jit(solution)/shard_map/ppermute | solution.py:22
  51.1 6.6 %collective-permute-start.3 = (f32[32,4,128]{2,1,0:T(4,128)S(1)}, f32[32,4,128]{2,1,0:T(4,128)S(1)}, u32[]{:S(2)}, u32[]{:S(2)}) collective-permute-start(f32[32,4,128]{2,1,0:T(4,128)S(1)} %get-tuple-element.31), channel_id=1, source_target_pairs={{0,480},{32,0},{64,32},{96,64},{128,96},{160,128},{192,160},{224,1... | collective-permute-start | bytes 196616 | tf_op jit(solution)/shard_map/ppermute | solution.py:22
  54.0 20.2 %copy-start = (f32[64,4,128]{2,1,0:T(4,128)S(1)}, f32[64,4,128]{2,1,0:T(4,128)}, u32[]{:S(2)}) copy-start(f32[64,4,128]{2,1,0:T(4,128)} %param.11) | copy-start | bytes 393220
  54.0 20.2 %copy-start.1 = (f32[64,3,128]{2,0,1:T(8,128)S(1)}, f32[64,3,128]{2,0,1:T(8,128)}, u32[]{:S(2)}) copy-start(f32[64,3,128]{2,0,1:T(8,128)} %param.13) | copy-start | bytes 294916
  54.0 20.2 %copy-start.2 = (f32[64,128]{1,0:T(8,128)S(1)}, f32[64,128]{1,0:T(8,128)}, u32[]{:S(2)}) copy-start(f32[64,128]{1,0:T(8,128)} %storage_ref.1) | copy-start | bytes 98308
  54.0 20.2 %copy-start.3 = (s32[1,3,32,1]{2,3,1,0:T(1,128)S(1)}, s32[1,3,32,1]{2,3,1,0:T(1,128)}, u32[]{:S(2)}) copy-start(s32[1,3,32,1]{2,3,1,0:T(1,128)} %param.14) | copy-start | bytes 1156
  54.1 20.2 %copy-start.4 = (s32[1,32,1]{1,2,0:T(1,128)S(1)}, s32[1,32,1]{1,2,0:T(1,128)}, u32[]{:S(2)}) copy-start(s32[1,32,1]{1,2,0:T(1,128)} %param.19) | copy-start | bytes 388

commit v5 on v4

--- a/solution.py
+++ b/solution.py
@@ -152,16 +152,16 @@
     weigh(0, 0)
 
     def body(k, carry):
-        weigh(2 * k + 1, 1)
-        add_up(2 * k, 0)
-        weigh(2 * k + 2, 0)
-        add_up(2 * k + 1, 1)
+        for n in range(4):
+            weigh(4 * k + n + 1, (n + 1) % 4)
+            add_up(4 * k + n, n)
         return carry
 
-    lax.fori_loop(0, steps // 2 - 1, body, 0)
-    weigh(steps - 1, 1)
-    add_up(steps - 2, 0)
-    add_up(steps - 1, 1)
+    lax.fori_loop(0, steps // 4 - 1, body, 0)
+    for n in range(4):
+        if n < 3:
+            weigh(steps - 3 + n, n + 1)
+        add_up(steps - 4 + n, n)
 
 
 def block_terms(sums_ref, first, blocks_ref, count, put):
@@ -399,8 +399,8 @@
         scratch_shapes=[
             pltpu.VMEM((count, 16, 128), f32),
             pltpu.VMEM((slots // 16, 128, 128), f32),
-            pltpu.VMEM((2, 4, 256, 256), bf16),
-            pltpu.VMEM((2, 2, 48, 128), bf16),
+            pltpu.VMEM((4, 4, 256, 256), bf16),
+            pltpu.VMEM((4, 2, 48, 128), bf16),
             pltpu.VMEM((slots, 16, 128), f32),
             pltpu.VMEM((slots, 8, 128), f32),
         ],
@@ -420,7 +420,7 @@
         scratch_shapes=[
             pltpu.VMEM((count, 16, 128), f32),
             pltpu.VMEM((count // 16, 128, 128), f32),
-            pltpu.VMEM((2, 4, 256, 256), bf16),
+            pltpu.VMEM((4, 4, 256, 256), bf16),
         ],
         compiler_params=params(),
         cost_estimate=cost(4 * 10**9),

time: 90.8 us -> 89.5 us (0.986)
  Pallas kernels: 30.3 us -> 28.5 us
    pallas_call x3, Pallas kernels: 18.8 us -> 17.4 us  [remote_tiles(): pl.pallas_call(functools.partial(remote_kernel, parts, len(adds), len(ear...]
  transfers between devices with their start and end apart: 5 -> 5, of which waited for: 2 -> 2; matrix products, arithmetic and copies ran while one was open for 0% -> 0% of each run, Pallas kernels for 16% -> 15%
where the time goes in v5:
time: 89.5 us; the launch traced here: 89.1 us
  blocking collectives  30.1 us (34%)
  Pallas kernels  28.5 us (32%)
  starting transfers between devices  18.8 us (21%)
  waiting for transfers between devices  8.1 us (9%)
  local copies, waits for them, and re-layouts  2.71 us (3%)
    pallas_call x3, Pallas kernels, remote_tiles(): pl.pallas_call(functools.partial(remote_kernel, parts, len(adds), len(ear...  17.4 us
    all_to_all x1, blocking collectives, per_device(): lax.all_to_all(stacked, 'bulk', split_axis=0, concat_axis=0, tiled=True)  16.3 us
    all_to_all x1, blocking collectives, per_device(): lax.all_to_all(moving, 'bulk', split_axis=0, concat_axis=0, tiled=True)  13.8 us
    all_to_all x1, starting transfers between devices, per_device(): lax.all_to_all(outgoing, 'bulk', split_axis=0, concat_axis=0, tiled=True)  10.2 us
    ppermute x4, starting transfers between devices, from_behind(): lax.ppermute(shard, axis, [(i, (i + by) % peers) for i in range(peers)])  8.64 us
    pallas_call x1, Pallas kernels, local_tiles(): pl.pallas_call(local_kernel, out_shape=[shape(4, count, 128), shape(count...  6.59 us
    all_to_all x1, waiting for transfers between devices, per_device(): lax.all_to_all(outgoing, 'bulk', split_axis=0, concat_axis=0, tiled=True)  5.43 us
    unnamed x22, local copies, waits for them, and re-layouts  2.7 us
  transfers between devices with their start and end apart: 5, of which 2 were waited for; matrix products, arithmetic and copies ran while one was open for 0% of the time, Pallas kernels for 15%

profile of v5, /device:TPU:8, one launch (start us, length us, event | category | flops | bytes accessed | tf_op | source)
XLA Modules:
  0.0 89.1 jit_solution(18258941775626850059)
XLA Ops:
  0.6 2.2 %pack.1 = (f32[32,24,128]{2,1,0:T(8,128)}, f32[64,8,128]{2,1,0:T(8,128)}) custom-call(s32[3,1,32]{2,1,0:T(1,128)} %bitcast.23, s32[1,1,32]{2,1,0:T(1,128)} %bitcast.25, f32[3,64,128]{2,1,0:T(8,128)} %bitcast.36, f32[256,128]{1,0:T(8,128)} %bitcast.19), custom_call_target="tpu_custom_call" | custom-call | tf_op jit(solution)/shard_map/pack/pallas_call | solution.py:449
  2.8 10.2 %all-to-all-start = ((f32[32,24,128]{2,1,0:T(8,128)}), f32[32,24,128]{2,1,0:T(8,128)S(1)}, u32[]{:S(2)}, u32[]{:S(2)}) async-start(f32[32,24,128]{2,1,0:T(8,128)} %get-tuple-element.20), calls=%async_computation | async-start | bytes 786432 | tf_op jit(solution)/shard_map/all_to_all | solution.py:464
  13.0 0.0 copy-start.6
  13.0 1.0 %copy-done.6 = s32[1,64,16,128]{3,2,1,0:T(8,128)S(1)} copy-done((s32[1,64,16,128]{3,2,1,0:T(8,128)S(1)}, s32[1,64,16,128]{3,2,1,0:T(8,128)}, u32[]{:S(2)}) %copy-start.6) | copy-done | bytes 524312
  14.0 0.0 copy-start.7
  14.0 0.9 %copy-done.7 = f32[64,8,128]{2,1,0:T(8,128)S(1)} copy-done((f32[64,8,128]{2,1,0:T(8,128)S(1)}, f32[64,8,128]{2,1,0:T(8,128)}, u32[]{:S(2)}) %copy-start.7) | copy-done | bytes 262168
  15.0 0.0 copy-start.9
  15.0 0.7 copy-done.9
  15.6 0.0 copy-start.5
  15.7 0.0 copy-start.8
  15.7 0.0 copy-start.10
  15.7 6.6 %local_tiles.1 = (f32[4,64,128]{2,1,0:T(8,128)S(1)}, bf16[64,48,128]{2,1,0:T(8,128)(2,1)S(1)}) custom-call(s32[2,64]{1,0:T(2,128)S(1)} %bitcast.31, f32[64,8,128]{2,1,0:T(8,128)S(1)} %copy-done.7, s32[64,16,128]{2,1,0:T(8,128)S(1)} %bitcast.30), custom_call_target="tpu_custom_call" | custom-call | flops 4000000000 | bytes 2097152 | tf_op jit(solution)/shard_map/local_tiles/pallas_call | solution.py:415
  22.3 5.4 %all-to-all-done.rest_0_.early_ref = f32[32,24,128]{2,1,0:T(8,128)S(1)} async-done(((f32[32,24,128]{2,1,0:T(8,128)}), f32[32,24,128]{2,1,0:T(8,128)S(1)}, u32[]{:S(2)}, u32[]{:S(2)}) %all-to-all-start) | async-done | bytes 393248 | tf_op jit(solution)/shard_map/all_to_all | solution.py:464
  27.7 5.7 %collective-permute-start = (f32[32,8,128]{2,1,0:T(8,128)S(1)}, f32[32,8,128]{2,1,0:T(8,128)S(1)}, u32[]{:S(2)}, u32[]{:S(2)}) collective-permute-start(f32[32,8,128]{2,1,0:T(8,128)S(1)} %get-tuple-element.36), channel_id=1, source_target_pairs={{0,480},{32,0},{64,32},{96,64},{128,96},{160,128},{192,160},{224,1... | collective-permute-start | bytes 393224 | tf_op jit(solution)/shard_map/ppermute | solution.py:22
  33.4 0.0 collective-permute-start.1
  33.4 0.0 copy-done.5
  33.4 0.0 copy-done.8
  33.4 0.0 copy-done.10
  33.4 3.4 %remote_tiles.3 = (f32[4,64,128]{2,1,0:T(8,128)S(1)}, f32[16,4,128]{2,1,0:T(4,128)S(1)}) custom-call(s32[2,96]{1,0:T(2,128)S(1)} %bitcast.32, f32[64,8,128]{2,1,0:T(8,128)S(1)} %copy-done.8, bf16[64,48,128]{2,1,0:T(8,128)(2,1)S(1)} %get-tuple-element.22.feature_ref, s32[192,16,128]{2,1,0:T(8,128)S(1)} %bitcast.27, ...), custom_call_target="tpu_custom_call" | custom-call | flops 1600000000 | bytes 2097152 | tf_op jit(solution)/shard_map/remote_tiles/pallas_call | solution.py:394
  36.8 0.0 collective-permute-done.rest_0_
  36.9 2.7 %collective-permute-done.1.rest_1_ = f32[32,8,128]{2,1,0:T(8,128)S(1)} collective-permute-done((f32[32,8,128]{2,1,0:T(8,128)S(1)}, f32[32,8,128]{2,1,0:T(8,128)S(1)}, u32[]{:S(2)}, u32[]{:S(2)}) %collective-permute-start.1) | collective-permute-done | bytes 131104 | tf_op jit(solution)/shard_map/ppermute | solution.py:22
  39.5 10.5 %remote_tiles.4 = (f32[4,64,128]{2,1,0:T(8,128)S(1)}, f32[32,4,128]{2,1,0:T(4,128)S(1)}, f32[32,4,128]{2,1,0:T(4,128)S(1)}) custom-call(s32[2,96]{1,0:T(2,128)S(1)} %bitcast.33, f32[64,8,128]{2,1,0:T(8,128)S(1)} %copy-done.8, bf16[64,48,128]{2,1,0:T(8,128)(2,1)S(1)} %get-tuple-element.22.feature_ref, s32[192,16,128]{2,1,0:T(8,128)S(1)} %bitcast.28, ...), custom_call_target="tpu_custom_call" | custom-call | flops 6400000000 | bytes 2097152 | tf_op jit(solution)/shard_map/remote_tiles/pallas_call | solution.py:394
  50.1 0.0 collective-permute-start.2
  50.1 2.9 %collective-permute-start.3 = (f32[32,4,128]{2,1,0:T(4,128)S(1)}, f32[32,4,128]{2,1,0:T(4,128)S(1)}, u32[]{:S(2)}, u32[]{:S(2)}) collective-permute-start(f32[32,4,128]{2,1,0:T(4,128)S(1)} %get-tuple-element.31), channel_id=1, source_target_pairs={{0,480},{32,0},{64,32},{96,64},{128,96},{160,128},{192,160},{224,1... | collective-permute-start | bytes 196616 | tf_op jit(solution)/shard_map/ppermute | solution.py:22
  53.0 0.0 copy-start
  53.0 0.0 copy-start.1
  53.0 0.0 copy-start.2
  53.0 0.0 copy-start.3
  53.0 0.0 copy-start.4
  53.0 3.5 %remote_tiles.5 = (f32[4,64,128]{2,1,0:T(8,128)S(1)}, f32[32,4,128]{2,1,0:T(4,128)S(1)}) custom-call(s32[2,96]{1,0:T(2,128)S(1)} %bitcast.34, f32[64,8,128]{2,1,0:T(8,128)S(1)} %copy-done.8, bf16[64,48,128]{2,1,0:T(8,128)(2,1)S(1)} %get-tuple-element.22.feature_ref, s32[192,16,128]{2,1,0:T(8,128)S(1)} %bitcast.29, ...), custom_call_target="tpu_custom_call" | custom-call | flops 1600000000 | bytes 2097152 | tf_op jit(solution)/shard_map/remote_tiles/pallas_call | solution.py:394
  56.5 0.0 collective-permute-done.2
  56.5 0.0 collective-permute-done.3
  56.6 16.3 %all_to_all.15.returned_ref = f32[32,3,4,128]{3,2,1,0:T(4,128)S(1)} all-to-all(f32[32,3,4,128]{3,2,1,0:T(4,128)S(1)} %pad_maximum_fusion), channel_id=1, replica_groups=mesh['region'=16,'bulk'=32] {'bulk'}, dimensions={0} | all-to-all | bytes 393216 | tf_op jit(solution)/shard_map/all_to_all | solution.py:484
  72.9 0.0 copy-done
  72.9 0.0 copy-done.1
  72.9 0.0 copy-done.2
  72.9 0.0 copy-done.3
  73.0 0.0 copy-done.4
  73.0 1.7 %update.1 = (f32[256,128]{1,0:T(8,128)}, f32[3,64,128]{2,1,0:T(8,128)}, f32[32,8,128]{2,1,0:T(8,128)S(1)}) custom-call(s32[3,1,32]{2,1,0:T(1,128)S(1)} %bitcast.24, s32[1,1,32]{2,1,0:T(1,128)S(1)} %bitcast.26, f32[4,64,128]{2,1,0:T(8,128)S(1)} %get-tuple-element.28.totals_ref, f32[32,3,4,128]{3,2,1,0:T(4,128)S(1)} %all_to_all.15.returned_ref, ...), custom_call_target="tpu_custom_call" | custom-call | tf_op jit(solution)/shard_map/update/pallas_call | solution.py:485
  74.6 13.8 %all_to_all.16.late_ref = f32[32,8,128]{2,1,0:T(8,128)S(1)} all-to-all(f32[32,8,128]{2,1,0:T(8,128)S(1)} %get-tuple-element.34), channel_id=1, replica_groups=mesh['region'=16,'bulk'=32] {'bulk'}, dimensions={0} | all-to-all | bytes 262144 | tf_op jit(solution)/shard_map/all_to_all | solution.py:494
  88.4 0.7 arrive.1
  (2 shorter events, 0.1 us)
Async XLA Ops:
  2.8 24.9 %all-to-all-start = ((f32[32,24,128]{2,1,0:T(8,128)}), f32[32,24,128]{2,1,0:T(8,128)S(1)}, u32[]{:S(2)}, u32[]{:S(2)}) async-start(f32[32,24,128]{2,1,0:T(8,128)} %get-tuple-element.20), calls=%async_computation | async-start | bytes 786432 | tf_op jit(solution)/shard_map/all_to_all | solution.py:464
  13.0 1.0 %copy-start.6 = (s32[1,64,16,128]{3,2,1,0:T(8,128)S(1)}, s32[1,64,16,128]{3,2,1,0:T(8,128)}, u32[]{:S(2)}) copy-start(s32[1,64,16,128]{3,2,1,0:T(8,128)} %param.18) | copy-start | bytes 1572868
  14.0 0.9 %copy-start.7 = (f32[64,8,128]{2,1,0:T(8,128)S(1)}, f32[64,8,128]{2,1,0:T(8,128)}, u32[]{:S(2)}) copy-start(f32[64,8,128]{2,1,0:T(8,128)} %get-tuple-element.19.points_ref) | copy-start | bytes 786436
  15.0 0.7 copy-start.9
  15.6 17.7 %copy-start.5 = (s32[1,96,2,16,128]{4,3,2,1,0:T(8,128)S(1)}, s32[1,96,2,16,128]{4,3,2,1,0:T(8,128)}, u32[]{:S(2)}) copy-start(s32[1,96,2,16,128]{4,3,2,1,0:T(8,128)} %param.16) | copy-start | bytes 4718596
  15.7 17.7 %copy-start.8 = (f32[64,8,128]{2,1,0:T(8,128)S(1)}, f32[64,8,128]{2,1,0:T(8,128)}, u32[]{:S(2)}) copy-start(f32[64,8,128]{2,1,0:T(8,128)} %get-tuple-element.19.points_ref) | copy-start | bytes 786436
  15.7 17.7 %copy-start.10 = (s32[1,96,2]{1,2,0:T(2,128)S(1)}, s32[1,96,2]{1,2,0:T(2,128)}, u32[]{:S(2)}) copy-start(s32[1,96,2]{1,2,0:T(2,128)} %param.15) | copy-start | bytes 2308
  27.7 9.1 %collective-permute-start = (f32[32,8,128]{2,1,0:T(8,128)S(1)}, f32[32,8,128]{2,1,0:T(8,128)S(1)}, u32[]{:S(2)}, u32[]{:S(2)}) collective-permute-start(f32[32,8,128]{2,1,0:T(8,128)S(1)} %get-tuple-element.36), channel_id=1, source_target_pairs={{0,480},{32,0},{64,32},{96,64},{128,96},{160,128},{192,160},{224,1... | collective-permute-start | bytes 393224 | tf_op jit(solution)/shard_map/ppermute | solution.py:22
  33.4 6.1 %collective-permute-start.1 = (f32[32,8,128]{2,1,0:T(8,128)S(1)}, f32[32,8,128]{2,1,0:T(8,128)S(1)}, u32[]{:S(2)}, u32[]{:S(2)}) collective-permute-start(f32[32,8,128]{2,1,0:T(8,128)S(1)} %get-tuple-element.35), channel_id=1, source_target_pairs={{0,32},{32,64},{64,96},{96,128},{128,160},{160,192},{192,224},{224... | collective-permute-start | bytes 393224 | tf_op jit(solution)/shard_map/ppermute | solution.py:22
  50.1 6.5 %collective-permute-start.2 = (f32[32,4,128]{2,1,0:T(4,128)S(1)}, f32[32,4,128]{2,1,0:T(4,128)S(1)}, u32[]{:S(2)}, u32[]{:S(2)}) collective-permute-start(f32[32,4,128]{2,1,0:T(4,128)S(1)} %get-tuple-element.29), channel_id=1, source_target_pairs={{0,32},{32,64},{64,96},{96,128},{128,160},{160,192},{192,224},{224... | collective-permute-start | bytes 196616 | tf_op jit(solution)/shard_map/ppermute | solution.py:22
  50.1 6.4 %collective-permute-start.3 = (f32[32,4,128]{2,1,0:T(4,128)S(1)}, f32[32,4,128]{2,1,0:T(4,128)S(1)}, u32[]{:S(2)}, u32[]{:S(2)}) collective-permute-start(f32[32,4,128]{2,1,0:T(4,128)S(1)} %get-tuple-element.31), channel_id=1, source_target_pairs={{0,480},{32,0},{64,32},{96,64},{128,96},{160,128},{192,160},{224,1... | collective-permute-start | bytes 196616 | tf_op jit(solution)/shard_map/ppermute | solution.py:22
  53.0 19.9 %copy-start = (f32[64,4,128]{2,1,0:T(4,128)S(1)}, f32[64,4,128]{2,1,0:T(4,128)}, u32[]{:S(2)}) copy-start(f32[64,4,128]{2,1,0:T(4,128)} %param.11) | copy-start | bytes 393220
  53.0 19.9 %copy-start.1 = (f32[64,3,128]{2,0,1:T(8,128)S(1)}, f32[64,3,128]{2,0,1:T(8,128)}, u32[]{:S(2)}) copy-start(f32[64,3,128]{2,0,1:T(8,128)} %param.13) | copy-start | bytes 294916
  53.0 19.9 %copy-start.2 = (f32[64,128]{1,0:T(8,128)S(1)}, f32[64,128]{1,0:T(8,128)}, u32[]{:S(2)}) copy-start(f32[64,128]{1,0:T(8,128)} %storage_ref.1) | copy-start | bytes 98308
  53.0 19.9 %copy-start.3 = (s32[1,3,32,1]{2,3,1,0:T(1,128)S(1)}, s32[1,3,32,1]{2,3,1,0:T(1,128)}, u32[]{:S(2)}) copy-start(s32[1,3,32,1]{2,3,1,0:T(1,128)} %param.14) | copy-start | bytes 1156
  53.0 19.9 %copy-start.4 = (s32[1,32,1]{1,2,0:T(1,128)S(1)}, s32[1,32,1]{1,2,0:T(1,128)}, u32[]{:S(2)}) copy-start(s32[1,32,1]{1,2,0:T(1,128)} %param.19) | copy-start | bytes 388

commit v6 on v5

--- a/solution.py
+++ b/solution.py
@@ -187,8 +187,8 @@
 
 
 def pack_kernel(
-    sends_any, moves_any, positions_any, fields_any, out_ref, points_ref,
-    sends_ref, moves_ref, positions_ref, fields_ref, sems,
+    sends_any, moves_any, positions_any, fields_any, out_any, points_any,
+    sends_ref, moves_ref, positions_ref, fields_ref, out_ref, points_ref, sems,
 ):
     pairs = (
         (positions_any, positions_ref),
@@ -204,6 +204,8 @@
         flat[pl.ds(4 + k, count, stride=8), :] = block_rows(fields_ref, k, count, 4)
     flat[pl.ds(3, count, stride=8), :] = block_rows(fields_ref, 3, count, 4)
     flat[pl.ds(7, count, stride=8), :] = jnp.zeros((count, 128), f32)
+    away = [pltpu.make_async_copy(points_ref, points_any, sems.at[4])]
+    away[0].start()
     last = lax.broadcasted_iota(jnp.int32, (8, 128), 0) == 7
 
     def one_peer(peer, carry):
@@ -215,7 +217,14 @@
             out_ref[peer, 8 * o : 8 * o + 8] = jnp.where(last, moved[o : o + 1], block)
         return carry
 
-    lax.fori_loop(0, out_ref.shape[0], one_peer, 0, unroll=8)
+    peers = out_ref.shape[0]
+    for n in range(4):
+        low, high = n * peers // 4, (n + 1) * peers // 4
+        lax.fori_loop(low, high, one_peer, 0, unroll=True)
+        away.append(pltpu.make_async_copy(out_ref.at[low:high], out_any.at[low:high], sems.at[5 + n]))
+        away[-1].start()
+    for copy in away:
+        copy.wait()
 
 
 def local_kernel(
@@ -305,7 +314,7 @@
 
 def update_kernel(
     sends_ref, moves_ref, totals_ref, returned_ref, fields_ref, velocity_ref, storage_ref,
-    new_fields_ref, new_velocity_ref, moving_ref, down_ref, here_ref, up_ref, rows_ref,
+    rows_ref, moving_ref, down_ref, here_ref, up_ref,
 ):
     count = storage_ref.shape[0]
     peers = returned_ref.shape[0]
@@ -329,8 +338,6 @@
     for k in range(3):
         speed = velocity_ref[k] + time_step * total(k)
         moved = block_rows(fields_ref, k, count, 4) + time_step * speed
-        new_velocity_ref[k] = speed
-        new_fields_ref[pl.ds(k, count, stride=4), :] = moved
         rows[pl.ds(k, count, stride=8), :] = moved
         rows[pl.ds(4 + k, count, stride=8), :] = speed
     stored = storage_ref[...]
@@ -338,7 +345,6 @@
         block_rows(fields_ref, 3, count, 4)
         + time_step * total(3) / stored
     )
-    new_fields_ref[pl.ds(3, count, stride=4), :] = pressure
     rows[pl.ds(3, count, stride=8), :] = pressure
     rows[pl.ds(7, count, stride=8), :] = stored
 
@@ -349,6 +355,15 @@
         return carry
 
     lax.fori_loop(0, peers, one_move, 0, unroll=4)
+
+
+def store_kernel(rows_ref, new_fields_ref, new_velocity_ref):
+    count = rows_ref.shape[0]
+    rows = rows_ref.reshape(count * 8, 128)
+    for k in range(4):
+        new_fields_ref[pl.ds(k, count, stride=4), :] = block_rows(rows, k, count, 8)
+    for k in range(3):
+        new_velocity_ref[k] = block_rows(rows, 4 + k, count, 8)
 
 
 def arrive_kernel(late_ref, early_ref, out_ref):
@@ -450,13 +465,15 @@
         pack_kernel,
         out_shape=[shape(peers, 24, 128), shape(count, 8, 128)],
         in_specs=[anywhere()] * 4,
-        out_specs=[in_vmem()] * 2,
+        out_specs=[anywhere()] * 2,
         scratch_shapes=[
             pltpu.SMEM(sends.shape, jnp.int32),
             pltpu.SMEM(moves.shape, jnp.int32),
             pltpu.VMEM(rows_first.shape, f32),
             pltpu.VMEM(flat_fields.shape, f32),
-            pltpu.SemaphoreType.DMA((4,)),
+            pltpu.VMEM((peers, 24, 128), f32),
+            pltpu.VMEM((count, 8, 128), f32),
+            pltpu.SemaphoreType.DMA((9,)),
         ],
         compiler_params=pltpu.CompilerParams(vmem_limit_bytes=60 * 1024 * 1024),
         name="pack",
@@ -482,16 +499,25 @@
     )
     stacked = jnp.stack([down_back, here_back, up_back], axis=1)
     returned = lax.all_to_all(stacked, "bulk", split_axis=0, concat_axis=0, tiled=True)
-    new_fields, new_velocity, moving = pl.pallas_call(
+    rows, moving = pl.pallas_call(
         update_kernel,
-        out_shape=[shape(count * 4, 128), shape(3, count, 128), shape(peers, 8, 128)],
+        out_shape=[shape(count, 8, 128), shape(peers, 8, 128)],
         in_specs=[in_smem()] * 2 + [in_vmem()] * 5,
-        out_specs=[in_vmem()] * 3,
-        scratch_shapes=[pltpu.VMEM((count, 4, 128), f32)] * 3 + [pltpu.VMEM((count, 8, 128), f32)],
+        out_specs=[in_vmem()] * 2,
+        scratch_shapes=[pltpu.VMEM((count, 4, 128), f32)] * 3,
         compiler_params=params(),
         name="update",
     )(sends, moves, totals, returned, flat_fields, velocity.transpose(1, 0, 2), storage)
     late = lax.all_to_all(moving, "bulk", split_axis=0, concat_axis=0, tiled=True)
+    new_fields, new_velocity = pl.pallas_call(
+        store_kernel,
+        out_shape=[shape(count * 4, 128), shape(3, count, 128)],
+        in_specs=[in_vmem()],
+        out_specs=[in_vmem()] * 2,
+        compiler_params=params(),
+        cost_estimate=cost(10**9),
+        name="store",
+    )(rows)
     arrived = pl.pallas_call(
         arrive_kernel,
         out_shape=shape(11, peers, 128),

time: 89.5 us -> 89.7 us (level)
  blocking collectives: 30.1 us -> 16.4 us
  waiting for transfers between devices: 8.1 us -> 17 us
  starting transfers between devices: 18.8 us -> 23.4 us
    all_to_all x1 -> x0, blocking collectives: 13.8 us -> none  [per_device(): lax.all_to_all(moving, 'bulk', split_axis=0, concat_axis=0, tiled=True)]
    all_to_all x0 -> x1, waiting for transfers between devices: none -> 8.89 us  [per_device(): lax.all_to_all(moving, 'bulk', split_axis=0, concat_axis=0, tiled=True)]
    all_to_all x0 -> x1, starting transfers between devices: none -> 4.61 us  [per_device(): lax.all_to_all(moving, 'bulk', split_axis=0, concat_axis=0, tiled=True)]
    pallas_call x1 -> x2, Pallas kernels: 1.68 us -> 2.38 us  [the longest x1 1.65 us: per_device(): pl.pallas_call(update_kernel, out_shape=[shape(count, 8, 128), shape(peer...]
  transfers between devices with their start and end apart: 5 -> 6, of which waited for: 2 -> 3; matrix products, arithmetic and copies ran while one was open for 0% -> 0% of each run, Pallas kernels for 15% -> 16%
where the time goes in v6:
time: 89.7 us; the launch traced here: 89.4 us
  Pallas kernels  29 us (32%)
  starting transfers between devices  23.4 us (26%)
  waiting for transfers between devices  17 us (19%)
  blocking collectives  16.4 us (18%)
  local copies, waits for them, and re-layouts  2.71 us (3%)
    pallas_call x3, Pallas kernels, remote_tiles(): pl.pallas_call(functools.partial(remote_kernel, parts, len(adds), len(ear...  17.4 us
    all_to_all x1, blocking collectives, per_device(): lax.all_to_all(stacked, 'bulk', split_axis=0, concat_axis=0, tiled=True)  16.4 us
    all_to_all x1, starting transfers between devices, per_device(): lax.all_to_all(outgoing, 'bulk', split_axis=0, concat_axis=0, tiled=True)  10.2 us
    all_to_all x1, waiting for transfers between devices, per_device(): lax.all_to_all(moving, 'bulk', split_axis=0, concat_axis=0, tiled=True)  8.89 us
    ppermute x4, starting transfers between devices, from_behind(): lax.ppermute(shard, axis, [(i, (i + by) % peers) for i in range(peers)])  8.64 us
    pallas_call x1, Pallas kernels, local_tiles(): pl.pallas_call(local_kernel, out_shape=[shape(4, count, 128), shape(count...  6.59 us
    all_to_all x1, waiting for transfers between devices, per_device(): lax.all_to_all(outgoing, 'bulk', split_axis=0, concat_axis=0, tiled=True)  5.43 us
    all_to_all x1, starting transfers between devices, per_device(): lax.all_to_all(moving, 'bulk', split_axis=0, concat_axis=0, tiled=True)  4.61 us
  transfers between devices with their start and end apart: 6, of which 3 were waited for; matrix products, arithmetic and copies ran while one was open for 0% of the time, Pallas kernels for 16%

profile of v6, /device:TPU:8, one launch (start us, length us, event | category | flops | bytes accessed | tf_op | source)
XLA Modules:
  0.0 89.4 jit_solution(13520465418052386951)
XLA Ops:
  0.6 2.0 %pack.1 = (f32[32,24,128]{2,1,0:T(8,128)}, f32[64,8,128]{2,1,0:T(8,128)}) custom-call(s32[3,1,32]{2,1,0:T(1,128)} %bitcast.23, s32[1,1,32]{2,1,0:T(1,128)} %bitcast.25, f32[3,64,128]{2,1,0:T(8,128)} %bitcast.36, f32[256,128]{1,0:T(8,128)} %bitcast.19), custom_call_target="tpu_custom_call" | custom-call | tf_op jit(solution)/shard_map/pack/pallas_call | solution.py:464
  2.6 10.2 %all-to-all-start = ((f32[32,24,128]{2,1,0:T(8,128)}), f32[32,24,128]{2,1,0:T(8,128)S(1)}, u32[]{:S(2)}, u32[]{:S(2)}) async-start(f32[32,24,128]{2,1,0:T(8,128)} %get-tuple-element.21), calls=%async_computation | async-start | bytes 786432 | tf_op jit(solution)/shard_map/all_to_all | solution.py:481
  12.8 0.0 copy-start.6
  12.8 1.0 %copy-done.6 = s32[1,64,16,128]{3,2,1,0:T(8,128)S(1)} copy-done((s32[1,64,16,128]{3,2,1,0:T(8,128)S(1)}, s32[1,64,16,128]{3,2,1,0:T(8,128)}, u32[]{:S(2)}) %copy-start.6) | copy-done | bytes 524312
  13.8 0.0 copy-start.7
  13.8 0.9 %copy-done.7 = f32[64,8,128]{2,1,0:T(8,128)S(1)} copy-done((f32[64,8,128]{2,1,0:T(8,128)S(1)}, f32[64,8,128]{2,1,0:T(8,128)}, u32[]{:S(2)}) %copy-start.7) | copy-done | bytes 262168
  14.8 0.0 copy-start.9
  14.8 0.7 copy-done.9
  15.5 0.0 copy-start.5
  15.5 0.0 copy-start.8
  15.5 0.0 copy-start.10
  15.5 6.6 %local_tiles.1 = (f32[4,64,128]{2,1,0:T(8,128)S(1)}, bf16[64,48,128]{2,1,0:T(8,128)(2,1)S(1)}) custom-call(s32[2,64]{1,0:T(2,128)S(1)} %bitcast.31, f32[64,8,128]{2,1,0:T(8,128)S(1)} %copy-done.7, s32[64,16,128]{2,1,0:T(8,128)S(1)} %bitcast.30), custom_call_target="tpu_custom_call" | custom-call | flops 4000000000 | bytes 2097152 | tf_op jit(solution)/shard_map/local_tiles/pallas_call | solution.py:430
  22.1 5.4 %all-to-all-done.rest_0_.early_ref = f32[32,24,128]{2,1,0:T(8,128)S(1)} async-done(((f32[32,24,128]{2,1,0:T(8,128)}), f32[32,24,128]{2,1,0:T(8,128)S(1)}, u32[]{:S(2)}, u32[]{:S(2)}) %all-to-all-start) | async-done | bytes 393248 | tf_op jit(solution)/shard_map/all_to_all | solution.py:481
  27.5 5.7 %collective-permute-start = (f32[32,8,128]{2,1,0:T(8,128)S(1)}, f32[32,8,128]{2,1,0:T(8,128)S(1)}, u32[]{:S(2)}, u32[]{:S(2)}) collective-permute-start(f32[32,8,128]{2,1,0:T(8,128)S(1)} %get-tuple-element.38), channel_id=1, source_target_pairs={{0,480},{32,0},{64,32},{96,64},{128,96},{160,128},{192,160},{224,1... | collective-permute-start | bytes 393224 | tf_op jit(solution)/shard_map/ppermute | solution.py:22
  33.2 0.0 collective-permute-start.1
  33.2 0.0 copy-done.5
  33.2 0.0 copy-done.8
  33.2 0.0 copy-done.10
  33.2 3.4 %remote_tiles.3 = (f32[4,64,128]{2,1,0:T(8,128)S(1)}, f32[16,4,128]{2,1,0:T(4,128)S(1)}) custom-call(s32[2,96]{1,0:T(2,128)S(1)} %bitcast.32, f32[64,8,128]{2,1,0:T(8,128)S(1)} %copy-done.8, bf16[64,48,128]{2,1,0:T(8,128)(2,1)S(1)} %get-tuple-element.23.feature_ref, s32[192,16,128]{2,1,0:T(8,128)S(1)} %bitcast.27, ...), custom_call_target="tpu_custom_call" | custom-call | flops 1600000000 | bytes 2097152 | tf_op jit(solution)/shard_map/remote_tiles/pallas_call | solution.py:409
  36.6 0.0 collective-permute-done.rest_0_
  36.7 2.7 %collective-permute-done.1.rest_1_ = f32[32,8,128]{2,1,0:T(8,128)S(1)} collective-permute-done((f32[32,8,128]{2,1,0:T(8,128)S(1)}, f32[32,8,128]{2,1,0:T(8,128)S(1)}, u32[]{:S(2)}, u32[]{:S(2)}) %collective-permute-start.1) | collective-permute-done | bytes 131104 | tf_op jit(solution)/shard_map/ppermute | solution.py:22
  39.3 10.5 %remote_tiles.4 = (f32[4,64,128]{2,1,0:T(8,128)S(1)}, f32[32,4,128]{2,1,0:T(4,128)S(1)}, f32[32,4,128]{2,1,0:T(4,128)S(1)}) custom-call(s32[2,96]{1,0:T(2,128)S(1)} %bitcast.33, f32[64,8,128]{2,1,0:T(8,128)S(1)} %copy-done.8, bf16[64,48,128]{2,1,0:T(8,128)(2,1)S(1)} %get-tuple-element.23.feature_ref, s32[192,16,128]{2,1,0:T(8,128)S(1)} %bitcast.28, ...), custom_call_target="tpu_custom_call" | custom-call | flops 6400000000 | bytes 2097152 | tf_op jit(solution)/shard_map/remote_tiles/pallas_call | solution.py:409
  49.9 0.0 collective-permute-start.2
  49.9 2.9 %collective-permute-start.3 = (f32[32,4,128]{2,1,0:T(4,128)S(1)}, f32[32,4,128]{2,1,0:T(4,128)S(1)}, u32[]{:S(2)}, u32[]{:S(2)}) collective-permute-start(f32[32,4,128]{2,1,0:T(4,128)S(1)} %get-tuple-element.32), channel_id=1, source_target_pairs={{0,480},{32,0},{64,32},{96,64},{128,96},{160,128},{192,160},{224,1... | collective-permute-start | bytes 196616 | tf_op jit(solution)/shard_map/ppermute | solution.py:22
  52.8 0.0 copy-start
  52.8 0.0 copy-start.1
  52.8 0.0 copy-start.2
  52.8 0.0 copy-start.3
  52.8 0.0 copy-start.4
  52.8 3.5 %remote_tiles.5 = (f32[4,64,128]{2,1,0:T(8,128)S(1)}, f32[32,4,128]{2,1,0:T(4,128)S(1)}) custom-call(s32[2,96]{1,0:T(2,128)S(1)} %bitcast.34, f32[64,8,128]{2,1,0:T(8,128)S(1)} %copy-done.8, bf16[64,48,128]{2,1,0:T(8,128)(2,1)S(1)} %get-tuple-element.23.feature_ref, s32[192,16,128]{2,1,0:T(8,128)S(1)} %bitcast.29, ...), custom_call_target="tpu_custom_call" | custom-call | flops 1600000000 | bytes 2097152 | tf_op jit(solution)/shard_map/remote_tiles/pallas_call | solution.py:409
  56.3 0.0 collective-permute-done.2
  56.3 0.0 collective-permute-done.3
  56.4 16.4 %all_to_all.15.returned_ref = f32[32,3,4,128]{3,2,1,0:T(4,128)S(1)} all-to-all(f32[32,3,4,128]{3,2,1,0:T(4,128)S(1)} %pad_maximum_fusion), channel_id=1, replica_groups=mesh['region'=16,'bulk'=32] {'bulk'}, dimensions={0} | all-to-all | bytes 393216 | tf_op jit(solution)/shard_map/all_to_all | solution.py:501
  72.7 0.0 copy-done
  72.7 0.0 copy-done.1
  72.7 0.0 copy-done.2
  72.7 0.0 copy-done.3
  72.8 0.0 copy-done.4
  72.8 1.6 %update.1 = (f32[64,8,128]{2,1,0:T(8,128)S(1)}, f32[32,8,128]{2,1,0:T(8,128)}) custom-call(s32[3,1,32]{2,1,0:T(1,128)S(1)} %bitcast.24, s32[1,1,32]{2,1,0:T(1,128)S(1)} %bitcast.26, f32[4,64,128]{2,1,0:T(8,128)S(1)} %get-tuple-element.29.totals_ref, f32[32,3,4,128]{3,2,1,0:T(4,128)S(1)} %all_to_all.15.returned_ref, f32[256,128]{1,0:T(8,128)S(1)} %bitcast.20, ...), custom_call_target="tpu_custom_call" | custom-call | tf_op jit(solution)/shard_map/update/pallas_call | solution.py:502
  74.4 4.6 %all-to-all-start.2 = ((f32[32,8,128]{2,1,0:T(8,128)}), f32[32,8,128]{2,1,0:T(8,128)S(1)}, u32[]{:S(2)}, u32[]{:S(2)}) async-start(f32[32,8,128]{2,1,0:T(8,128)} %get-tuple-element.36), calls=%async_computation.2 | async-start | bytes 262144 | tf_op jit(solution)/shard_map/all_to_all | solution.py:511
  79.0 0.7 store.1
  79.8 8.9 %all-to-all-done.2.late_ref = f32[32,8,128]{2,1,0:T(8,128)S(1)} async-done(((f32[32,8,128]{2,1,0:T(8,128)}), f32[32,8,128]{2,1,0:T(8,128)S(1)}, u32[]{:S(2)}, u32[]{:S(2)}) %all-to-all-start.2) | async-done | bytes 131104 | tf_op jit(solution)/shard_map/all_to_all | solution.py:511
  88.6 0.7 arrive.1
  (2 shorter events, 0.1 us)
Async XLA Ops:
  2.6 24.9 %all-to-all-start = ((f32[32,24,128]{2,1,0:T(8,128)}), f32[32,24,128]{2,1,0:T(8,128)S(1)}, u32[]{:S(2)}, u32[]{:S(2)}) async-start(f32[32,24,128]{2,1,0:T(8,128)} %get-tuple-element.21), calls=%async_computation | async-start | bytes 786432 | tf_op jit(solution)/shard_map/all_to_all | solution.py:481
  12.8 1.0 %copy-start.6 = (s32[1,64,16,128]{3,2,1,0:T(8,128)S(1)}, s32[1,64,16,128]{3,2,1,0:T(8,128)}, u32[]{:S(2)}) copy-start(s32[1,64,16,128]{3,2,1,0:T(8,128)} %param.18) | copy-start | bytes 1572868
  13.8 0.9 %copy-start.7 = (f32[64,8,128]{2,1,0:T(8,128)S(1)}, f32[64,8,128]{2,1,0:T(8,128)}, u32[]{:S(2)}) copy-start(f32[64,8,128]{2,1,0:T(8,128)} %get-tuple-element.20.points_ref) | copy-start | bytes 786436
  14.8 0.7 copy-start.9
  15.5 17.7 %copy-start.5 = (s32[1,96,2,16,128]{4,3,2,1,0:T(8,128)S(1)}, s32[1,96,2,16,128]{4,3,2,1,0:T(8,128)}, u32[]{:S(2)}) copy-start(s32[1,96,2,16,128]{4,3,2,1,0:T(8,128)} %param.16) | copy-start | bytes 4718596
  15.5 17.7 %copy-start.8 = (f32[64,8,128]{2,1,0:T(8,128)S(1)}, f32[64,8,128]{2,1,0:T(8,128)}, u32[]{:S(2)}) copy-start(f32[64,8,128]{2,1,0:T(8,128)} %get-tuple-element.20.points_ref) | copy-start | bytes 786436
  15.5 17.7 %copy-start.10 = (s32[1,96,2]{1,2,0:T(2,128)S(1)}, s32[1,96,2]{1,2,0:T(2,128)}, u32[]{:S(2)}) copy-start(s32[1,96,2]{1,2,0:T(2,128)} %param.15) | copy-start | bytes 2308
  27.5 9.1 %collective-permute-start = (f32[32,8,128]{2,1,0:T(8,128)S(1)}, f32[32,8,128]{2,1,0:T(8,128)S(1)}, u32[]{:S(2)}, u32[]{:S(2)}) collective-permute-start(f32[32,8,128]{2,1,0:T(8,128)S(1)} %get-tuple-element.38), channel_id=1, source_target_pairs={{0,480},{32,0},{64,32},{96,64},{128,96},{160,128},{192,160},{224,1... | collective-permute-start | bytes 393224 | tf_op jit(solution)/shard_map/ppermute | solution.py:22
  33.2 6.1 %collective-permute-start.1 = (f32[32,8,128]{2,1,0:T(8,128)S(1)}, f32[32,8,128]{2,1,0:T(8,128)S(1)}, u32[]{:S(2)}, u32[]{:S(2)}) collective-permute-start(f32[32,8,128]{2,1,0:T(8,128)S(1)} %get-tuple-element.37), channel_id=1, source_target_pairs={{0,32},{32,64},{64,96},{96,128},{128,160},{160,192},{192,224},{224... | collective-permute-start | bytes 393224 | tf_op jit(solution)/shard_map/ppermute | solution.py:22
  49.9 6.5 %collective-permute-start.2 = (f32[32,4,128]{2,1,0:T(4,128)S(1)}, f32[32,4,128]{2,1,0:T(4,128)S(1)}, u32[]{:S(2)}, u32[]{:S(2)}) collective-permute-start(f32[32,4,128]{2,1,0:T(4,128)S(1)} %get-tuple-element.30), channel_id=1, source_target_pairs={{0,32},{32,64},{64,96},{96,128},{128,160},{160,192},{192,224},{224... | collective-permute-start | bytes 196616 | tf_op jit(solution)/shard_map/ppermute | solution.py:22
  49.9 6.4 %collective-permute-start.3 = (f32[32,4,128]{2,1,0:T(4,128)S(1)}, f32[32,4,128]{2,1,0:T(4,128)S(1)}, u32[]{:S(2)}, u32[]{:S(2)}) collective-permute-start(f32[32,4,128]{2,1,0:T(4,128)S(1)} %get-tuple-element.32), channel_id=1, source_target_pairs={{0,480},{32,0},{64,32},{96,64},{128,96},{160,128},{192,160},{224,1... | collective-permute-start | bytes 196616 | tf_op jit(solution)/shard_map/ppermute | solution.py:22
  52.8 19.9 %copy-start = (f32[64,4,128]{2,1,0:T(4,128)S(1)}, f32[64,4,128]{2,1,0:T(4,128)}, u32[]{:S(2)}) copy-start(f32[64,4,128]{2,1,0:T(4,128)} %param.11) | copy-start | bytes 393220
  52.8 19.9 %copy-start.1 = (f32[64,3,128]{2,0,1:T(8,128)S(1)}, f32[64,3,128]{2,0,1:T(8,128)}, u32[]{:S(2)}) copy-start(f32[64,3,128]{2,0,1:T(8,128)} %param.13) | copy-start | bytes 294916
  52.8 19.9 %copy-start.2 = (f32[64,128]{1,0:T(8,128)S(1)}, f32[64,128]{1,0:T(8,128)}, u32[]{:S(2)}) copy-start(f32[64,128]{1,0:T(8,128)} %storage_ref.1) | copy-start | bytes 98308
  52.8 19.9 %copy-start.3 = (s32[1,3,32,1]{2,3,1,0:T(1,128)S(1)}, s32[1,3,32,1]{2,3,1,0:T(1,128)}, u32[]{:S(2)}) copy-start(s32[1,3,32,1]{2,3,1,0:T(1,128)} %param.14) | copy-start | bytes 1156
  52.8 19.9 %copy-start.4 = (s32[1,32,1]{1,2,0:T(1,128)S(1)}, s32[1,32,1]{1,2,0:T(1,128)}, u32[]{:S(2)}) copy-start(s32[1,32,1]{1,2,0:T(1,128)} %param.19) | copy-start | bytes 388
  74.4 14.2 %all-to-all-start.2 = ((f32[32,8,128]{2,1,0:T(8,128)}), f32[32,8,128]{2,1,0:T(8,128)S(1)}, u32[]{:S(2)}, u32[]{:S(2)}) async-start(f32[32,8,128]{2,1,0:T(8,128)} %get-tuple-element.36), calls=%async_computation.2 | async-start | bytes 262144 | tf_op jit(solution)/shard_map/all_to_all | solution.py:511

commit v7 on v6

--- a/solution.py
+++ b/solution.py
@@ -484,12 +484,12 @@
     local = remote_local[0].transpose(1, 0)
     mask = remote_mask[0].reshape(-1, remote_mask.shape[3], remote_mask.shape[4])
     tile_args = (local, points, feature, mask)
+    up = from_behind(spread[:, 16:24], "region", 1)
     down = from_behind(spread[:, 0:8], "region", -1)
-    up = from_behind(spread[:, 16:24], "region", 1)
     half = peers // 2
     first_totals, first_back = remote_tiles(((1, 8, 0, half, peers),), *tile_args, [spread])
-    far_totals, down_back, up_back = remote_tiles(
-        ((0, 0, 0, peers, peers), (2, 0, 0, peers, peers)), *tile_args, [down, up]
+    far_totals, up_back, down_back = remote_tiles(
+        ((2, 0, 0, peers, peers), (0, 0, 0, peers, peers)), *tile_args, [up, down]
     )
     down_back = from_behind(down_back, "region", 1)
     up_back = from_behind(up_back, "region", -1)

time: 89.7 us -> 87.7 us (0.978)
  waiting for transfers between devices: 17 us -> 14.3 us
    ppermute x4, waiting for transfers between devices: 2.68 us -> 0.01 us  [from_behind(): lax.ppermute(shard, axis, [(i, (i + by) % peers) for i in range(peers)])]
  transfers between devices with their start and end apart: 6 -> 6, of which waited for: 3 -> 2; matrix products, arithmetic and copies ran while one was open for 0% -> 0% of each run, Pallas kernels for 16% -> 16%
where the time goes in v7:
time: 87.7 us; the launch traced here: 87.3 us
  Pallas kernels  29 us (33%)
  starting transfers between devices  24 us (27%)
  blocking collectives  16.3 us (19%)
  waiting for transfers between devices  14.3 us (16%)
  local copies, waits for them, and re-layouts  2.71 us (3%)
    pallas_call x3, Pallas kernels, remote_tiles(): pl.pallas_call(functools.partial(remote_kernel, parts, len(adds), len(ear...  17.4 us
    all_to_all x1, blocking collectives, per_device(): lax.all_to_all(stacked, 'bulk', split_axis=0, concat_axis=0, tiled=True)  16.3 us
    all_to_all x1, starting transfers between devices, per_device(): lax.all_to_all(outgoing, 'bulk', split_axis=0, concat_axis=0, tiled=True)  10.2 us
    ppermute x4, starting transfers between devices, from_behind(): lax.ppermute(shard, axis, [(i, (i + by) % peers) for i in range(peers)])  9.22 us
    all_to_all x1, waiting for transfers between devices, per_device(): lax.all_to_all(moving, 'bulk', split_axis=0, concat_axis=0, tiled=True)  8.89 us
    pallas_call x1, Pallas kernels, local_tiles(): pl.pallas_call(local_kernel, out_shape=[shape(4, count, 128), shape(count...  6.59 us
    all_to_all x1, waiting for transfers between devices, per_device(): lax.all_to_all(outgoing, 'bulk', split_axis=0, concat_axis=0, tiled=True)  5.43 us
    all_to_all x1, starting transfers between devices, per_device(): lax.all_to_all(moving, 'bulk', split_axis=0, concat_axis=0, tiled=True)  4.61 us
  transfers between devices with their start and end apart: 6, of which 2 were waited for; matrix products, arithmetic and copies ran while one was open for 0% of the time, Pallas kernels for 16%

profile of v7, /device:TPU:8, one launch (start us, length us, event | category | flops | bytes accessed | tf_op | source)
XLA Modules:
  0.0 87.3 jit_solution(10213936385615908314)
XLA Ops:
  0.6 2.0 %pack.1 = (f32[32,24,128]{2,1,0:T(8,128)}, f32[64,8,128]{2,1,0:T(8,128)}) custom-call(s32[3,1,32]{2,1,0:T(1,128)} %bitcast.23, s32[1,1,32]{2,1,0:T(1,128)} %bitcast.25, f32[3,64,128]{2,1,0:T(8,128)} %bitcast.36, f32[256,128]{1,0:T(8,128)} %bitcast.19), custom_call_target="tpu_custom_call" | custom-call | tf_op jit(solution)/shard_map/pack/pallas_call | solution.py:464
  2.6 10.2 %all-to-all-start = ((f32[32,24,128]{2,1,0:T(8,128)}), f32[32,24,128]{2,1,0:T(8,128)S(1)}, u32[]{:S(2)}, u32[]{:S(2)}) async-start(f32[32,24,128]{2,1,0:T(8,128)} %get-tuple-element.21), calls=%async_computation | async-start | bytes 786432 | tf_op jit(solution)/shard_map/all_to_all | solution.py:481
  12.8 0.0 copy-start.6
  12.8 1.0 %copy-done.6 = s32[1,64,16,128]{3,2,1,0:T(8,128)S(1)} copy-done((s32[1,64,16,128]{3,2,1,0:T(8,128)S(1)}, s32[1,64,16,128]{3,2,1,0:T(8,128)}, u32[]{:S(2)}) %copy-start.6) | copy-done | bytes 524312
  13.8 0.0 copy-start.7
  13.8 0.9 %copy-done.7 = f32[64,8,128]{2,1,0:T(8,128)S(1)} copy-done((f32[64,8,128]{2,1,0:T(8,128)S(1)}, f32[64,8,128]{2,1,0:T(8,128)}, u32[]{:S(2)}) %copy-start.7) | copy-done | bytes 262168
  14.8 0.0 copy-start.9
  14.8 0.7 copy-done.9
  15.5 0.0 copy-start.5
  15.5 0.0 copy-start.8
  15.5 0.0 copy-start.10
  15.5 6.6 %local_tiles.1 = (f32[4,64,128]{2,1,0:T(8,128)S(1)}, bf16[64,48,128]{2,1,0:T(8,128)(2,1)S(1)}) custom-call(s32[2,64]{1,0:T(2,128)S(1)} %bitcast.31, f32[64,8,128]{2,1,0:T(8,128)S(1)} %copy-done.7, s32[64,16,128]{2,1,0:T(8,128)S(1)} %bitcast.30), custom_call_target="tpu_custom_call" | custom-call | flops 4000000000 | bytes 2097152 | tf_op jit(solution)/shard_map/local_tiles/pallas_call | solution.py:430
  22.1 5.4 %all-to-all-done.rest_0_.early_ref = f32[32,24,128]{2,1,0:T(8,128)S(1)} async-done(((f32[32,24,128]{2,1,0:T(8,128)}), f32[32,24,128]{2,1,0:T(8,128)S(1)}, u32[]{:S(2)}, u32[]{:S(2)}) %all-to-all-start) | async-done | bytes 393248 | tf_op jit(solution)/shard_map/all_to_all | solution.py:481
  27.5 0.0 collective-permute-start
  27.5 5.7 %collective-permute-start.1 = (f32[32,8,128]{2,1,0:T(8,128)S(1)}, f32[32,8,128]{2,1,0:T(8,128)S(1)}, u32[]{:S(2)}, u32[]{:S(2)}) collective-permute-start(f32[32,8,128]{2,1,0:T(8,128)S(1)} %get-tuple-element.37), channel_id=1, source_target_pairs={{0,480},{32,0},{64,32},{96,64},{128,96},{160,128},{192,160},{224,1... | collective-permute-start | bytes 393224 | tf_op jit(solution)/shard_map/ppermute | solution.py:22
  33.2 0.0 copy-done.5
  33.2 0.0 copy-done.8
  33.2 0.0 copy-done.10
  33.2 3.4 %remote_tiles.3 = (f32[4,64,128]{2,1,0:T(8,128)S(1)}, f32[16,4,128]{2,1,0:T(4,128)S(1)}) custom-call(s32[2,96]{1,0:T(2,128)S(1)} %bitcast.32, f32[64,8,128]{2,1,0:T(8,128)S(1)} %copy-done.8, bf16[64,48,128]{2,1,0:T(8,128)(2,1)S(1)} %get-tuple-element.23.feature_ref, s32[192,16,128]{2,1,0:T(8,128)S(1)} %bitcast.27, ...), custom_call_target="tpu_custom_call" | custom-call | flops 1600000000 | bytes 2097152 | tf_op jit(solution)/shard_map/remote_tiles/pallas_call | solution.py:409
  36.7 0.0 collective-permute-done.rest_0_
  36.7 0.0 collective-permute-done.1.rest_1_
  36.7 10.5 %remote_tiles.4 = (f32[4,64,128]{2,1,0:T(8,128)S(1)}, f32[32,4,128]{2,1,0:T(4,128)S(1)}, f32[32,4,128]{2,1,0:T(4,128)S(1)}) custom-call(s32[2,96]{1,0:T(2,128)S(1)} %bitcast.33, f32[64,8,128]{2,1,0:T(8,128)S(1)} %copy-done.8, bf16[64,48,128]{2,1,0:T(8,128)(2,1)S(1)} %get-tuple-element.23.feature_ref, s32[192,16,128]{2,1,0:T(8,128)S(1)} %bitcast.28, ...), custom_call_target="tpu_custom_call" | custom-call | flops 6400000000 | bytes 2097152 | tf_op jit(solution)/shard_map/remote_tiles/pallas_call | solution.py:409
  47.2 0.0 collective-permute-start.2
  47.2 3.5 %collective-permute-start.3 = (f32[32,4,128]{2,1,0:T(4,128)S(1)}, f32[32,4,128]{2,1,0:T(4,128)S(1)}, u32[]{:S(2)}, u32[]{:S(2)}) collective-permute-start(f32[32,4,128]{2,1,0:T(4,128)S(1)} %get-tuple-element.32), channel_id=1, source_target_pairs={{0,480},{32,0},{64,32},{96,64},{128,96},{160,128},{192,160},{224,1... | collective-permute-start | bytes 196616 | tf_op jit(solution)/shard_map/ppermute | solution.py:22
  50.8 0.0 copy-start
  50.8 0.0 copy-start.1
  50.8 0.0 copy-start.2
  50.8 0.0 copy-start.3
  50.8 0.0 copy-start.4
  50.8 3.4 %remote_tiles.5 = (f32[4,64,128]{2,1,0:T(8,128)S(1)}, f32[32,4,128]{2,1,0:T(4,128)S(1)}) custom-call(s32[2,96]{1,0:T(2,128)S(1)} %bitcast.34, f32[64,8,128]{2,1,0:T(8,128)S(1)} %copy-done.8, bf16[64,48,128]{2,1,0:T(8,128)(2,1)S(1)} %get-tuple-element.23.feature_ref, s32[192,16,128]{2,1,0:T(8,128)S(1)} %bitcast.29, ...), custom_call_target="tpu_custom_call" | custom-call | flops 1600000000 | bytes 2097152 | tf_op jit(solution)/shard_map/remote_tiles/pallas_call | solution.py:409
  54.2 0.0 collective-permute-done.2
  54.2 0.0 collective-permute-done.3
  54.3 16.3 %all_to_all.15.returned_ref = f32[32,3,4,128]{3,2,1,0:T(4,128)S(1)} all-to-all(f32[32,3,4,128]{3,2,1,0:T(4,128)S(1)} %pad_maximum_fusion), channel_id=1, replica_groups=mesh['region'=16,'bulk'=32] {'bulk'}, dimensions={0} | all-to-all | bytes 393216 | tf_op jit(solution)/shard_map/all_to_all | solution.py:501
  70.6 0.0 copy-done
  70.6 0.0 copy-done.1
  70.6 0.0 copy-done.2
  70.6 0.0 copy-done.3
  70.7 0.0 copy-done.4
  70.7 1.6 %update.1 = (f32[64,8,128]{2,1,0:T(8,128)S(1)}, f32[32,8,128]{2,1,0:T(8,128)}) custom-call(s32[3,1,32]{2,1,0:T(1,128)S(1)} %bitcast.24, s32[1,1,32]{2,1,0:T(1,128)S(1)} %bitcast.26, f32[4,64,128]{2,1,0:T(8,128)S(1)} %get-tuple-element.29.totals_ref, f32[32,3,4,128]{3,2,1,0:T(4,128)S(1)} %all_to_all.15.returned_ref, f32[256,128]{1,0:T(8,128)S(1)} %bitcast.20, ...), custom_call_target="tpu_custom_call" | custom-call | tf_op jit(solution)/shard_map/update/pallas_call | solution.py:502
  72.3 4.6 %all-to-all-start.2 = ((f32[32,8,128]{2,1,0:T(8,128)}), f32[32,8,128]{2,1,0:T(8,128)S(1)}, u32[]{:S(2)}, u32[]{:S(2)}) async-start(f32[32,8,128]{2,1,0:T(8,128)} %get-tuple-element.36), calls=%async_computation.2 | async-start | bytes 262144 | tf_op jit(solution)/shard_map/all_to_all | solution.py:511
  76.9 0.7 store.1
  77.7 8.9 %all-to-all-done.2.late_ref = f32[32,8,128]{2,1,0:T(8,128)S(1)} async-done(((f32[32,8,128]{2,1,0:T(8,128)}), f32[32,8,128]{2,1,0:T(8,128)S(1)}, u32[]{:S(2)}, u32[]{:S(2)}) %all-to-all-start.2) | async-done | bytes 131104 | tf_op jit(solution)/shard_map/all_to_all | solution.py:511
  86.5 0.7 arrive.1
  (2 shorter events, 0.1 us)
Async XLA Ops:
  2.6 24.9 %all-to-all-start = ((f32[32,24,128]{2,1,0:T(8,128)}), f32[32,24,128]{2,1,0:T(8,128)S(1)}, u32[]{:S(2)}, u32[]{:S(2)}) async-start(f32[32,24,128]{2,1,0:T(8,128)} %get-tuple-element.21), calls=%async_computation | async-start | bytes 786432 | tf_op jit(solution)/shard_map/all_to_all | solution.py:481
  12.8 1.0 %copy-start.6 = (s32[1,64,16,128]{3,2,1,0:T(8,128)S(1)}, s32[1,64,16,128]{3,2,1,0:T(8,128)}, u32[]{:S(2)}) copy-start(s32[1,64,16,128]{3,2,1,0:T(8,128)} %param.18) | copy-start | bytes 1572868
  13.8 0.9 %copy-start.7 = (f32[64,8,128]{2,1,0:T(8,128)S(1)}, f32[64,8,128]{2,1,0:T(8,128)}, u32[]{:S(2)}) copy-start(f32[64,8,128]{2,1,0:T(8,128)} %get-tuple-element.20.points_ref) | copy-start | bytes 786436
  14.8 0.7 copy-start.9
  15.5 17.8 %copy-start.5 = (s32[1,96,2,16,128]{4,3,2,1,0:T(8,128)S(1)}, s32[1,96,2,16,128]{4,3,2,1,0:T(8,128)}, u32[]{:S(2)}) copy-start(s32[1,96,2,16,128]{4,3,2,1,0:T(8,128)} %param.16) | copy-start | bytes 4718596
  15.5 17.8 %copy-start.8 = (f32[64,8,128]{2,1,0:T(8,128)S(1)}, f32[64,8,128]{2,1,0:T(8,128)}, u32[]{:S(2)}) copy-start(f32[64,8,128]{2,1,0:T(8,128)} %get-tuple-element.20.points_ref) | copy-start | bytes 786436
  15.5 17.8 %copy-start.10 = (s32[1,96,2]{1,2,0:T(2,128)S(1)}, s32[1,96,2]{1,2,0:T(2,128)}, u32[]{:S(2)}) copy-start(s32[1,96,2]{1,2,0:T(2,128)} %param.15) | copy-start | bytes 2308
  27.5 9.1 %collective-permute-start = (f32[32,8,128]{2,1,0:T(8,128)S(1)}, f32[32,8,128]{2,1,0:T(8,128)S(1)}, u32[]{:S(2)}, u32[]{:S(2)}) collective-permute-start(f32[32,8,128]{2,1,0:T(8,128)S(1)} %get-tuple-element.38), channel_id=1, source_target_pairs={{0,32},{32,64},{64,96},{96,128},{128,160},{160,192},{192,224},{224... | collective-permute-start | bytes 393224 | tf_op jit(solution)/shard_map/ppermute | solution.py:22
  27.5 9.1 %collective-permute-start.1 = (f32[32,8,128]{2,1,0:T(8,128)S(1)}, f32[32,8,128]{2,1,0:T(8,128)S(1)}, u32[]{:S(2)}, u32[]{:S(2)}) collective-permute-start(f32[32,8,128]{2,1,0:T(8,128)S(1)} %get-tuple-element.37), channel_id=1, source_target_pairs={{0,480},{32,0},{64,32},{96,64},{128,96},{160,128},{192,160},{224,1... | collective-permute-start | bytes 393224 | tf_op jit(solution)/shard_map/ppermute | solution.py:22
  47.2 7.0 %collective-permute-start.2 = (f32[32,4,128]{2,1,0:T(4,128)S(1)}, f32[32,4,128]{2,1,0:T(4,128)S(1)}, u32[]{:S(2)}, u32[]{:S(2)}) collective-permute-start(f32[32,4,128]{2,1,0:T(4,128)S(1)} %get-tuple-element.30), channel_id=1, source_target_pairs={{0,32},{32,64},{64,96},{96,128},{128,160},{160,192},{192,224},{224... | collective-permute-start | bytes 196616 | tf_op jit(solution)/shard_map/ppermute | solution.py:22
  47.2 7.0 %collective-permute-start.3 = (f32[32,4,128]{2,1,0:T(4,128)S(1)}, f32[32,4,128]{2,1,0:T(4,128)S(1)}, u32[]{:S(2)}, u32[]{:S(2)}) collective-permute-start(f32[32,4,128]{2,1,0:T(4,128)S(1)} %get-tuple-element.32), channel_id=1, source_target_pairs={{0,480},{32,0},{64,32},{96,64},{128,96},{160,128},{192,160},{224,1... | collective-permute-start | bytes 196616 | tf_op jit(solution)/shard_map/ppermute | solution.py:22
  50.8 19.9 %copy-start = (f32[64,4,128]{2,1,0:T(4,128)S(1)}, f32[64,4,128]{2,1,0:T(4,128)}, u32[]{:S(2)}) copy-start(f32[64,4,128]{2,1,0:T(4,128)} %param.11) | copy-start | bytes 393220
  50.8 19.9 %copy-start.1 = (f32[64,3,128]{2,0,1:T(8,128)S(1)}, f32[64,3,128]{2,0,1:T(8,128)}, u32[]{:S(2)}) copy-start(f32[64,3,128]{2,0,1:T(8,128)} %param.13) | copy-start | bytes 294916
  50.8 19.9 %copy-start.2 = (f32[64,128]{1,0:T(8,128)S(1)}, f32[64,128]{1,0:T(8,128)}, u32[]{:S(2)}) copy-start(f32[64,128]{1,0:T(8,128)} %storage_ref.1) | copy-start | bytes 98308
  50.8 19.9 %copy-start.3 = (s32[1,3,32,1]{2,3,1,0:T(1,128)S(1)}, s32[1,3,32,1]{2,3,1,0:T(1,128)}, u32[]{:S(2)}) copy-start(s32[1,3,32,1]{2,3,1,0:T(1,128)} %param.14) | copy-start | bytes 1156
  50.8 19.9 %copy-start.4 = (s32[1,32,1]{1,2,0:T(1,128)S(1)}, s32[1,32,1]{1,2,0:T(1,128)}, u32[]{:S(2)}) copy-start(s32[1,32,1]{1,2,0:T(1,128)} %param.19) | copy-start | bytes 388
  72.3 14.2 %all-to-all-start.2 = ((f32[32,8,128]{2,1,0:T(8,128)}), f32[32,8,128]{2,1,0:T(8,128)S(1)}, u32[]{:S(2)}, u32[]{:S(2)}) async-start(f32[32,8,128]{2,1,0:T(8,128)} %get-tuple-element.36), calls=%async_computation.2 | async-start | bytes 262144 | tf_op jit(solution)/shard_map/all_to_all | solution.py:511

commit v8 on v5

--- a/solution.py
+++ b/solution.py
@@ -187,8 +187,8 @@
 
 
 def pack_kernel(
-    sends_any, moves_any, positions_any, fields_any, out_ref, points_ref,
-    sends_ref, moves_ref, positions_ref, fields_ref, sems,
+    sends_any, moves_any, positions_any, fields_any, out_any, points_any,
+    sends_ref, moves_ref, positions_ref, fields_ref, out_ref, points_ref, sems,
 ):
     pairs = (
         (positions_any, positions_ref),
@@ -204,6 +204,8 @@
         flat[pl.ds(4 + k, count, stride=8), :] = block_rows(fields_ref, k, count, 4)
     flat[pl.ds(3, count, stride=8), :] = block_rows(fields_ref, 3, count, 4)
     flat[pl.ds(7, count, stride=8), :] = jnp.zeros((count, 128), f32)
+    away = [pltpu.make_async_copy(points_ref, points_any, sems.at[4])]
+    away[0].start()
     last = lax.broadcasted_iota(jnp.int32, (8, 128), 0) == 7
 
     def one_peer(peer, carry):
@@ -215,7 +217,14 @@
             out_ref[peer, 8 * o : 8 * o + 8] = jnp.where(last, moved[o : o + 1], block)
         return carry
 
-    lax.fori_loop(0, out_ref.shape[0], one_peer, 0, unroll=8)
+    peers = out_ref.shape[0]
+    for n in range(4):
+        low, high = n * peers // 4, (n + 1) * peers // 4
+        lax.fori_loop(low, high, one_peer, 0, unroll=True)
+        away.append(pltpu.make_async_copy(out_ref.at[low:high], out_any.at[low:high], sems.at[5 + n]))
+        away[-1].start()
+    for copy in away:
+        copy.wait()
 
 
 def local_kernel(
@@ -318,7 +327,7 @@
             sums_ref[sends_ref[o, 0, peer]] += returned_ref[peer, o]
         return carry
 
-    lax.fori_loop(0, peers, one_peer, 0, unroll=8)
+    lax.fori_loop(0, peers, one_peer, 0, unroll=True)
     flats = [sums_ref.reshape(count * 4, 128) for sums_ref in sums_refs]
 
     def total(k):
@@ -348,7 +357,7 @@
         moving_ref[peer] = jnp.where(move >= 0, block, jnp.zeros_like(block))
         return carry
 
-    lax.fori_loop(0, peers, one_move, 0, unroll=4)
+    lax.fori_loop(0, peers, one_move, 0, unroll=True)
 
 
 def arrive_kernel(late_ref, early_ref, out_ref):
@@ -450,13 +459,15 @@
         pack_kernel,
         out_shape=[shape(peers, 24, 128), shape(count, 8, 128)],
         in_specs=[anywhere()] * 4,
-        out_specs=[in_vmem()] * 2,
+        out_specs=[anywhere()] * 2,
         scratch_shapes=[
             pltpu.SMEM(sends.shape, jnp.int32),
             pltpu.SMEM(moves.shape, jnp.int32),
             pltpu.VMEM(rows_first.shape, f32),
             pltpu.VMEM(flat_fields.shape, f32),
-            pltpu.SemaphoreType.DMA((4,)),
+            pltpu.VMEM((peers, 24, 128), f32),
+            pltpu.VMEM((count, 8, 128), f32),
+            pltpu.SemaphoreType.DMA((9,)),
         ],
         compiler_params=pltpu.CompilerParams(vmem_limit_bytes=60 * 1024 * 1024),
         name="pack",
@@ -467,12 +478,12 @@
     local = remote_local[0].transpose(1, 0)
     mask = remote_mask[0].reshape(-1, remote_mask.shape[3], remote_mask.shape[4])
     tile_args = (local, points, feature, mask)
+    up = from_behind(spread[:, 16:24], "region", 1)
     down = from_behind(spread[:, 0:8], "region", -1)
-    up = from_behind(spread[:, 16:24], "region", 1)
     half = peers // 2
     first_totals, first_back = remote_tiles(((1, 8, 0, half, peers),), *tile_args, [spread])
-    far_totals, down_back, up_back = remote_tiles(
-        ((0, 0, 0, peers, peers), (2, 0, 0, peers, peers)), *tile_args, [down, up]
+    far_totals, up_back, down_back = remote_tiles(
+        ((2, 0, 0, peers, peers), (0, 0, 0, peers, peers)), *tile_args, [up, down]
     )
     down_back = from_behind(down_back, "region", 1)
     up_back = from_behind(up_back, "region", -1)

time: 89.5 us -> 87.2 us (0.974)
  waiting for transfers between devices: 8.1 us -> 5.44 us
    ppermute x4, waiting for transfers between devices: 2.68 us -> 0.01 us  [from_behind(): lax.ppermute(shard, axis, [(i, (i + by) % peers) for i in range(peers)])]
  transfers between devices with their start and end apart: 5 -> 5, of which waited for: 2 -> 1; matrix products, arithmetic and copies ran while one was open for 0% -> 0% of each run, Pallas kernels for 15% -> 16%
where the time goes in v8:
time: 87.2 us; the launch traced here: 86.8 us
  blocking collectives  30.1 us (35%)
  Pallas kernels  28.3 us (32%)
  starting transfers between devices  19.4 us (22%)
  waiting for transfers between devices  5.44 us (6%)
  local copies, waits for them, and re-layouts  2.71 us (3%)
    pallas_call x3, Pallas kernels, remote_tiles(): pl.pallas_call(functools.partial(remote_kernel, parts, len(adds), len(ear...  17.4 us
    all_to_all x1, blocking collectives, per_device(): lax.all_to_all(stacked, 'bulk', split_axis=0, concat_axis=0, tiled=True)  16.3 us
    all_to_all x1, blocking collectives, per_device(): lax.all_to_all(moving, 'bulk', split_axis=0, concat_axis=0, tiled=True)  13.8 us
    all_to_all x1, starting transfers between devices, per_device(): lax.all_to_all(outgoing, 'bulk', split_axis=0, concat_axis=0, tiled=True)  10.2 us
    ppermute x4, starting transfers between devices, from_behind(): lax.ppermute(shard, axis, [(i, (i + by) % peers) for i in range(peers)])  9.22 us
    pallas_call x1, Pallas kernels, local_tiles(): pl.pallas_call(local_kernel, out_shape=[shape(4, count, 128), shape(count...  6.59 us
    all_to_all x1, waiting for transfers between devices, per_device(): lax.all_to_all(outgoing, 'bulk', split_axis=0, concat_axis=0, tiled=True)  5.43 us
    unnamed x22, local copies, waits for them, and re-layouts  2.7 us
  transfers between devices with their start and end apart: 5, of which 1 were waited for; matrix products, arithmetic and copies ran while one was open for 0% of the time, Pallas kernels for 16%

profile of v8, /device:TPU:8, one launch (start us, length us, event | category | flops | bytes accessed | tf_op | source)
XLA Modules:
  0.0 86.8 jit_solution(3214339939057887781)
XLA Ops:
  0.6 2.0 %pack.1 = (f32[32,24,128]{2,1,0:T(8,128)}, f32[64,8,128]{2,1,0:T(8,128)}) custom-call(s32[3,1,32]{2,1,0:T(1,128)} %bitcast.23, s32[1,1,32]{2,1,0:T(1,128)} %bitcast.25, f32[3,64,128]{2,1,0:T(8,128)} %bitcast.36, f32[256,128]{1,0:T(8,128)} %bitcast.19), custom_call_target="tpu_custom_call" | custom-call | tf_op jit(solution)/shard_map/pack/pallas_call | solution.py:458
  2.6 10.2 %all-to-all-start = ((f32[32,24,128]{2,1,0:T(8,128)}), f32[32,24,128]{2,1,0:T(8,128)S(1)}, u32[]{:S(2)}, u32[]{:S(2)}) async-start(f32[32,24,128]{2,1,0:T(8,128)} %get-tuple-element.20), calls=%async_computation | async-start | bytes 786432 | tf_op jit(solution)/shard_map/all_to_all | solution.py:475
  12.8 0.0 copy-start.6
  12.8 1.0 %copy-done.6 = s32[1,64,16,128]{3,2,1,0:T(8,128)S(1)} copy-done((s32[1,64,16,128]{3,2,1,0:T(8,128)S(1)}, s32[1,64,16,128]{3,2,1,0:T(8,128)}, u32[]{:S(2)}) %copy-start.6) | copy-done | bytes 524312
  13.9 0.0 copy-start.7
  13.9 0.9 %copy-done.7 = f32[64,8,128]{2,1,0:T(8,128)S(1)} copy-done((f32[64,8,128]{2,1,0:T(8,128)S(1)}, f32[64,8,128]{2,1,0:T(8,128)}, u32[]{:S(2)}) %copy-start.7) | copy-done | bytes 262168
  14.8 0.0 copy-start.9
  14.8 0.7 copy-done.9
  15.5 0.0 copy-start.5
  15.5 0.0 copy-start.8
  15.5 0.0 copy-start.10
  15.5 6.6 %local_tiles.1 = (f32[4,64,128]{2,1,0:T(8,128)S(1)}, bf16[64,48,128]{2,1,0:T(8,128)(2,1)S(1)}) custom-call(s32[2,64]{1,0:T(2,128)S(1)} %bitcast.31, f32[64,8,128]{2,1,0:T(8,128)S(1)} %copy-done.7, s32[64,16,128]{2,1,0:T(8,128)S(1)} %bitcast.30), custom_call_target="tpu_custom_call" | custom-call | flops 4000000000 | bytes 2097152 | tf_op jit(solution)/shard_map/local_tiles/pallas_call | solution.py:424
  22.1 5.4 %all-to-all-done.rest_0_.early_ref = f32[32,24,128]{2,1,0:T(8,128)S(1)} async-done(((f32[32,24,128]{2,1,0:T(8,128)}), f32[32,24,128]{2,1,0:T(8,128)S(1)}, u32[]{:S(2)}, u32[]{:S(2)}) %all-to-all-start) | async-done | bytes 393248 | tf_op jit(solution)/shard_map/all_to_all | solution.py:475
  27.5 0.0 collective-permute-start
  27.6 5.7 %collective-permute-start.1 = (f32[32,8,128]{2,1,0:T(8,128)S(1)}, f32[32,8,128]{2,1,0:T(8,128)S(1)}, u32[]{:S(2)}, u32[]{:S(2)}) collective-permute-start(f32[32,8,128]{2,1,0:T(8,128)S(1)} %get-tuple-element.35), channel_id=1, source_target_pairs={{0,480},{32,0},{64,32},{96,64},{128,96},{160,128},{192,160},{224,1... | collective-permute-start | bytes 393224 | tf_op jit(solution)/shard_map/ppermute | solution.py:22
  33.2 0.0 copy-done.5
  33.2 0.0 copy-done.8
  33.3 0.0 copy-done.10
  33.3 3.4 %remote_tiles.3 = (f32[4,64,128]{2,1,0:T(8,128)S(1)}, f32[16,4,128]{2,1,0:T(4,128)S(1)}) custom-call(s32[2,96]{1,0:T(2,128)S(1)} %bitcast.32, f32[64,8,128]{2,1,0:T(8,128)S(1)} %copy-done.8, bf16[64,48,128]{2,1,0:T(8,128)(2,1)S(1)} %get-tuple-element.22.feature_ref, s32[192,16,128]{2,1,0:T(8,128)S(1)} %bitcast.27, ...), custom_call_target="tpu_custom_call" | custom-call | flops 1600000000 | bytes 2097152 | tf_op jit(solution)/shard_map/remote_tiles/pallas_call | solution.py:403
  36.7 0.0 collective-permute-done.rest_0_
  36.7 0.0 collective-permute-done.1.rest_1_
  36.7 10.5 %remote_tiles.4 = (f32[4,64,128]{2,1,0:T(8,128)S(1)}, f32[32,4,128]{2,1,0:T(4,128)S(1)}, f32[32,4,128]{2,1,0:T(4,128)S(1)}) custom-call(s32[2,96]{1,0:T(2,128)S(1)} %bitcast.33, f32[64,8,128]{2,1,0:T(8,128)S(1)} %copy-done.8, bf16[64,48,128]{2,1,0:T(8,128)(2,1)S(1)} %get-tuple-element.22.feature_ref, s32[192,16,128]{2,1,0:T(8,128)S(1)} %bitcast.28, ...), custom_call_target="tpu_custom_call" | custom-call | flops 6400000000 | bytes 2097152 | tf_op jit(solution)/shard_map/remote_tiles/pallas_call | solution.py:403
  47.2 0.0 collective-permute-start.2
  47.3 3.5 %collective-permute-start.3 = (f32[32,4,128]{2,1,0:T(4,128)S(1)}, f32[32,4,128]{2,1,0:T(4,128)S(1)}, u32[]{:S(2)}, u32[]{:S(2)}) collective-permute-start(f32[32,4,128]{2,1,0:T(4,128)S(1)} %get-tuple-element.31), channel_id=1, source_target_pairs={{0,480},{32,0},{64,32},{96,64},{128,96},{160,128},{192,160},{224,1... | collective-permute-start | bytes 196616 | tf_op jit(solution)/shard_map/ppermute | solution.py:22
  50.8 0.0 copy-start
  50.8 0.0 copy-start.1
  50.8 0.0 copy-start.2
  50.8 0.0 copy-start.3
  50.8 0.0 copy-start.4
  50.8 3.5 %remote_tiles.5 = (f32[4,64,128]{2,1,0:T(8,128)S(1)}, f32[32,4,128]{2,1,0:T(4,128)S(1)}) custom-call(s32[2,96]{1,0:T(2,128)S(1)} %bitcast.34, f32[64,8,128]{2,1,0:T(8,128)S(1)} %copy-done.8, bf16[64,48,128]{2,1,0:T(8,128)(2,1)S(1)} %get-tuple-element.22.feature_ref, s32[192,16,128]{2,1,0:T(8,128)S(1)} %bitcast.29, ...), custom_call_target="tpu_custom_call" | custom-call | flops 1600000000 | bytes 2097152 | tf_op jit(solution)/shard_map/remote_tiles/pallas_call | solution.py:403
  54.3 0.0 collective-permute-done.2
  54.3 0.0 collective-permute-done.3
  54.3 16.3 %all_to_all.15.returned_ref = f32[32,3,4,128]{3,2,1,0:T(4,128)S(1)} all-to-all(f32[32,3,4,128]{3,2,1,0:T(4,128)S(1)} %pad_maximum_fusion), channel_id=1, replica_groups=mesh['region'=16,'bulk'=32] {'bulk'}, dimensions={0} | all-to-all | bytes 393216 | tf_op jit(solution)/shard_map/all_to_all | solution.py:495
  70.7 0.0 copy-done
  70.7 0.0 copy-done.1
  70.7 0.0 copy-done.2
  70.7 0.0 copy-done.3
  70.7 0.0 copy-done.4
  70.7 1.6 %update.1 = (f32[256,128]{1,0:T(8,128)}, f32[3,64,128]{2,1,0:T(8,128)}, f32[32,8,128]{2,1,0:T(8,128)S(1)}) custom-call(s32[3,1,32]{2,1,0:T(1,128)S(1)} %bitcast.24, s32[1,1,32]{2,1,0:T(1,128)S(1)} %bitcast.26, f32[4,64,128]{2,1,0:T(8,128)S(1)} %get-tuple-element.28.totals_ref, f32[32,3,4,128]{3,2,1,0:T(4,128)S(1)} %all_to_all.15.returned_ref, ...), custom_call_target="tpu_custom_call" | custom-call | tf_op jit(solution)/shard_map/update/pallas_call | solution.py:496
  72.3 13.8 %all_to_all.16.late_ref = f32[32,8,128]{2,1,0:T(8,128)S(1)} all-to-all(f32[32,8,128]{2,1,0:T(8,128)S(1)} %get-tuple-element.34), channel_id=1, replica_groups=mesh['region'=16,'bulk'=32] {'bulk'}, dimensions={0} | all-to-all | bytes 262144 | tf_op jit(solution)/shard_map/all_to_all | solution.py:505
  86.1 0.7 arrive.1
  (2 shorter events, 0.1 us)
Async XLA Ops:
  2.6 24.9 %all-to-all-start = ((f32[32,24,128]{2,1,0:T(8,128)}), f32[32,24,128]{2,1,0:T(8,128)S(1)}, u32[]{:S(2)}, u32[]{:S(2)}) async-start(f32[32,24,128]{2,1,0:T(8,128)} %get-tuple-element.20), calls=%async_computation | async-start | bytes 786432 | tf_op jit(solution)/shard_map/all_to_all | solution.py:475
  12.8 1.0 %copy-start.6 = (s32[1,64,16,128]{3,2,1,0:T(8,128)S(1)}, s32[1,64,16,128]{3,2,1,0:T(8,128)}, u32[]{:S(2)}) copy-start(s32[1,64,16,128]{3,2,1,0:T(8,128)} %param.18) | copy-start | bytes 1572868
  13.9 0.9 %copy-start.7 = (f32[64,8,128]{2,1,0:T(8,128)S(1)}, f32[64,8,128]{2,1,0:T(8,128)}, u32[]{:S(2)}) copy-start(f32[64,8,128]{2,1,0:T(8,128)} %get-tuple-element.19.points_ref) | copy-start | bytes 786436
  14.8 0.7 copy-start.9
  15.5 17.8 %copy-start.5 = (s32[1,96,2,16,128]{4,3,2,1,0:T(8,128)S(1)}, s32[1,96,2,16,128]{4,3,2,1,0:T(8,128)}, u32[]{:S(2)}) copy-start(s32[1,96,2,16,128]{4,3,2,1,0:T(8,128)} %param.16) | copy-start | bytes 4718596
  15.5 17.8 %copy-start.8 = (f32[64,8,128]{2,1,0:T(8,128)S(1)}, f32[64,8,128]{2,1,0:T(8,128)}, u32[]{:S(2)}) copy-start(f32[64,8,128]{2,1,0:T(8,128)} %get-tuple-element.19.points_ref) | copy-start | bytes 786436
  15.5 17.8 %copy-start.10 = (s32[1,96,2]{1,2,0:T(2,128)S(1)}, s32[1,96,2]{1,2,0:T(2,128)}, u32[]{:S(2)}) copy-start(s32[1,96,2]{1,2,0:T(2,128)} %param.15) | copy-start | bytes 2308
  27.5 9.1 %collective-permute-start = (f32[32,8,128]{2,1,0:T(8,128)S(1)}, f32[32,8,128]{2,1,0:T(8,128)S(1)}, u32[]{:S(2)}, u32[]{:S(2)}) collective-permute-start(f32[32,8,128]{2,1,0:T(8,128)S(1)} %get-tuple-element.36), channel_id=1, source_target_pairs={{0,32},{32,64},{64,96},{96,128},{128,160},{160,192},{192,224},{224... | collective-permute-start | bytes 393224 | tf_op jit(solution)/shard_map/ppermute | solution.py:22
  27.6 9.1 %collective-permute-start.1 = (f32[32,8,128]{2,1,0:T(8,128)S(1)}, f32[32,8,128]{2,1,0:T(8,128)S(1)}, u32[]{:S(2)}, u32[]{:S(2)}) collective-permute-start(f32[32,8,128]{2,1,0:T(8,128)S(1)} %get-tuple-element.35), channel_id=1, source_target_pairs={{0,480},{32,0},{64,32},{96,64},{128,96},{160,128},{192,160},{224,1... | collective-permute-start | bytes 393224 | tf_op jit(solution)/shard_map/ppermute | solution.py:22
  47.2 7.0 %collective-permute-start.2 = (f32[32,4,128]{2,1,0:T(4,128)S(1)}, f32[32,4,128]{2,1,0:T(4,128)S(1)}, u32[]{:S(2)}, u32[]{:S(2)}) collective-permute-start(f32[32,4,128]{2,1,0:T(4,128)S(1)} %get-tuple-element.29), channel_id=1, source_target_pairs={{0,32},{32,64},{64,96},{96,128},{128,160},{160,192},{192,224},{224... | collective-permute-start | bytes 196616 | tf_op jit(solution)/shard_map/ppermute | solution.py:22
  47.3 7.0 %collective-permute-start.3 = (f32[32,4,128]{2,1,0:T(4,128)S(1)}, f32[32,4,128]{2,1,0:T(4,128)S(1)}, u32[]{:S(2)}, u32[]{:S(2)}) collective-permute-start(f32[32,4,128]{2,1,0:T(4,128)S(1)} %get-tuple-element.31), channel_id=1, source_target_pairs={{0,480},{32,0},{64,32},{96,64},{128,96},{160,128},{192,160},{224,1... | collective-permute-start | bytes 196616 | tf_op jit(solution)/shard_map/ppermute | solution.py:22
  50.8 19.9 %copy-start = (f32[64,4,128]{2,1,0:T(4,128)S(1)}, f32[64,4,128]{2,1,0:T(4,128)}, u32[]{:S(2)}) copy-start(f32[64,4,128]{2,1,0:T(4,128)} %param.11) | copy-start | bytes 393220
  50.8 19.9 %copy-start.1 = (f32[64,3,128]{2,0,1:T(8,128)S(1)}, f32[64,3,128]{2,0,1:T(8,128)}, u32[]{:S(2)}) copy-start(f32[64,3,128]{2,0,1:T(8,128)} %param.13) | copy-start | bytes 294916
  50.8 19.9 %copy-start.2 = (f32[64,128]{1,0:T(8,128)S(1)}, f32[64,128]{1,0:T(8,128)}, u32[]{:S(2)}) copy-start(f32[64,128]{1,0:T(8,128)} %storage_ref.1) | copy-start | bytes 98308
  50.8 19.9 %copy-start.3 = (s32[1,3,32,1]{2,3,1,0:T(1,128)S(1)}, s32[1,3,32,1]{2,3,1,0:T(1,128)}, u32[]{:S(2)}) copy-start(s32[1,3,32,1]{2,3,1,0:T(1,128)} %param.14) | copy-start | bytes 1156
  50.8 19.9 %copy-start.4 = (s32[1,32,1]{1,2,0:T(1,128)S(1)}, s32[1,32,1]{1,2,0:T(1,128)}, u32[]{:S(2)}) copy-start(s32[1,32,1]{1,2,0:T(1,128)} %param.19) | copy-start | bytes 388

commit v9 on v8

--- a/solution.py
+++ b/solution.py
@@ -242,7 +242,7 @@
     lax.fori_loop(0, count, one_block, 0, unroll=8)
 
     def words_of(slot, e):
-        return jnp.concatenate([mask_ref[slot, pl.ds(j, 8, stride=0), :] for j in range(16)], axis=0)
+        return jnp.broadcast_to(mask_ref[slot][:, None, :], (16, 8, 128)).reshape(128, 128)
 
     def store_other(slot, on_other):
         sums_ref[pairs_ref[1, slot]] += on_other
@@ -284,7 +284,7 @@
 
     def words_of(slot, e):
         tile = 2 * entry(slot) + e
-        return jnp.concatenate([mask_ref[tile, pl.ds(j, 8, stride=0), :] for j in range(16)], axis=0)
+        return jnp.broadcast_to(mask_ref[tile][:, None, :], (16, 8, 128)).reshape(128, 128)
 
     def store_other(slot, on_other):
         other_sums[slot] = on_other

time: 87.2 us -> 87.6 us (level)
  no operation moved by 1% of the time
where the time goes in v9:
time: 87.6 us; the launch traced here: 87.3 us
  blocking collectives  30.1 us (34%)
  Pallas kernels  28.8 us (33%)
  starting transfers between devices  19.4 us (22%)
  waiting for transfers between devices  5.42 us (6%)
  local copies, waits for them, and re-layouts  2.71 us (3%)
    pallas_call x3, Pallas kernels, remote_tiles(): pl.pallas_call(functools.partial(remote_kernel, parts, len(adds), len(ear...  17.9 us
    all_to_all x1, blocking collectives, per_device(): lax.all_to_all(stacked, 'bulk', split_axis=0, concat_axis=0, tiled=True)  16.4 us
    all_to_all x1, blocking collectives, per_device(): lax.all_to_all(moving, 'bulk', split_axis=0, concat_axis=0, tiled=True)  13.8 us
    all_to_all x1, starting transfers between devices, per_device(): lax.all_to_all(outgoing, 'bulk', split_axis=0, concat_axis=0, tiled=True)  10.2 us
    ppermute x4, starting transfers between devices, from_behind(): lax.ppermute(shard, axis, [(i, (i + by) % peers) for i in range(peers)])  9.21 us
    pallas_call x1, Pallas kernels, local_tiles(): pl.pallas_call(local_kernel, out_shape=[shape(4, count, 128), shape(count...  6.62 us
    all_to_all x1, waiting for transfers between devices, per_device(): lax.all_to_all(outgoing, 'bulk', split_axis=0, concat_axis=0, tiled=True)  5.4 us
    unnamed x22, local copies, waits for them, and re-layouts  2.7 us
  transfers between devices with their start and end apart: 5, of which 1 were waited for; matrix products, arithmetic and copies ran while one was open for 0% of the time, Pallas kernels for 16%

profile of v9, /device:TPU:8, one launch (start us, length us, event | category | flops | bytes accessed | tf_op | source)
XLA Modules:
  0.0 87.3 jit_solution(15245133843903071937)
XLA Ops:
  0.6 2.0 %pack.1 = (f32[32,24,128]{2,1,0:T(8,128)}, f32[64,8,128]{2,1,0:T(8,128)}) custom-call(s32[3,1,32]{2,1,0:T(1,128)} %bitcast.23, s32[1,1,32]{2,1,0:T(1,128)} %bitcast.25, f32[3,64,128]{2,1,0:T(8,128)} %bitcast.36, f32[256,128]{1,0:T(8,128)} %bitcast.19), custom_call_target="tpu_custom_call" | custom-call | tf_op jit(solution)/shard_map/pack/pallas_call | solution.py:458
  2.6 10.2 %all-to-all-start = ((f32[32,24,128]{2,1,0:T(8,128)}), f32[32,24,128]{2,1,0:T(8,128)S(1)}, u32[]{:S(2)}, u32[]{:S(2)}) async-start(f32[32,24,128]{2,1,0:T(8,128)} %get-tuple-element.20), calls=%async_computation | async-start | bytes 786432 | tf_op jit(solution)/shard_map/all_to_all | solution.py:475
  12.8 0.0 copy-start.6
  12.8 1.0 %copy-done.6 = s32[1,64,16,128]{3,2,1,0:T(8,128)S(1)} copy-done((s32[1,64,16,128]{3,2,1,0:T(8,128)S(1)}, s32[1,64,16,128]{3,2,1,0:T(8,128)}, u32[]{:S(2)}) %copy-start.6) | copy-done | bytes 524312
  13.9 0.0 copy-start.7
  13.9 0.9 %copy-done.7 = f32[64,8,128]{2,1,0:T(8,128)S(1)} copy-done((f32[64,8,128]{2,1,0:T(8,128)S(1)}, f32[64,8,128]{2,1,0:T(8,128)}, u32[]{:S(2)}) %copy-start.7) | copy-done | bytes 262168
  14.8 0.0 copy-start.9
  14.8 0.7 copy-done.9
  15.5 0.0 copy-start.5
  15.5 0.0 copy-start.8
  15.5 0.0 copy-start.10
  15.5 6.6 %local_tiles.1 = (f32[4,64,128]{2,1,0:T(8,128)S(1)}, bf16[64,48,128]{2,1,0:T(8,128)(2,1)S(1)}) custom-call(s32[2,64]{1,0:T(2,128)S(1)} %bitcast.31, f32[64,8,128]{2,1,0:T(8,128)S(1)} %copy-done.7, s32[64,16,128]{2,1,0:T(8,128)S(1)} %bitcast.30), custom_call_target="tpu_custom_call" | custom-call | flops 4000000000 | bytes 2097152 | tf_op jit(solution)/shard_map/local_tiles/pallas_call | solution.py:424
  22.1 5.4 %all-to-all-done.rest_0_.early_ref = f32[32,24,128]{2,1,0:T(8,128)S(1)} async-done(((f32[32,24,128]{2,1,0:T(8,128)}), f32[32,24,128]{2,1,0:T(8,128)S(1)}, u32[]{:S(2)}, u32[]{:S(2)}) %all-to-all-start) | async-done | bytes 393248 | tf_op jit(solution)/shard_map/all_to_all | solution.py:475
  27.5 0.0 collective-permute-start
  27.6 5.7 %collective-permute-start.1 = (f32[32,8,128]{2,1,0:T(8,128)S(1)}, f32[32,8,128]{2,1,0:T(8,128)S(1)}, u32[]{:S(2)}, u32[]{:S(2)}) collective-permute-start(f32[32,8,128]{2,1,0:T(8,128)S(1)} %get-tuple-element.35), channel_id=1, source_target_pairs={{0,480},{32,0},{64,32},{96,64},{128,96},{160,128},{192,160},{224,1... | collective-permute-start | bytes 393224 | tf_op jit(solution)/shard_map/ppermute | solution.py:22
  33.2 0.0 copy-done.5
  33.2 0.0 copy-done.8
  33.3 0.0 copy-done.10
  33.3 3.5 %remote_tiles.3 = (f32[4,64,128]{2,1,0:T(8,128)S(1)}, f32[16,4,128]{2,1,0:T(4,128)S(1)}) custom-call(s32[2,96]{1,0:T(2,128)S(1)} %bitcast.32, f32[64,8,128]{2,1,0:T(8,128)S(1)} %copy-done.8, bf16[64,48,128]{2,1,0:T(8,128)(2,1)S(1)} %get-tuple-element.22.feature_ref, s32[192,16,128]{2,1,0:T(8,128)S(1)} %bitcast.27, ...), custom_call_target="tpu_custom_call" | custom-call | flops 1600000000 | bytes 2097152 | tf_op jit(solution)/shard_map/remote_tiles/pallas_call | solution.py:403
  36.8 0.0 collective-permute-done.rest_0_
  36.8 0.0 collective-permute-done.1.rest_1_
  36.8 10.8 %remote_tiles.4 = (f32[4,64,128]{2,1,0:T(8,128)S(1)}, f32[32,4,128]{2,1,0:T(4,128)S(1)}, f32[32,4,128]{2,1,0:T(4,128)S(1)}) custom-call(s32[2,96]{1,0:T(2,128)S(1)} %bitcast.33, f32[64,8,128]{2,1,0:T(8,128)S(1)} %copy-done.8, bf16[64,48,128]{2,1,0:T(8,128)(2,1)S(1)} %get-tuple-element.22.feature_ref, s32[192,16,128]{2,1,0:T(8,128)S(1)} %bitcast.28, ...), custom_call_target="tpu_custom_call" | custom-call | flops 6400000000 | bytes 2097152 | tf_op jit(solution)/shard_map/remote_tiles/pallas_call | solution.py:403
  47.6 0.0 collective-permute-start.2
  47.6 3.5 %collective-permute-start.3 = (f32[32,4,128]{2,1,0:T(4,128)S(1)}, f32[32,4,128]{2,1,0:T(4,128)S(1)}, u32[]{:S(2)}, u32[]{:S(2)}) collective-permute-start(f32[32,4,128]{2,1,0:T(4,128)S(1)} %get-tuple-element.31), channel_id=1, source_target_pairs={{0,480},{32,0},{64,32},{96,64},{128,96},{160,128},{192,160},{224,1... | collective-permute-start | bytes 196616 | tf_op jit(solution)/shard_map/ppermute | solution.py:22
  51.1 0.0 copy-start
  51.1 0.0 copy-start.1
  51.1 0.0 copy-start.2
  51.1 0.0 copy-start.3
  51.1 0.0 copy-start.4
  51.1 3.6 %remote_tiles.5 = (f32[4,64,128]{2,1,0:T(8,128)S(1)}, f32[32,4,128]{2,1,0:T(4,128)S(1)}) custom-call(s32[2,96]{1,0:T(2,128)S(1)} %bitcast.34, f32[64,8,128]{2,1,0:T(8,128)S(1)} %copy-done.8, bf16[64,48,128]{2,1,0:T(8,128)(2,1)S(1)} %get-tuple-element.22.feature_ref, s32[192,16,128]{2,1,0:T(8,128)S(1)} %bitcast.29, ...), custom_call_target="tpu_custom_call" | custom-call | flops 1600000000 | bytes 2097152 | tf_op jit(solution)/shard_map/remote_tiles/pallas_call | solution.py:403
  54.7 0.0 collective-permute-done.2
  54.7 0.0 collective-permute-done.3
  54.8 16.4 %all_to_all.15.returned_ref = f32[32,3,4,128]{3,2,1,0:T(4,128)S(1)} all-to-all(f32[32,3,4,128]{3,2,1,0:T(4,128)S(1)} %pad_maximum_fusion), channel_id=1, replica_groups=mesh['region'=16,'bulk'=32] {'bulk'}, dimensions={0} | all-to-all | bytes 393216 | tf_op jit(solution)/shard_map/all_to_all | solution.py:495
  71.2 0.0 copy-done
  71.2 0.0 copy-done.1
  71.2 0.0 copy-done.2
  71.2 0.0 copy-done.3
  71.2 0.0 copy-done.4
  71.2 1.6 %update.1 = (f32[256,128]{1,0:T(8,128)}, f32[3,64,128]{2,1,0:T(8,128)}, f32[32,8,128]{2,1,0:T(8,128)S(1)}) custom-call(s32[3,1,32]{2,1,0:T(1,128)S(1)} %bitcast.24, s32[1,1,32]{2,1,0:T(1,128)S(1)} %bitcast.26, f32[4,64,128]{2,1,0:T(8,128)S(1)} %get-tuple-element.28.totals_ref, f32[32,3,4,128]{3,2,1,0:T(4,128)S(1)} %all_to_all.15.returned_ref, ...), custom_call_target="tpu_custom_call" | custom-call | tf_op jit(solution)/shard_map/update/pallas_call | solution.py:496
  72.8 13.8 %all_to_all.16.late_ref = f32[32,8,128]{2,1,0:T(8,128)S(1)} all-to-all(f32[32,8,128]{2,1,0:T(8,128)S(1)} %get-tuple-element.34), channel_id=1, replica_groups=mesh['region'=16,'bulk'=32] {'bulk'}, dimensions={0} | all-to-all | bytes 262144 | tf_op jit(solution)/shard_map/all_to_all | solution.py:505
  86.6 0.7 arrive.1
  (2 shorter events, 0.1 us)
Async XLA Ops:
  2.6 24.9 %all-to-all-start = ((f32[32,24,128]{2,1,0:T(8,128)}), f32[32,24,128]{2,1,0:T(8,128)S(1)}, u32[]{:S(2)}, u32[]{:S(2)}) async-start(f32[32,24,128]{2,1,0:T(8,128)} %get-tuple-element.20), calls=%async_computation | async-start | bytes 786432 | tf_op jit(solution)/shard_map/all_to_all | solution.py:475
  12.8 1.0 %copy-start.6 = (s32[1,64,16,128]{3,2,1,0:T(8,128)S(1)}, s32[1,64,16,128]{3,2,1,0:T(8,128)}, u32[]{:S(2)}) copy-start(s32[1,64,16,128]{3,2,1,0:T(8,128)} %param.18) | copy-start | bytes 1572868
  13.9 0.9 %copy-start.7 = (f32[64,8,128]{2,1,0:T(8,128)S(1)}, f32[64,8,128]{2,1,0:T(8,128)}, u32[]{:S(2)}) copy-start(f32[64,8,128]{2,1,0:T(8,128)} %get-tuple-element.19.points_ref) | copy-start | bytes 786436
  14.8 0.7 copy-start.9
  15.5 17.8 %copy-start.5 = (s32[1,96,2,16,128]{4,3,2,1,0:T(8,128)S(1)}, s32[1,96,2,16,128]{4,3,2,1,0:T(8,128)}, u32[]{:S(2)}) copy-start(s32[1,96,2,16,128]{4,3,2,1,0:T(8,128)} %param.16) | copy-start | bytes 4718596
  15.5 17.8 %copy-start.8 = (f32[64,8,128]{2,1,0:T(8,128)S(1)}, f32[64,8,128]{2,1,0:T(8,128)}, u32[]{:S(2)}) copy-start(f32[64,8,128]{2,1,0:T(8,128)} %get-tuple-element.19.points_ref) | copy-start | bytes 786436
  15.5 17.8 %copy-start.10 = (s32[1,96,2]{1,2,0:T(2,128)S(1)}, s32[1,96,2]{1,2,0:T(2,128)}, u32[]{:S(2)}) copy-start(s32[1,96,2]{1,2,0:T(2,128)} %param.15) | copy-start | bytes 2308
  27.5 9.3 %collective-permute-start = (f32[32,8,128]{2,1,0:T(8,128)S(1)}, f32[32,8,128]{2,1,0:T(8,128)S(1)}, u32[]{:S(2)}, u32[]{:S(2)}) collective-permute-start(f32[32,8,128]{2,1,0:T(8,128)S(1)} %get-tuple-element.36), channel_id=1, source_target_pairs={{0,32},{32,64},{64,96},{96,128},{128,160},{160,192},{192,224},{224... | collective-permute-start | bytes 393224 | tf_op jit(solution)/shard_map/ppermute | solution.py:22
  27.6 9.3 %collective-permute-start.1 = (f32[32,8,128]{2,1,0:T(8,128)S(1)}, f32[32,8,128]{2,1,0:T(8,128)S(1)}, u32[]{:S(2)}, u32[]{:S(2)}) collective-permute-start(f32[32,8,128]{2,1,0:T(8,128)S(1)} %get-tuple-element.35), channel_id=1, source_target_pairs={{0,480},{32,0},{64,32},{96,64},{128,96},{160,128},{192,160},{224,1... | collective-permute-start | bytes 393224 | tf_op jit(solution)/shard_map/ppermute | solution.py:22
  47.6 7.1 %collective-permute-start.2 = (f32[32,4,128]{2,1,0:T(4,128)S(1)}, f32[32,4,128]{2,1,0:T(4,128)S(1)}, u32[]{:S(2)}, u32[]{:S(2)}) collective-permute-start(f32[32,4,128]{2,1,0:T(4,128)S(1)} %get-tuple-element.29), channel_id=1, source_target_pairs={{0,32},{32,64},{64,96},{96,128},{128,160},{160,192},{192,224},{224... | collective-permute-start | bytes 196616 | tf_op jit(solution)/shard_map/ppermute | solution.py:22
  47.6 7.1 %collective-permute-start.3 = (f32[32,4,128]{2,1,0:T(4,128)S(1)}, f32[32,4,128]{2,1,0:T(4,128)S(1)}, u32[]{:S(2)}, u32[]{:S(2)}) collective-permute-start(f32[32,4,128]{2,1,0:T(4,128)S(1)} %get-tuple-element.31), channel_id=1, source_target_pairs={{0,480},{32,0},{64,32},{96,64},{128,96},{160,128},{192,160},{224,1... | collective-permute-start | bytes 196616 | tf_op jit(solution)/shard_map/ppermute | solution.py:22
  51.1 20.0 %copy-start = (f32[64,4,128]{2,1,0:T(4,128)S(1)}, f32[64,4,128]{2,1,0:T(4,128)}, u32[]{:S(2)}) copy-start(f32[64,4,128]{2,1,0:T(4,128)} %param.11) | copy-start | bytes 393220
  51.1 20.0 %copy-start.1 = (f32[64,3,128]{2,0,1:T(8,128)S(1)}, f32[64,3,128]{2,0,1:T(8,128)}, u32[]{:S(2)}) copy-start(f32[64,3,128]{2,0,1:T(8,128)} %param.13) | copy-start | bytes 294916
  51.1 20.0 %copy-start.2 = (f32[64,128]{1,0:T(8,128)S(1)}, f32[64,128]{1,0:T(8,128)}, u32[]{:S(2)}) copy-start(f32[64,128]{1,0:T(8,128)} %storage_ref.1) | copy-start | bytes 98308
  51.1 20.0 %copy-start.3 = (s32[1,3,32,1]{2,3,1,0:T(1,128)S(1)}, s32[1,3,32,1]{2,3,1,0:T(1,128)}, u32[]{:S(2)}) copy-start(s32[1,3,32,1]{2,3,1,0:T(1,128)} %param.14) | copy-start | bytes 1156
  51.1 20.0 %copy-start.4 = (s32[1,32,1]{1,2,0:T(1,128)S(1)}, s32[1,32,1]{1,2,0:T(1,128)}, u32[]{:S(2)}) copy-start(s32[1,32,1]{1,2,0:T(1,128)} %param.19) | copy-start | bytes 388
